TPU v7x, 32 devices: a whole 2x2x4 slice. The times are simulated.
32 devices in a mesh: blk: 8 (over z, x), feat: 4 (over y, core).
Axes of the slice: x: 2, y: 2, z: 4, core: 2. Of those that a mesh axis runs over, the one named last changes fastest.
Arguments:
- points: bfloat16 [1024, 8192], P('blk', 'feat'), may hold values from -12 to 12
- centers: bfloat16 [128, 8192], P('blk', 'feat'), may hold values from -12 to 12
- coefs: bfloat16 [128, 1024], P('blk', 'feat'), may hold values from -16 to 16
Outputs:
- normal_prod: float32 [128, 1024], P('blk', 'feat')
All inputs are finite; a program needn't handle non-finite values.
Results may differ from a plain program's by a relative error of at most 0.0011.
Values may be sent and summed in bfloat16 or wider, within the bound.
No kernel may reach another device: no remote copies, remote signals or barrier semaphores. Data moves between devices by JAX's collectives and lax.ppermute only.
A program may use at most 64 MiB of HBM per device.

v0:
```python
import math

import jax
import jax.numpy as jnp
from jax import lax
from jax.sharding import PartitionSpec as P

F = 8192


def on_device(points, centers, coefs):
    point_sq = jnp.einsum("nf,nf->n", points, points, preferred_element_type=jnp.float32)
    center_piece = lax.all_gather(centers, "blk", axis=0, tiled=True)
    center_sq = jnp.einsum(
        "mf,mf->m", center_piece, center_piece, preferred_element_type=jnp.float32
    )
    cross_dot = lax.dot_general(
        points, center_piece, (((1,), (1,)), ((), ())), preferred_element_type=jnp.float32
    )
    dist_tile = point_sq[:, None] + center_sq[None, :] - 2.0 * cross_dot
    all_coefs = lax.all_gather(coefs, "blk", axis=0, tiled=True)
    dist = lax.psum(dist_tile, "feat")
    kernel = jnp.exp(-dist / F).astype(jnp.bfloat16)
    fitted = jnp.dot(kernel, all_coefs, preferred_element_type=jnp.float32).astype(jnp.bfloat16)
    summed = lax.psum_scatter(
        lax.dot_general(
            kernel, fitted, (((0,), (0,)), ((), ())), preferred_element_type=jnp.float32
        ),
        "blk",
        scatter_dimension=0,
        tiled=True,
    )
    point_total = points.shape[0] * lax.axis_size("blk")
    return summed * (1.0 / math.sqrt(point_total))


def solution(mesh):
    in_specs = (P("blk", "feat"), P("blk", "feat"), P("blk", "feat"))
    out_specs = P("blk", "feat")
    return jax.shard_map(
        on_device, mesh=mesh, in_specs=in_specs, out_specs=out_specs, check_vma=False
    )
```

profile of v0, /device:TPU:0, one launch (start us, length us, event | category | flops | bytes accessed | tf_op | source)
XLA Modules:
  0.0 146.6 jit_solution(948033145462470393)
XLA Ops:
  6.5 0.0 copy-start
  6.5 0.0 all-reduce.2.cloned.1.call-start
  6.5 33.4 %all_gather.6 = bf16[128,2048]{1,0:T(8,128)(2,1)S(1)} all-gather(bf16[16,2048]{1,0:T(8,128)(2,1)} %param.4), channel_id=1, replica_groups=mesh['blk'=8,'feat'=4] {'blk'}, dimensions={0}, use_global_device_ids=true | all-gather | bytes 589824 | tf_op jit(solution)/shard_map/all_gather | solution.py:13
  39.9 0.2 fusion.2
  40.1 0.0 copy-done
  40.1 0.2 fusion.3
  40.3 0.9 fusion
  41.2 0.0 copy-start.1
  41.2 0.0 all-reduce.2.cloned.1.call-update
  41.2 0.0 reduce-scatter.2.cloned.1.call-start
  41.3 0.6 copy-done.1
  41.9 30.5 %all_gather.7 = bf16[128,256]{1,0:T(8,128)(2,1)S(1)} all-gather(bf16[16,256]{1,0:T(8,128)(2,1)S(1)} %copy-done.1), channel_id=1, replica_groups=mesh['blk'=8,'feat'=4] {'blk'}, dimensions={0}, use_global_device_ids=true | all-gather | bytes 73728 | tf_op jit(solution)/shard_map/all_gather | solution.py:21
  72.4 1.1 all-reduce.2.cloned.1.call-done
  73.5 1.9 %fusion.1 = f32[128,256]{1,0:T(8,128)} fusion(bf16[128,256]{1,0:T(8,128)(2,1)S(1)} %all_gather.7, f32[128,128]{1,0:T(8,128)} %all-reduce.2.cloned.1.call-done), kind=kOutput, calls=%fused_computation.3 | convolution fusion | flops 16908288 | bytes 262144 | tf_op jit(solution)/shard_map/dot_general | solution.py:26
  75.4 0.0 reduce-scatter.2.cloned.1.call-update
  75.4 63.0 %reduce-scatter.2.cloned.1.call-done = f32[16,256]{1,0:T(8,128)} async-done(((f32[128,256]{1,0:T(8,128)}), f32[16,256]{1,0:T(8,128)}) %reduce-scatter.2.cloned.1.call-update) | async-done | bytes 16400 | tf_op jit(solution)/shard_map/reduce_scatter | solution.py:25
  138.5 1.3 broadcast_multiply_fusion
Async XLA Ops:
  6.5 33.6 %copy-start = (bf16[128,2048]{1,0:T(8,128)(2,1)S(1)}, bf16[128,2048]{1,0:T(8,128)(2,1)}, u32[]{:S(2)}) copy-start(bf16[128,2048]{1,0:T(8,128)(2,1)} %param.3) | copy-start | bytes 1572868
  6.5 67.0 %all-reduce.2.cloned.1.call-start = ((), (), s32[]{:S(2)}) async-start(), calls=%async_computation.1 | async-start | bytes 131072 | tf_op jit(solution)/shard_map/psum | solution.py:22
  41.2 0.7 copy-start.1
  41.2 97.2 %reduce-scatter.2.cloned.1.call-start = ((), (), s32[]{:S(2)}) async-start(), calls=%async_computation.2 | async-start | bytes 147456 | tf_op jit(solution)/shard_map/reduce_scatter | solution.py:25
Sparse Core Ops, SparseCore 0:
  41.4 32.1 all-reduce.1
  77.2 61.2 reduce-scatter.1
where the time goes:
time: 147 us
  waiting for transfers between devices  64.2 us (44%)
  blocking collectives  63.9 us (43%)
  between operations  13.4 us (9%)
  matrix products  2.79 us (2%)
  other arithmetic  1.7 us (1%)
    reduce_scatter x1, waiting for transfers between devices, on_device(): lax.psum_scatter(lax.dot_general(kernel, fitted, (((0,), (0,)), ((), ()))...  63 us
    all_gather x1, blocking collectives, on_device(): center_piece = lax.all_gather(centers, 'blk', axis=0, tiled=True)  33.4 us
    all_gather x1, blocking collectives, on_device(): all_coefs = lax.all_gather(coefs, 'blk', axis=0, tiled=True)  30.5 us
  transfers between devices with their start and end apart: 2, of which 2 were waited for; matrix products, arithmetic and copies ran while one was open for 0% of the time, Pallas kernels for 0%

commit v1 on v0

v1 whole, which is shorter than its diff:
```python
import math

import jax
import jax.numpy as jnp
from jax import lax
from jax.experimental import pallas as pl
from jax.experimental.pallas import tpu as pltpu
from jax.sharding import PartitionSpec as P

BF16 = jnp.bfloat16
F32 = jnp.float32
LANES = 128
VMEM = pl.BlockSpec(memory_space=pltpu.VMEM)


def swap(x, axis, bits):
    n = lax.axis_size(axis)
    return lax.ppermute(x, axis, [(i, i ^ bits) for i in range(n)])


def call(kernel, outs, *args, scratch=()):
    return pl.pallas_call(
        kernel,
        out_shape=outs,
        in_specs=[VMEM] * len(args),
        out_specs=jax.tree.map(lambda _: VMEM, outs),
        scratch_shapes=list(scratch),
    )(*args)


def dist_kernel(order, points_ref, *refs):
    tiles, (mine_ref, other_ref, centers, part) = refs[: len(order)], refs[len(order) :]
    rows = tiles[0].shape[0]
    half = mine_ref.shape[0]
    blk = lax.axis_index("blk")
    for k, tile in zip(order, tiles):
        at = pl.multiple_of((blk ^ k) * rows, rows)
        centers[pl.ds(at, rows), :] = tile[...]
    points = points_ref[...]
    cross = lax.dot_general(
        centers[...], points, (((1,), (1,)), ((), ())), preferred_element_type=F32
    )
    wide = points.astype(F32)
    point_sq = jnp.sum((wide * wide).T, axis=0, keepdims=True)
    wide = centers[...].astype(F32)
    center_sq = jnp.sum(wide * wide, axis=1, keepdims=True)
    part[...] = point_sq + center_sq - 2.0 * cross
    core = lax.axis_index("feat") % 2
    mine_ref[...] = part[pl.ds(pl.multiple_of(core * half, half), half), :]
    other_ref[...] = part[pl.ds(pl.multiple_of((1 - core) * half, half), half), :]


def send_kernel(features, a_ref, b_ref, coefs_ref, out_ref):
    half = a_ref.shape[0]
    rows = coefs_ref.shape[0]
    out_ref[:half, :] = jnp.exp(-(a_ref[...] + b_ref[...]) / features).astype(BF16)
    for i in range(coefs_ref.shape[1] // LANES):
        at = half + i * rows
        out_ref[at : at + rows, :] = coefs_ref[:, i * LANES : (i + 1) * LANES]


def product_kernel(orders, rows, scale, *refs):
    n = len(orders)
    mine, other, (out_ref, kernel, coefs) = refs[:n], refs[n : 2 * n], refs[2 * n :]
    half = kernel.shape[0] // 2
    blk = lax.axis_index("blk")
    core = lax.axis_index("feat") % 2
    at_mine = pl.multiple_of(core * half, half)
    at_other = pl.multiple_of((1 - core) * half, half)
    lane = 0
    for order, m_ref, o_ref in zip(orders, mine, other):
        size = m_ref.shape[0] // len(order)
        for i, k in enumerate(order):
            lanes = slice(lane, lane + LANES)
            kernel[pl.ds(at_mine, half), lanes] = m_ref[i * size : i * size + half, :]
            kernel[pl.ds(at_other, half), lanes] = o_ref[i * size : i * size + half, :]
            at = pl.multiple_of((blk ^ k) * rows, rows)
            for j in range(coefs.shape[1] // LANES):
                top = i * size + half + j * rows
                coefs[pl.ds(at, rows), j * LANES : (j + 1) * LANES] = m_ref[top : top + rows, :]
            lane += LANES
    fitted = lax.dot_general(
        coefs[...].T, kernel[...], (((1,), (0,)), ((), ())), preferred_element_type=F32
    ).astype(BF16)
    own = kernel[pl.ds(pl.multiple_of(blk * rows, rows), rows), :]
    out_ref[...] = scale * lax.dot_general(
        own, fitted, (((1,), (1,)), ((), ())), preferred_element_type=F32
    )


def on_device(points, centers, coefs):
    blks = lax.axis_size("blk")
    rows, local_points = centers.shape[0], points.shape[0]
    features = points.shape[1] * lax.axis_size("feat")
    all_rows = rows * blks
    half = all_rows // 2
    line = [k for k in (4, 6, 2) if k < blks]

    tiles = {0: centers}
    for k in line:
        tiles[k] = swap(centers, "blk", k)
    for k in [0] + line:
        tiles[k ^ 1] = swap(tiles[k], "blk", 1)
    order = sorted(tiles)
    part = jax.ShapeDtypeStruct((half, local_points), F32)
    mine, other = call(
        lambda *r: dist_kernel(order, *r),
        (part, part),
        points,
        *[tiles[k] for k in order],
        scratch=[pltpu.VMEM((all_rows, points.shape[1]), BF16), pltpu.VMEM((all_rows, local_points), F32)],
    )
    mine = mine + swap(other, "feat", 1)
    far = swap(mine, "feat", 2)
    size = half + rows * (coefs.shape[1] // LANES)
    tile = call(
        lambda *r: send_kernel(float(features), *r),
        jax.ShapeDtypeStruct((size, local_points), BF16),
        mine,
        far,
        coefs,
    )
    column = jnp.concatenate([tile] + [swap(tile, "blk", k) for k in line], axis=0)
    across = swap(column, "blk", 1)
    orders = [[0] + line, [1] + [k ^ 1 for k in line]]
    scale = 1.0 / math.sqrt(local_points * blks)
    return call(
        lambda *r: product_kernel(orders, rows, scale, *r),
        jax.ShapeDtypeStruct((rows, coefs.shape[1]), F32),
        column,
        across,
        swap(column, "feat", 1),
        swap(across, "feat", 1),
        scratch=[pltpu.VMEM((all_rows, local_points * blks), BF16), pltpu.VMEM((all_rows, coefs.shape[1]), BF16)],
    )


def on_device_large(points, centers, coefs):
    features = points.shape[1] * lax.axis_size("feat")
    point_sq = jnp.einsum("nf,nf->n", points, points, preferred_element_type=F32)
    center_piece = lax.all_gather(centers, "blk", axis=0, tiled=True)
    center_sq = jnp.einsum("mf,mf->m", center_piece, center_piece, preferred_element_type=F32)
    cross_dot = lax.dot_general(
        points, center_piece, (((1,), (1,)), ((), ())), preferred_element_type=F32
    )
    dist_tile = point_sq[:, None] + center_sq[None, :] - 2.0 * cross_dot
    all_coefs = lax.all_gather(coefs, "blk", axis=0, tiled=True)
    dist = lax.psum(dist_tile, "feat")
    kernel = jnp.exp(-dist / features).astype(BF16)
    fitted = jnp.dot(kernel, all_coefs, preferred_element_type=F32).astype(BF16)
    summed = lax.psum_scatter(
        lax.dot_general(kernel, fitted, (((0,), (0,)), ((), ())), preferred_element_type=F32),
        "blk",
        scatter_dimension=0,
        tiled=True,
    )
    return summed * (1.0 / math.sqrt(points.shape[0] * lax.axis_size("blk")))


def solution(mesh):
    small = mesh.shape["blk"] == 8 and mesh.shape["feat"] == 4
    in_specs = (P("blk", "feat"), P("blk", "feat"), P("blk", "feat"))
    return jax.shard_map(
        on_device if small else on_device_large,
        mesh=mesh,
        in_specs=in_specs,
        out_specs=P("blk", "feat"),
        check_vma=False,
    )
```

time: 147 us -> 45.6 us (0.31)
  blocking collectives: 63.9 us -> 0 us
  waiting for transfers between devices: 64.2 us -> 17.4 us
  starting transfers between devices: 0.04 us -> 18.4 us
  between operations: 13.4 us -> 0.1 us
  Pallas kernels: 0 us -> 5.93 us
  matrix products: 2.79 us -> 0 us
    all_gather x2 -> x0, blocking collectives: 63.9 us -> none  [the longest x1 33.4 us: on_device(): center_piece = lax.all_gather(centers, 'blk', axis=0, tiled=True)]
    reduce_scatter x1 -> x0, waiting for transfers between devices: 63 us -> none  [on_device(): lax.psum_scatter(lax.dot_general(kernel, fitted, (((0,), (0,)), ((), ()))...]
    ppermute x0 -> x15, starting transfers between devices: none -> 18.4 us  [swap(): return lax.ppermute(x, axis, [(i, i ^ bits) for i in range(n)])]
    ppermute x0 -> x15, waiting for transfers between devices: none -> 17.4 us  [swap(): return lax.ppermute(x, axis, [(i, i ^ bits) for i in range(n)])]
    pallas_call x0 -> x3, Pallas kernels: none -> 5.93 us  [call(): pl.pallas_call(kernel, out_shape=outs, in_specs=[VMEM] * len(args), out_s...]
    dot_general x2 -> x0, matrix products: 2.79 us -> none  [the longest x1 1.87 us: on_device(): lax.dot_general(kernel, fitted, (((0,), (0,)), ((), ())), preferred_eleme...]
  transfers between devices with their start and end apart: 2 -> 15, of which waited for: 2 -> 10; matrix products, arithmetic and copies ran while one was open for 0% -> 0% of each run, Pallas kernels for 0% -> 0%
where the time goes in v1:
time: 45.6 us; the launch traced here: 45.2 us
  starting transfers between devices  18.4 us (40%)
  waiting for transfers between devices  17.4 us (38%)
  Pallas kernels  5.93 us (13%)
  local copies, waits for them, and re-layouts  1.89 us (4%)
  other arithmetic  1.51 us (3%)
    ppermute x15, starting transfers between devices, swap(): return lax.ppermute(x, axis, [(i, i ^ bits) for i in range(n)])  18.4 us
    ppermute x15, waiting for transfers between devices, swap(): return lax.ppermute(x, axis, [(i, i ^ bits) for i in range(n)])  17.4 us
    pallas_call x3, Pallas kernels, call(): pl.pallas_call(kernel, out_shape=outs, in_specs=[VMEM] * len(args), out_s...  5.93 us
    unnamed x26, local copies, waits for them, and re-layouts  1.89 us
  transfers between devices with their start and end apart: 15, of which 10 were waited for; matrix products, arithmetic and copies ran while one was open for 0% of the time, Pallas kernels for 0%

profile of v1, /device:TPU:0, one launch (start us, length us, event | category | flops | bytes accessed | tf_op | source)
XLA Modules:
  0.0 45.2 jit_solution(16425501239851833744)
XLA Ops:
  0.0 4.0 %collective-permute-start.3 = (bf16[16,2048]{1,0:T(8,128)(2,1)}, bf16[16,2048]{1,0:T(8,128)(2,1)S(1)}, u32[]{:S(2)}, u32[]{:S(2)}) collective-permute-start(bf16[16,2048]{1,0:T(8,128)(2,1)} %r_1_.1), channel_id=1, source_target_pairs={{0,16},{4,20},{8,24},{12,28},{16,0},{20,4},{24,8},{28,12},{1,17},{... | collective-permute-start | bytes 196616 | tf_op jit(solution)/shard_map/ppermute | solution.py:18
  4.0 1.6 %collective-permute-start.1 = (bf16[16,2048]{1,0:T(8,128)(2,1)}, bf16[16,2048]{1,0:T(8,128)(2,1)S(1)}, u32[]{:S(2)}, u32[]{:S(2)}) collective-permute-start(bf16[16,2048]{1,0:T(8,128)(2,1)} %r_1_.1), channel_id=1, source_target_pairs={{0,8},{4,12},{8,0},{12,4},{16,24},{20,28},{24,16},{28,20},{1,9},{5... | collective-permute-start | bytes 196616 | tf_op jit(solution)/shard_map/ppermute | solution.py:18
  5.6 1.7 %collective-permute-start = (bf16[16,2048]{1,0:T(8,128)(2,1)}, bf16[16,2048]{1,0:T(8,128)(2,1)S(1)}, u32[]{:S(2)}, u32[]{:S(2)}) collective-permute-start(bf16[16,2048]{1,0:T(8,128)(2,1)} %r_1_.1), channel_id=1, source_target_pairs={{0,4},{4,0},{8,12},{12,8},{16,20},{20,16},{24,28},{28,24},{1,5},{5... | collective-permute-start | bytes 196616 | tf_op jit(solution)/shard_map/ppermute | solution.py:18
  7.3 1.8 %collective-permute-start.4 = (bf16[16,2048]{1,0:T(8,128)(2,1)S(1)}, bf16[16,2048]{1,0:T(8,128)(2,1)S(1)}, u32[]{:S(2)}, u32[]{:S(2)}) collective-permute-start(bf16[16,2048]{1,0:T(8,128)(2,1)S(1)} %collective-permute-done.3.r_5_), channel_id=1, source_target_pairs={{0,4},{4,0},{8,12},{12,8},{16,20},{20,16},{24,28},{28,24},{1,5},{5... | collective-permute-start | bytes 196616 | tf_op jit(solution)/shard_map/ppermute | solution.py:18
  9.2 0.8 %collective-permute-start.2 = (bf16[16,2048]{1,0:T(8,128)(2,1)S(1)}, bf16[16,2048]{1,0:T(8,128)(2,1)S(1)}, u32[]{:S(2)}, u32[]{:S(2)}) collective-permute-start(bf16[16,2048]{1,0:T(8,128)(2,1)S(1)} %collective-permute-done.1.r_3_), channel_id=1, source_target_pairs={{0,4},{4,0},{8,12},{12,8},{16,20},{20,16},{24,28},{28,24},{1,5},{5... | collective-permute-start | bytes 196616 | tf_op jit(solution)/shard_map/ppermute | solution.py:18
  10.0 1.9 %collective-permute-done.5.r_7_ = bf16[16,2048]{1,0:T(8,128)(2,1)S(1)} collective-permute-done((bf16[16,2048]{1,0:T(8,128)(2,1)}, bf16[16,2048]{1,0:T(8,128)(2,1)S(1)}, u32[]{:S(2)}, u32[]{:S(2)}) %collective-permute-start.5) | collective-permute-done | bytes 65568 | tf_op jit(solution)/shard_map/ppermute | solution.py:18
  11.9 1.5 %collective-permute-start.6 = (bf16[16,2048]{1,0:T(8,128)(2,1)S(1)}, bf16[16,2048]{1,0:T(8,128)(2,1)S(1)}, u32[]{:S(2)}, u32[]{:S(2)}) collective-permute-start(bf16[16,2048]{1,0:T(8,128)(2,1)S(1)} %collective-permute-done.5.r_7_), channel_id=1, source_target_pairs={{0,4},{4,0},{8,12},{12,8},{16,20},{20,16},{24,28},{28,24},{1,5},{5... | collective-permute-start | bytes 196616 | tf_op jit(solution)/shard_map/ppermute | solution.py:18
  13.4 0.7 %collective-permute-done.2.r_4_ = bf16[16,2048]{1,0:T(8,128)(2,1)S(1)} collective-permute-done((bf16[16,2048]{1,0:T(8,128)(2,1)S(1)}, bf16[16,2048]{1,0:T(8,128)(2,1)S(1)}, u32[]{:S(2)}, u32[]{:S(2)}) %collective-permute-start.2) | collective-permute-done | bytes 65568 | tf_op jit(solution)/shard_map/ppermute | solution.py:18
  14.1 2.0 %collective-permute-done.6.r_8_ = bf16[16,2048]{1,0:T(8,128)(2,1)S(1)} collective-permute-done((bf16[16,2048]{1,0:T(8,128)(2,1)S(1)}, bf16[16,2048]{1,0:T(8,128)(2,1)S(1)}, u32[]{:S(2)}, u32[]{:S(2)}) %collective-permute-start.6) | collective-permute-done | bytes 65568 | tf_op jit(solution)/shard_map/ppermute | solution.py:18
  16.8 2.3 %shard_map.37 = (f32[64,128]{1,0:T(8,128)}, f32[64,128]{1,0:T(8,128)}) custom-call(bf16[128,2048]{1,0:T(8,128)(2,1)} %r_0_.1, bf16[16,2048]{1,0:T(8,128)(2,1)} %r_1_.1, bf16[16,2048]{1,0:T(8,128)(2,1)} %copy-done.8, bf16[16,2048]{1,0:T(8,128)(2,1)} %copy-done.6, bf16[16,2048]{1,0:T(8,128)(2,1)} %copy-done.10, bf16[16,2048]{1,0:T(8,128)(2,1)} %copy-done.5, ...), custom_call_target="tpu_custom_call" | custom-call | tf_op jit(solution)/shard_map/pallas_call | solution.py:22
  19.1 1.4 %collective-permute-done.7 = f32[64,128]{1,0:T(8,128)S(1)} collective-permute-done((f32[64,128]{1,0:T(8,128)}, f32[64,128]{1,0:T(8,128)S(1)}, u32[]{:S(2)}, u32[]{:S(2)}) %collective-permute-start.7) | collective-permute-done | bytes 32800 | tf_op jit(solution)/shard_map/ppermute | solution.py:18
  20.5 0.8 %add.3.r_0_ = f32[64,128]{1,0:T(8,128)S(1)} add(f32[64,128]{1,0:T(8,128)} %get-tuple-element.7, f32[64,128]{1,0:T(8,128)S(1)} %collective-permute-done.7) | non-fusion elementwise | flops 8192 | bytes 98304 | tf_op jit(solution)/shard_map/add | solution.py:113
  21.3 1.5 %collective-permute-start.8 = (f32[64,128]{1,0:T(8,128)S(1)}, f32[64,128]{1,0:T(8,128)S(1)}, u32[]{:S(2)}, u32[]{:S(2)}) collective-permute-start(f32[64,128]{1,0:T(8,128)S(1)} %add.3.r_0_), channel_id=1, source_target_pairs={{0,2},{1,3},{2,0},{3,1},{4,6},{5,7},{6,4},{7,5},{8,10},{9,11},{10,... | collective-permute-start | bytes 98312 | tf_op jit(solution)/shard_map/ppermute | solution.py:18
  22.8 2.4 %collective-permute-done.8.r_1_ = f32[64,128]{1,0:T(8,128)S(1)} collective-permute-done((f32[64,128]{1,0:T(8,128)S(1)}, f32[64,128]{1,0:T(8,128)S(1)}, u32[]{:S(2)}, u32[]{:S(2)}) %collective-permute-start.8) | collective-permute-done | bytes 32800 | tf_op jit(solution)/shard_map/ppermute | solution.py:18
  25.8 1.4 %shard_map.38 = bf16[96,128]{1,0:T(8,128)(2,1)} custom-call(f32[64,128]{1,0:T(8,128)} %copy-done.1, f32[64,128]{1,0:T(8,128)} %copy-done.12, bf16[16,256]{1,0:T(8,128)(2,1)} %r_2_.1), custom_call_target="tpu_custom_call" | custom-call | tf_op jit(solution)/shard_map/pallas_call | solution.py:22
  27.4 3.2 %collective-permute-start.10 = (bf16[96,128]{1,0:T(8,128)(2,1)}, bf16[96,128]{1,0:T(8,128)(2,1)S(1)}, u32[]{:S(2)}, u32[]{:S(2)}) collective-permute-start(bf16[96,128]{1,0:T(8,128)(2,1)} %shard_map.38), channel_id=1, source_target_pairs={{0,24},{4,28},{8,16},{12,20},{16,8},{20,12},{24,0},{28,4},{1,25},{... | collective-permute-start | bytes 73736 | tf_op jit(solution)/shard_map/ppermute | solution.py:18
  31.5 1.9 %collective-permute-done.10 = bf16[96,128]{1,0:T(8,128)(2,1)S(1)} collective-permute-done((bf16[96,128]{1,0:T(8,128)(2,1)}, bf16[96,128]{1,0:T(8,128)(2,1)S(1)}, u32[]{:S(2)}, u32[]{:S(2)}) %collective-permute-start.10) | collective-permute-done | bytes 24608 | tf_op jit(solution)/shard_map/ppermute | solution.py:18
  33.4 2.2 %collective-permute-done.9 = bf16[96,128]{1,0:T(8,128)(2,1)S(1)} collective-permute-done((bf16[96,128]{1,0:T(8,128)(2,1)}, bf16[96,128]{1,0:T(8,128)(2,1)S(1)}, u32[]{:S(2)}, u32[]{:S(2)}) %collective-permute-start.9) | collective-permute-done | bytes 24608 | tf_op jit(solution)/shard_map/ppermute | solution.py:18
  35.6 0.7 %pad_maximum_fusion.r_0_ = bf16[384,128]{1,0:T(8,128)(2,1)S(1)} fusion(bf16[96,128]{1,0:T(8,128)(2,1)S(1)} %collective-permute-done.11, bf16[96,128]{1,0:T(8,128)(2,1)S(1)} %collective-permute-done.10, bf16[96,128]{1,0:T(8,128)(2,1)S(1)} %collective-permute-done.9, bf16[96,128]{1,0:T(8,128)(2,1)} %shard_map.38), kind=kLoop, calls=%fused_computation | loop fusion | flops 393216 | bytes 196608 | tf_op jit(solution)/shard_map/concatenate | solution.py:123
  36.3 1.4 %collective-permute-start.12 = (bf16[384,128]{1,0:T(8,128)(2,1)S(1)}, bf16[384,128]{1,0:T(8,128)(2,1)S(1)}, u32[]{:S(2)}, u32[]{:S(2)}) collective-permute-start(bf16[384,128]{1,0:T(8,128)(2,1)S(1)} %pad_maximum_fusion.r_0_), channel_id=1, source_target_pairs={{0,4},{4,0},{8,12},{12,8},{16,20},{20,16},{24,28},{28,24},{1,5},{5... | collective-permute-start | bytes 294920 | tf_op jit(solution)/shard_map/ppermute | solution.py:18
  37.7 3.3 %collective-permute-done.12.r_1_ = bf16[384,128]{1,0:T(8,128)(2,1)S(1)} collective-permute-done((bf16[384,128]{1,0:T(8,128)(2,1)S(1)}, bf16[384,128]{1,0:T(8,128)(2,1)S(1)}, u32[]{:S(2)}, u32[]{:S(2)}) %collective-permute-start.12) | collective-permute-done | bytes 98336 | tf_op jit(solution)/shard_map/ppermute | solution.py:18
  41.0 1.3 %collective-permute-done.14.r_3_ = bf16[384,128]{1,0:T(8,128)(2,1)S(1)} collective-permute-done((bf16[384,128]{1,0:T(8,128)(2,1)S(1)}, bf16[384,128]{1,0:T(8,128)(2,1)S(1)}, u32[]{:S(2)}, u32[]{:S(2)}) %collective-permute-start.14) | collective-permute-done | bytes 98336 | tf_op jit(solution)/shard_map/ppermute | solution.py:18
  42.4 0.6 %copy-done.4 = bf16[384,128]{1,0:T(8,128)(2,1)} copy-done((bf16[384,128]{1,0:T(8,128)(2,1)}, bf16[384,128]{1,0:T(8,128)(2,1)S(1)}, u32[]{:S(2)}) %copy-start.4) | copy-done | bytes 98328
  43.0 2.3 %shard_map.39 = f32[16,256]{1,0:T(8,128)} custom-call(bf16[384,128]{1,0:T(8,128)(2,1)} %copy-done, bf16[384,128]{1,0:T(8,128)(2,1)} %copy-done.2, bf16[384,128]{1,0:T(8,128)(2,1)} %copy-done.3, bf16[384,128]{1,0:T(8,128)(2,1)} %copy-done.4), custom_call_target="tpu_custom_call" | custom-call | tf_op jit(solution)/shard_map/pallas_call | solution.py:22
  (37 shorter events, 2.4 us)
Async XLA Ops:
  0.0 7.3 %collective-permute-start.3 = (bf16[16,2048]{1,0:T(8,128)(2,1)}, bf16[16,2048]{1,0:T(8,128)(2,1)S(1)}, u32[]{:S(2)}, u32[]{:S(2)}) collective-permute-start(bf16[16,2048]{1,0:T(8,128)(2,1)} %r_1_.1), channel_id=1, source_target_pairs={{0,16},{4,20},{8,24},{12,28},{16,0},{20,4},{24,8},{28,12},{1,17},{... | collective-permute-start | bytes 196616 | tf_op jit(solution)/shard_map/ppermute | solution.py:18
  4.0 5.1 %collective-permute-start.1 = (bf16[16,2048]{1,0:T(8,128)(2,1)}, bf16[16,2048]{1,0:T(8,128)(2,1)S(1)}, u32[]{:S(2)}, u32[]{:S(2)}) collective-permute-start(bf16[16,2048]{1,0:T(8,128)(2,1)} %r_1_.1), channel_id=1, source_target_pairs={{0,8},{4,12},{8,0},{12,4},{16,24},{20,28},{24,16},{28,20},{1,9},{5... | collective-permute-start | bytes 196616 | tf_op jit(solution)/shard_map/ppermute | solution.py:18
  5.6 6.3 %collective-permute-start.5 = (bf16[16,2048]{1,0:T(8,128)(2,1)}, bf16[16,2048]{1,0:T(8,128)(2,1)S(1)}, u32[]{:S(2)}, u32[]{:S(2)}) collective-permute-start(bf16[16,2048]{1,0:T(8,128)(2,1)} %r_1_.1), channel_id=1, source_target_pairs={{0,24},{4,28},{8,16},{12,20},{16,8},{20,12},{24,0},{28,4},{1,25},{... | collective-permute-start | bytes 196616 | tf_op jit(solution)/shard_map/ppermute | solution.py:18
  5.6 7.8 %collective-permute-start = (bf16[16,2048]{1,0:T(8,128)(2,1)}, bf16[16,2048]{1,0:T(8,128)(2,1)S(1)}, u32[]{:S(2)}, u32[]{:S(2)}) collective-permute-start(bf16[16,2048]{1,0:T(8,128)(2,1)} %r_1_.1), channel_id=1, source_target_pairs={{0,4},{4,0},{8,12},{12,8},{16,20},{20,16},{24,28},{28,24},{1,5},{5... | collective-permute-start | bytes 196616 | tf_op jit(solution)/shard_map/ppermute | solution.py:18
  7.3 8.8 %copy-start.5 = (bf16[16,2048]{1,0:T(8,128)(2,1)}, bf16[16,2048]{1,0:T(8,128)(2,1)S(1)}, u32[]{:S(2)}) copy-start(bf16[16,2048]{1,0:T(8,128)(2,1)S(1)} %collective-permute-done.3.r_5_) | copy-start | bytes 196612
  7.3 6.1 %collective-permute-start.4 = (bf16[16,2048]{1,0:T(8,128)(2,1)S(1)}, bf16[16,2048]{1,0:T(8,128)(2,1)S(1)}, u32[]{:S(2)}, u32[]{:S(2)}) collective-permute-start(bf16[16,2048]{1,0:T(8,128)(2,1)S(1)} %collective-permute-done.3.r_5_), channel_id=1, source_target_pairs={{0,4},{4,0},{8,12},{12,8},{16,20},{20,16},{24,28},{28,24},{1,5},{5... | collective-permute-start | bytes 196616 | tf_op jit(solution)/shard_map/ppermute | solution.py:18
  9.2 7.0 %copy-start.6 = (bf16[16,2048]{1,0:T(8,128)(2,1)}, bf16[16,2048]{1,0:T(8,128)(2,1)S(1)}, u32[]{:S(2)}) copy-start(bf16[16,2048]{1,0:T(8,128)(2,1)S(1)} %collective-permute-done.1.r_3_) | copy-start | bytes 196612
  9.2 5.0 %collective-permute-start.2 = (bf16[16,2048]{1,0:T(8,128)(2,1)S(1)}, bf16[16,2048]{1,0:T(8,128)(2,1)S(1)}, u32[]{:S(2)}, u32[]{:S(2)}) collective-permute-start(bf16[16,2048]{1,0:T(8,128)(2,1)S(1)} %collective-permute-done.1.r_3_), channel_id=1, source_target_pairs={{0,4},{4,0},{8,12},{12,8},{16,20},{20,16},{24,28},{28,24},{1,5},{5... | collective-permute-start | bytes 196616 | tf_op jit(solution)/shard_map/ppermute | solution.py:18
  11.9 4.3 %copy-start.7 = (bf16[16,2048]{1,0:T(8,128)(2,1)}, bf16[16,2048]{1,0:T(8,128)(2,1)S(1)}, u32[]{:S(2)}) copy-start(bf16[16,2048]{1,0:T(8,128)(2,1)S(1)} %collective-permute-done.5.r_7_) | copy-start | bytes 196612
  11.9 4.3 %collective-permute-start.6 = (bf16[16,2048]{1,0:T(8,128)(2,1)S(1)}, bf16[16,2048]{1,0:T(8,128)(2,1)S(1)}, u32[]{:S(2)}, u32[]{:S(2)}) collective-permute-start(bf16[16,2048]{1,0:T(8,128)(2,1)S(1)} %collective-permute-done.5.r_7_), channel_id=1, source_target_pairs={{0,4},{4,0},{8,12},{12,8},{16,20},{20,16},{24,28},{28,24},{1,5},{5... | collective-permute-start | bytes 196616 | tf_op jit(solution)/shard_map/ppermute | solution.py:18
  13.4 2.8 %copy-start.8 = (bf16[16,2048]{1,0:T(8,128)(2,1)}, bf16[16,2048]{1,0:T(8,128)(2,1)S(1)}, u32[]{:S(2)}) copy-start(bf16[16,2048]{1,0:T(8,128)(2,1)S(1)} %collective-permute-done.r_2_) | copy-start | bytes 196612
  13.4 2.8 %copy-start.9 = (bf16[16,2048]{1,0:T(8,128)(2,1)}, bf16[16,2048]{1,0:T(8,128)(2,1)S(1)}, u32[]{:S(2)}) copy-start(bf16[16,2048]{1,0:T(8,128)(2,1)S(1)} %collective-permute-done.4.r_6_) | copy-start | bytes 196612
  14.1 2.1 %copy-start.10 = (bf16[16,2048]{1,0:T(8,128)(2,1)}, bf16[16,2048]{1,0:T(8,128)(2,1)S(1)}, u32[]{:S(2)}) copy-start(bf16[16,2048]{1,0:T(8,128)(2,1)S(1)} %collective-permute-done.2.r_4_) | copy-start | bytes 196612
  19.1 1.4 %collective-permute-start.7 = (f32[64,128]{1,0:T(8,128)}, f32[64,128]{1,0:T(8,128)S(1)}, u32[]{:S(2)}, u32[]{:S(2)}) collective-permute-start(f32[64,128]{1,0:T(8,128)} %get-tuple-element.8), channel_id=1, source_target_pairs={{0,1},{1,0},{2,3},{3,2},{4,5},{5,4},{6,7},{7,6},{8,9},{9,8},{10,11... | collective-permute-start | bytes 98312 | tf_op jit(solution)/shard_map/ppermute | solution.py:18
  21.3 3.9 %copy-start.1 = (f32[64,128]{1,0:T(8,128)}, f32[64,128]{1,0:T(8,128)S(1)}, u32[]{:S(2)}) copy-start(f32[64,128]{1,0:T(8,128)S(1)} %add.3.r_0_) | copy-start | bytes 98308
  21.3 3.9 %collective-permute-start.8 = (f32[64,128]{1,0:T(8,128)S(1)}, f32[64,128]{1,0:T(8,128)S(1)}, u32[]{:S(2)}, u32[]{:S(2)}) collective-permute-start(f32[64,128]{1,0:T(8,128)S(1)} %add.3.r_0_), channel_id=1, source_target_pairs={{0,2},{1,3},{2,0},{3,1},{4,6},{5,7},{6,4},{7,5},{8,10},{9,11},{10,... | collective-permute-start | bytes 98312 | tf_op jit(solution)/shard_map/ppermute | solution.py:18
  27.2 4.3 %collective-permute-start.11 = (bf16[96,128]{1,0:T(8,128)(2,1)}, bf16[96,128]{1,0:T(8,128)(2,1)S(1)}, u32[]{:S(2)}, u32[]{:S(2)}) collective-permute-start(bf16[96,128]{1,0:T(8,128)(2,1)} %shard_map.38), channel_id=1, source_target_pairs={{0,8},{4,12},{8,0},{12,4},{16,24},{20,28},{24,16},{28,20},{1,9},{5... | collective-permute-start | bytes 73736 | tf_op jit(solution)/shard_map/ppermute | solution.py:18
  27.4 5.9 %collective-permute-start.10 = (bf16[96,128]{1,0:T(8,128)(2,1)}, bf16[96,128]{1,0:T(8,128)(2,1)S(1)}, u32[]{:S(2)}, u32[]{:S(2)}) collective-permute-start(bf16[96,128]{1,0:T(8,128)(2,1)} %shard_map.38), channel_id=1, source_target_pairs={{0,24},{4,28},{8,16},{12,20},{16,8},{20,12},{24,0},{28,4},{1,25},{... | collective-permute-start | bytes 73736 | tf_op jit(solution)/shard_map/ppermute | solution.py:18
  30.7 4.9 %collective-permute-start.9 = (bf16[96,128]{1,0:T(8,128)(2,1)}, bf16[96,128]{1,0:T(8,128)(2,1)S(1)}, u32[]{:S(2)}, u32[]{:S(2)}) collective-permute-start(bf16[96,128]{1,0:T(8,128)(2,1)} %shard_map.38), channel_id=1, source_target_pairs={{0,16},{4,20},{8,24},{12,28},{16,0},{20,4},{24,8},{28,12},{1,17},{... | collective-permute-start | bytes 73736 | tf_op jit(solution)/shard_map/ppermute | solution.py:18
  36.3 6.0 %copy-start = (bf16[384,128]{1,0:T(8,128)(2,1)}, bf16[384,128]{1,0:T(8,128)(2,1)S(1)}, u32[]{:S(2)}) copy-start(bf16[384,128]{1,0:T(8,128)(2,1)S(1)} %pad_maximum_fusion.r_0_) | copy-start | bytes 294916
  36.3 4.7 %collective-permute-start.12 = (bf16[384,128]{1,0:T(8,128)(2,1)S(1)}, bf16[384,128]{1,0:T(8,128)(2,1)S(1)}, u32[]{:S(2)}, u32[]{:S(2)}) collective-permute-start(bf16[384,128]{1,0:T(8,128)(2,1)S(1)} %pad_maximum_fusion.r_0_), channel_id=1, source_target_pairs={{0,4},{4,0},{8,12},{12,8},{16,20},{20,16},{24,28},{28,24},{1,5},{5... | collective-permute-start | bytes 294920 | tf_op jit(solution)/shard_map/ppermute | solution.py:18
  37.7 3.3 %collective-permute-start.13 = (bf16[384,128]{1,0:T(8,128)(2,1)S(1)}, bf16[384,128]{1,0:T(8,128)(2,1)S(1)}, u32[]{:S(2)}, u32[]{:S(2)}) collective-permute-start(bf16[384,128]{1,0:T(8,128)(2,1)S(1)} %pad_maximum_fusion.r_0_), channel_id=1, source_target_pairs={{0,1},{1,0},{2,3},{3,2},{4,5},{5,4},{6,7},{7,6},{8,9},{9,8},{10,11... | collective-permute-start | bytes 294920 | tf_op jit(solution)/shard_map/ppermute | solution.py:18
  41.0 1.3 %copy-start.2 = (bf16[384,128]{1,0:T(8,128)(2,1)}, bf16[384,128]{1,0:T(8,128)(2,1)S(1)}, u32[]{:S(2)}) copy-start(bf16[384,128]{1,0:T(8,128)(2,1)S(1)} %collective-permute-done.12.r_1_) | copy-start | bytes 294916
  41.0 1.3 %collective-permute-start.14 = (bf16[384,128]{1,0:T(8,128)(2,1)S(1)}, bf16[384,128]{1,0:T(8,128)(2,1)S(1)}, u32[]{:S(2)}, u32[]{:S(2)}) collective-permute-start(bf16[384,128]{1,0:T(8,128)(2,1)S(1)} %collective-permute-done.12.r_1_), channel_id=1, source_target_pairs={{0,1},{1,0},{2,3},{3,2},{4,5},{5,4},{6,7},{7,6},{8,9},{9,8},{10,11... | collective-permute-start | bytes 294920 | tf_op jit(solution)/shard_map/ppermute | solution.py:18
  (4 other events, 3.2 us)

commit v2 on v1

--- a/solution.py
+++ b/solution.py
@@ -18,14 +18,18 @@
     return lax.ppermute(x, axis, [(i, i ^ bits) for i in range(n)])
 
 
+def near(x):
+    return pltpu.with_memory_space_constraint(x, pltpu.VMEM)
+
+
 def call(kernel, outs, *args, scratch=()):
     return pl.pallas_call(
         kernel,
-        out_shape=outs,
+        out_shape=[pltpu.VMEM(o.shape, o.dtype) for o in outs],
         in_specs=[VMEM] * len(args),
-        out_specs=jax.tree.map(lambda _: VMEM, outs),
+        out_specs=[VMEM] * len(outs),
         scratch_shapes=list(scratch),
-    )(*args)
+    )(*[near(x) for x in args])
 
 
 def dist_kernel(order, points_ref, *refs):
@@ -105,7 +109,7 @@
     part = jax.ShapeDtypeStruct((half, local_points), F32)
     mine, other = call(
         lambda *r: dist_kernel(order, *r),
-        (part, part),
+        [part, part],
         points,
         *[tiles[k] for k in order],
         scratch=[pltpu.VMEM((all_rows, points.shape[1]), BF16), pltpu.VMEM((all_rows, local_points), F32)],
@@ -113,9 +117,9 @@
     mine = mine + swap(other, "feat", 1)
     far = swap(mine, "feat", 2)
     size = half + rows * (coefs.shape[1] // LANES)
-    tile = call(
+    (tile,) = call(
         lambda *r: send_kernel(float(features), *r),
-        jax.ShapeDtypeStruct((size, local_points), BF16),
+        [jax.ShapeDtypeStruct((size, local_points), BF16)],
         mine,
         far,
         coefs,
@@ -124,15 +128,16 @@
     across = swap(column, "blk", 1)
     orders = [[0] + line, [1] + [k ^ 1 for k in line]]
     scale = 1.0 / math.sqrt(local_points * blks)
-    return call(
+    (out,) = call(
         lambda *r: product_kernel(orders, rows, scale, *r),
-        jax.ShapeDtypeStruct((rows, coefs.shape[1]), F32),
+        [jax.ShapeDtypeStruct((rows, coefs.shape[1]), F32)],
         column,
         across,
         swap(column, "feat", 1),
         swap(across, "feat", 1),
         scratch=[pltpu.VMEM((all_rows, local_points * blks), BF16), pltpu.VMEM((all_rows, coefs.shape[1]), BF16)],
     )
+    return out
 
 
 def on_device_large(points, centers, coefs):

time: 45.6 us -> 39.5 us (0.87)
  Pallas kernels: 5.93 us -> 1.01 us
  other arithmetic: 1.51 us -> 0.01 us
  local copies, waits for them, and re-layouts: 1.89 us -> 2.56 us
    pallas_call x3, Pallas kernels: 5.93 us -> 1.01 us  [call(): pl.pallas_call(kernel, out_shape=[pltpu.VMEM(o.shape, o.dtype) for o in o...]
    add x1, other arithmetic: 0.77 us -> 0.01 us  [on_device(): mine = mine + swap(other, 'feat', 1)]
    concatenate x1, other arithmetic: 0.74 us -> 0.01 us  [on_device(): jnp.concatenate([tile] + [swap(tile, 'blk', k) for k in line], axis=0)]
    unnamed x26 -> x7, local copies, waits for them, and re-layouts: 1.89 us -> 2.56 us
  transfers between devices with their start and end apart: 15 -> 15, of which waited for: 10 -> 9; matrix products, arithmetic and copies ran while one was open for 0% -> 0% of each run, Pallas kernels for 0% -> 0%
where the time goes in v2:
time: 39.5 us; the launch traced here: 39.3 us
  starting transfers between devices  18.6 us (47%)
  waiting for transfers between devices  17.1 us (43%)
  local copies, waits for them, and re-layouts  2.56 us (6%)
  Pallas kernels  1.01 us (3%)
    ppermute x15, starting transfers between devices, swap(): return lax.ppermute(x, axis, [(i, i ^ bits) for i in range(n)])  18.6 us
    ppermute x15, waiting for transfers between devices, swap(): return lax.ppermute(x, axis, [(i, i ^ bits) for i in range(n)])  17.1 us
    unnamed x7, local copies, waits for them, and re-layouts  2.56 us
    pallas_call x3, Pallas kernels, call(): pl.pallas_call(kernel, out_shape=[pltpu.VMEM(o.shape, o.dtype) for o in o...  1.01 us
  transfers between devices with their start and end apart: 15, of which 9 were waited for; matrix products, arithmetic and copies ran while one was open for 0% of the time, Pallas kernels for 0%

profile of v2, /device:TPU:0, one launch (start us, length us, event | category | flops | bytes accessed | tf_op | source)
XLA Modules:
  0.0 39.3 jit_solution(13966902794402575153)
XLA Ops:
  0.0 4.0 %collective-permute-start.3 = (bf16[16,2048]{1,0:T(8,128)(2,1)}, bf16[16,2048]{1,0:T(8,128)(2,1)S(1)}, u32[]{:S(2)}, u32[]{:S(2)}) collective-permute-start(bf16[16,2048]{1,0:T(8,128)(2,1)} %r_1_.1), channel_id=1, source_target_pairs={{0,16},{4,20},{8,24},{12,28},{16,0},{20,4},{24,8},{28,12},{1,17},{... | collective-permute-start | bytes 196616 | tf_op jit(solution)/shard_map/ppermute | solution.py:18
  4.0 1.6 %collective-permute-start.1 = (bf16[16,2048]{1,0:T(8,128)(2,1)}, bf16[16,2048]{1,0:T(8,128)(2,1)S(1)}, u32[]{:S(2)}, u32[]{:S(2)}) collective-permute-start(bf16[16,2048]{1,0:T(8,128)(2,1)} %r_1_.1), channel_id=1, source_target_pairs={{0,8},{4,12},{8,0},{12,4},{16,24},{20,28},{24,16},{28,20},{1,9},{5... | collective-permute-start | bytes 196616 | tf_op jit(solution)/shard_map/ppermute | solution.py:18
  5.6 1.7 %collective-permute-start = (bf16[16,2048]{1,0:T(8,128)(2,1)}, bf16[16,2048]{1,0:T(8,128)(2,1)S(1)}, u32[]{:S(2)}, u32[]{:S(2)}) collective-permute-start(bf16[16,2048]{1,0:T(8,128)(2,1)} %r_1_.1), channel_id=1, source_target_pairs={{0,4},{4,0},{8,12},{12,8},{16,20},{20,16},{24,28},{28,24},{1,5},{5... | collective-permute-start | bytes 196616 | tf_op jit(solution)/shard_map/ppermute | solution.py:18
  7.3 1.8 %collective-permute-start.4 = (bf16[16,2048]{1,0:T(8,128)(2,1)S(1)}, bf16[16,2048]{1,0:T(8,128)(2,1)S(1)}, u32[]{:S(2)}, u32[]{:S(2)}) collective-permute-start(bf16[16,2048]{1,0:T(8,128)(2,1)S(1)} %collective-permute-done.3.r_5_), channel_id=1, source_target_pairs={{0,4},{4,0},{8,12},{12,8},{16,20},{20,16},{24,28},{28,24},{1,5},{5... | collective-permute-start | bytes 196616 | tf_op jit(solution)/shard_map/ppermute | solution.py:18
  9.2 0.9 %collective-permute-start.2 = (bf16[16,2048]{1,0:T(8,128)(2,1)S(1)}, bf16[16,2048]{1,0:T(8,128)(2,1)S(1)}, u32[]{:S(2)}, u32[]{:S(2)}) collective-permute-start(bf16[16,2048]{1,0:T(8,128)(2,1)S(1)} %collective-permute-done.1.r_3_), channel_id=1, source_target_pairs={{0,4},{4,0},{8,12},{12,8},{16,20},{20,16},{24,28},{28,24},{1,5},{5... | collective-permute-start | bytes 196616 | tf_op jit(solution)/shard_map/ppermute | solution.py:18
  10.0 1.9 %collective-permute-done.5.r_7_ = bf16[16,2048]{1,0:T(8,128)(2,1)S(1)} collective-permute-done((bf16[16,2048]{1,0:T(8,128)(2,1)}, bf16[16,2048]{1,0:T(8,128)(2,1)S(1)}, u32[]{:S(2)}, u32[]{:S(2)}) %collective-permute-start.5) | collective-permute-done | bytes 65568 | tf_op jit(solution)/shard_map/ppermute | solution.py:18
  11.9 1.5 %collective-permute-start.6 = (bf16[16,2048]{1,0:T(8,128)(2,1)S(1)}, bf16[16,2048]{1,0:T(8,128)(2,1)S(1)}, u32[]{:S(2)}, u32[]{:S(2)}) collective-permute-start(bf16[16,2048]{1,0:T(8,128)(2,1)S(1)} %collective-permute-done.5.r_7_), channel_id=1, source_target_pairs={{0,4},{4,0},{8,12},{12,8},{16,20},{20,16},{24,28},{28,24},{1,5},{5... | collective-permute-start | bytes 196616 | tf_op jit(solution)/shard_map/ppermute | solution.py:18
  13.4 0.7 %collective-permute-done.2.r_4_ = bf16[16,2048]{1,0:T(8,128)(2,1)S(1)} collective-permute-done((bf16[16,2048]{1,0:T(8,128)(2,1)S(1)}, bf16[16,2048]{1,0:T(8,128)(2,1)S(1)}, u32[]{:S(2)}, u32[]{:S(2)}) %collective-permute-start.2) | collective-permute-done | bytes 65568 | tf_op jit(solution)/shard_map/ppermute | solution.py:18
  14.1 2.0 %collective-permute-done.6.r_8_ = bf16[16,2048]{1,0:T(8,128)(2,1)S(1)} collective-permute-done((bf16[16,2048]{1,0:T(8,128)(2,1)S(1)}, bf16[16,2048]{1,0:T(8,128)(2,1)S(1)}, u32[]{:S(2)}, u32[]{:S(2)}) %collective-permute-start.6) | collective-permute-done | bytes 65568 | tf_op jit(solution)/shard_map/ppermute | solution.py:18
  16.2 1.0 %copy-done = bf16[128,2048]{1,0:T(8,128)(2,1)S(1)} copy-done((bf16[128,2048]{1,0:T(8,128)(2,1)S(1)}, bf16[128,2048]{1,0:T(8,128)(2,1)}, u32[]{:S(2)}) %copy-start) | copy-done | bytes 524312
  17.2 0.8 %copy-done.1 = bf16[16,2048]{1,0:T(8,128)(2,1)S(1)} copy-done((bf16[16,2048]{1,0:T(8,128)(2,1)S(1)}, bf16[16,2048]{1,0:T(8,128)(2,1)}, u32[]{:S(2)}) %copy-start.1) | copy-done | bytes 65560
  18.0 0.4 %shard_map.37 = (f32[64,128]{1,0:T(8,128)S(1)}, f32[64,128]{1,0:T(8,128)S(1)}) custom-call(bf16[128,2048]{1,0:T(8,128)(2,1)S(1)} %copy-done, bf16[16,2048]{1,0:T(8,128)(2,1)S(1)} %copy-done.1, bf16[16,2048]{1,0:T(8,128)(2,1)S(1)} %collective-permute-done.r_2_, bf16[16,2048]{1,0:T(8,128)(2,1)S(1)} %collective-permute-done.1.r_3_, ...), custom_call_target="tpu_custom_call" | custom-call | tf_op jit(solution)/shard_map/pallas_call | solution.py:26
  18.6 1.2 %collective-permute-done.7 = f32[64,128]{1,0:T(8,128)S(1)} collective-permute-done((f32[64,128]{1,0:T(8,128)S(1)}, f32[64,128]{1,0:T(8,128)S(1)}, u32[]{:S(2)}, u32[]{:S(2)}) %collective-permute-start.7) | collective-permute-done | bytes 32800 | tf_op jit(solution)/shard_map/ppermute | solution.py:18
  19.8 1.6 %collective-permute-start.8 = (f32[64,128]{1,0:T(8,128)S(1)}, f32[64,128]{1,0:T(8,128)S(1)}, u32[]{:S(2)}, u32[]{:S(2)}) collective-permute-start(f32[64,128]{1,0:T(8,128)S(1)} %add.3.r_0_), channel_id=1, source_target_pairs={{0,2},{1,3},{2,0},{3,1},{4,6},{5,7},{6,4},{7,5},{8,10},{9,11},{10,... | collective-permute-start | bytes 98312 | tf_op jit(solution)/shard_map/ppermute | solution.py:18
  21.4 2.4 %collective-permute-done.8.r_1_ = f32[64,128]{1,0:T(8,128)S(1)} collective-permute-done((f32[64,128]{1,0:T(8,128)S(1)}, f32[64,128]{1,0:T(8,128)S(1)}, u32[]{:S(2)}, u32[]{:S(2)}) %collective-permute-start.8) | collective-permute-done | bytes 32800 | tf_op jit(solution)/shard_map/ppermute | solution.py:18
  24.1 3.3 %collective-permute-start.10 = (bf16[96,128]{1,0:T(8,128)(2,1)S(1)}, bf16[96,128]{1,0:T(8,128)(2,1)S(1)}, u32[]{:S(2)}, u32[]{:S(2)}) collective-permute-start(bf16[96,128]{1,0:T(8,128)(2,1)S(1)} %shard_map.38), channel_id=1, source_target_pairs={{0,24},{4,28},{8,16},{12,20},{16,8},{20,12},{24,0},{28,4},{1,25},{... | collective-permute-start | bytes 73736 | tf_op jit(solution)/shard_map/ppermute | solution.py:18
  27.4 0.5 %collective-permute-start.9 = (bf16[96,128]{1,0:T(8,128)(2,1)S(1)}, bf16[96,128]{1,0:T(8,128)(2,1)S(1)}, u32[]{:S(2)}, u32[]{:S(2)}) collective-permute-start(bf16[96,128]{1,0:T(8,128)(2,1)S(1)} %shard_map.38), channel_id=1, source_target_pairs={{0,16},{4,20},{8,24},{12,28},{16,0},{20,4},{24,8},{28,12},{1,17},{... | collective-permute-start | bytes 73736 | tf_op jit(solution)/shard_map/ppermute | solution.py:18
  27.9 1.9 %collective-permute-done.10 = bf16[96,128]{1,0:T(8,128)(2,1)S(1)} collective-permute-done((bf16[96,128]{1,0:T(8,128)(2,1)S(1)}, bf16[96,128]{1,0:T(8,128)(2,1)S(1)}, u32[]{:S(2)}, u32[]{:S(2)}) %collective-permute-start.10) | collective-permute-done | bytes 24608 | tf_op jit(solution)/shard_map/ppermute | solution.py:18
  29.8 2.3 %collective-permute-done.9 = bf16[96,128]{1,0:T(8,128)(2,1)S(1)} collective-permute-done((bf16[96,128]{1,0:T(8,128)(2,1)S(1)}, bf16[96,128]{1,0:T(8,128)(2,1)S(1)}, u32[]{:S(2)}, u32[]{:S(2)}) %collective-permute-start.9) | collective-permute-done | bytes 24608 | tf_op jit(solution)/shard_map/ppermute | solution.py:18
  32.1 1.4 %collective-permute-start.12 = (bf16[384,128]{1,0:T(8,128)(2,1)S(1)}, bf16[384,128]{1,0:T(8,128)(2,1)S(1)}, u32[]{:S(2)}, u32[]{:S(2)}) collective-permute-start(bf16[384,128]{1,0:T(8,128)(2,1)S(1)} %pad_maximum_fusion.r_0_), channel_id=1, source_target_pairs={{0,4},{4,0},{8,12},{12,8},{16,20},{20,16},{24,28},{28,24},{1,5},{5... | collective-permute-start | bytes 294920 | tf_op jit(solution)/shard_map/ppermute | solution.py:18
  33.5 3.3 %collective-permute-done.12.r_1_ = bf16[384,128]{1,0:T(8,128)(2,1)S(1)} collective-permute-done((bf16[384,128]{1,0:T(8,128)(2,1)S(1)}, bf16[384,128]{1,0:T(8,128)(2,1)S(1)}, u32[]{:S(2)}, u32[]{:S(2)}) %collective-permute-start.12) | collective-permute-done | bytes 98336 | tf_op jit(solution)/shard_map/ppermute | solution.py:18
  36.8 1.3 %collective-permute-done.14.r_3_ = bf16[384,128]{1,0:T(8,128)(2,1)S(1)} collective-permute-done((bf16[384,128]{1,0:T(8,128)(2,1)S(1)}, bf16[384,128]{1,0:T(8,128)(2,1)S(1)}, u32[]{:S(2)}, u32[]{:S(2)}) %collective-permute-start.14) | collective-permute-done | bytes 98336 | tf_op jit(solution)/shard_map/ppermute | solution.py:18
  38.1 0.6 %shard_map.39 = f32[16,256]{1,0:T(8,128)S(1)} custom-call(bf16[384,128]{1,0:T(8,128)(2,1)S(1)} %pad_maximum_fusion.r_0_, bf16[384,128]{1,0:T(8,128)(2,1)S(1)} %collective-permute-done.12.r_1_, bf16[384,128]{1,0:T(8,128)(2,1)S(1)} %collective-permute-done.13.r_2_, bf16[384,128]{1,0:T(8,128)(2,1)S(1)} %collective-permute-done.14.r_3_), custom_call_target="tpu_custom_call" | custom-call | tf_op jit(solution)/shard_map/pallas_call | solution.py:26
  38.6 0.7 %copy.4 = f32[16,256]{1,0:T(8,128)} copy(f32[16,256]{1,0:T(8,128)S(1)} %shard_map.39) | data formatting | bytes 32768
  (18 shorter events, 0.5 us)
Async XLA Ops:
  0.0 7.3 %collective-permute-start.3 = (bf16[16,2048]{1,0:T(8,128)(2,1)}, bf16[16,2048]{1,0:T(8,128)(2,1)S(1)}, u32[]{:S(2)}, u32[]{:S(2)}) collective-permute-start(bf16[16,2048]{1,0:T(8,128)(2,1)} %r_1_.1), channel_id=1, source_target_pairs={{0,16},{4,20},{8,24},{12,28},{16,0},{20,4},{24,8},{28,12},{1,17},{... | collective-permute-start | bytes 196616 | tf_op jit(solution)/shard_map/ppermute | solution.py:18
  4.0 5.1 %collective-permute-start.1 = (bf16[16,2048]{1,0:T(8,128)(2,1)}, bf16[16,2048]{1,0:T(8,128)(2,1)S(1)}, u32[]{:S(2)}, u32[]{:S(2)}) collective-permute-start(bf16[16,2048]{1,0:T(8,128)(2,1)} %r_1_.1), channel_id=1, source_target_pairs={{0,8},{4,12},{8,0},{12,4},{16,24},{20,28},{24,16},{28,20},{1,9},{5... | collective-permute-start | bytes 196616 | tf_op jit(solution)/shard_map/ppermute | solution.py:18
  5.6 6.3 %collective-permute-start.5 = (bf16[16,2048]{1,0:T(8,128)(2,1)}, bf16[16,2048]{1,0:T(8,128)(2,1)S(1)}, u32[]{:S(2)}, u32[]{:S(2)}) collective-permute-start(bf16[16,2048]{1,0:T(8,128)(2,1)} %r_1_.1), channel_id=1, source_target_pairs={{0,24},{4,28},{8,16},{12,20},{16,8},{20,12},{24,0},{28,4},{1,25},{... | collective-permute-start | bytes 196616 | tf_op jit(solution)/shard_map/ppermute | solution.py:18
  5.6 7.8 %collective-permute-start = (bf16[16,2048]{1,0:T(8,128)(2,1)}, bf16[16,2048]{1,0:T(8,128)(2,1)S(1)}, u32[]{:S(2)}, u32[]{:S(2)}) collective-permute-start(bf16[16,2048]{1,0:T(8,128)(2,1)} %r_1_.1), channel_id=1, source_target_pairs={{0,4},{4,0},{8,12},{12,8},{16,20},{20,16},{24,28},{28,24},{1,5},{5... | collective-permute-start | bytes 196616 | tf_op jit(solution)/shard_map/ppermute | solution.py:18
  7.3 6.1 %collective-permute-start.4 = (bf16[16,2048]{1,0:T(8,128)(2,1)S(1)}, bf16[16,2048]{1,0:T(8,128)(2,1)S(1)}, u32[]{:S(2)}, u32[]{:S(2)}) collective-permute-start(bf16[16,2048]{1,0:T(8,128)(2,1)S(1)} %collective-permute-done.3.r_5_), channel_id=1, source_target_pairs={{0,4},{4,0},{8,12},{12,8},{16,20},{20,16},{24,28},{28,24},{1,5},{5... | collective-permute-start | bytes 196616 | tf_op jit(solution)/shard_map/ppermute | solution.py:18
  9.2 5.0 %collective-permute-start.2 = (bf16[16,2048]{1,0:T(8,128)(2,1)S(1)}, bf16[16,2048]{1,0:T(8,128)(2,1)S(1)}, u32[]{:S(2)}, u32[]{:S(2)}) collective-permute-start(bf16[16,2048]{1,0:T(8,128)(2,1)S(1)} %collective-permute-done.1.r_3_), channel_id=1, source_target_pairs={{0,4},{4,0},{8,12},{12,8},{16,20},{20,16},{24,28},{28,24},{1,5},{5... | collective-permute-start | bytes 196616 | tf_op jit(solution)/shard_map/ppermute | solution.py:18
  11.9 4.3 %collective-permute-start.6 = (bf16[16,2048]{1,0:T(8,128)(2,1)S(1)}, bf16[16,2048]{1,0:T(8,128)(2,1)S(1)}, u32[]{:S(2)}, u32[]{:S(2)}) collective-permute-start(bf16[16,2048]{1,0:T(8,128)(2,1)S(1)} %collective-permute-done.5.r_7_), channel_id=1, source_target_pairs={{0,4},{4,0},{8,12},{12,8},{16,20},{20,16},{24,28},{28,24},{1,5},{5... | collective-permute-start | bytes 196616 | tf_op jit(solution)/shard_map/ppermute | solution.py:18
  16.2 1.0 %copy-start = (bf16[128,2048]{1,0:T(8,128)(2,1)S(1)}, bf16[128,2048]{1,0:T(8,128)(2,1)}, u32[]{:S(2)}) copy-start(bf16[128,2048]{1,0:T(8,128)(2,1)} %r_0_.1) | copy-start | bytes 1572868
  17.2 0.8 %copy-start.1 = (bf16[16,2048]{1,0:T(8,128)(2,1)S(1)}, bf16[16,2048]{1,0:T(8,128)(2,1)}, u32[]{:S(2)}) copy-start(bf16[16,2048]{1,0:T(8,128)(2,1)} %r_1_.1) | copy-start | bytes 196612
  18.5 1.3 %collective-permute-start.7 = (f32[64,128]{1,0:T(8,128)S(1)}, f32[64,128]{1,0:T(8,128)S(1)}, u32[]{:S(2)}, u32[]{:S(2)}) collective-permute-start(f32[64,128]{1,0:T(8,128)S(1)} %get-tuple-element.8), channel_id=1, source_target_pairs={{0,1},{1,0},{2,3},{3,2},{4,5},{5,4},{6,7},{7,6},{8,9},{9,8},{10,11... | collective-permute-start | bytes 98312 | tf_op jit(solution)/shard_map/ppermute | solution.py:18
  19.8 4.0 %copy-start.2 = (bf16[16,256]{1,0:T(8,128)(2,1)S(1)}, bf16[16,256]{1,0:T(8,128)(2,1)}, u32[]{:S(2)}) copy-start(bf16[16,256]{1,0:T(8,128)(2,1)} %r_2_.1) | copy-start | bytes 24580
  19.8 4.0 %collective-permute-start.8 = (f32[64,128]{1,0:T(8,128)S(1)}, f32[64,128]{1,0:T(8,128)S(1)}, u32[]{:S(2)}, u32[]{:S(2)}) collective-permute-start(f32[64,128]{1,0:T(8,128)S(1)} %add.3.r_0_), channel_id=1, source_target_pairs={{0,2},{1,3},{2,0},{3,1},{4,6},{5,7},{6,4},{7,5},{8,10},{9,11},{10,... | collective-permute-start | bytes 98312 | tf_op jit(solution)/shard_map/ppermute | solution.py:18
  23.8 4.1 %collective-permute-start.11 = (bf16[96,128]{1,0:T(8,128)(2,1)S(1)}, bf16[96,128]{1,0:T(8,128)(2,1)S(1)}, u32[]{:S(2)}, u32[]{:S(2)}) collective-permute-start(bf16[96,128]{1,0:T(8,128)(2,1)S(1)} %shard_map.38), channel_id=1, source_target_pairs={{0,8},{4,12},{8,0},{12,4},{16,24},{20,28},{24,16},{28,20},{1,9},{5... | collective-permute-start | bytes 73736 | tf_op jit(solution)/shard_map/ppermute | solution.py:18
  24.1 5.7 %collective-permute-start.10 = (bf16[96,128]{1,0:T(8,128)(2,1)S(1)}, bf16[96,128]{1,0:T(8,128)(2,1)S(1)}, u32[]{:S(2)}, u32[]{:S(2)}) collective-permute-start(bf16[96,128]{1,0:T(8,128)(2,1)S(1)} %shard_map.38), channel_id=1, source_target_pairs={{0,24},{4,28},{8,16},{12,20},{16,8},{20,12},{24,0},{28,4},{1,25},{... | collective-permute-start | bytes 73736 | tf_op jit(solution)/shard_map/ppermute | solution.py:18
  27.4 4.7 %collective-permute-start.9 = (bf16[96,128]{1,0:T(8,128)(2,1)S(1)}, bf16[96,128]{1,0:T(8,128)(2,1)S(1)}, u32[]{:S(2)}, u32[]{:S(2)}) collective-permute-start(bf16[96,128]{1,0:T(8,128)(2,1)S(1)} %shard_map.38), channel_id=1, source_target_pairs={{0,16},{4,20},{8,24},{12,28},{16,0},{20,4},{24,8},{28,12},{1,17},{... | collective-permute-start | bytes 73736 | tf_op jit(solution)/shard_map/ppermute | solution.py:18
  32.1 4.7 %collective-permute-start.12 = (bf16[384,128]{1,0:T(8,128)(2,1)S(1)}, bf16[384,128]{1,0:T(8,128)(2,1)S(1)}, u32[]{:S(2)}, u32[]{:S(2)}) collective-permute-start(bf16[384,128]{1,0:T(8,128)(2,1)S(1)} %pad_maximum_fusion.r_0_), channel_id=1, source_target_pairs={{0,4},{4,0},{8,12},{12,8},{16,20},{20,16},{24,28},{28,24},{1,5},{5... | collective-permute-start | bytes 294920 | tf_op jit(solution)/shard_map/ppermute | solution.py:18
  33.5 3.3 %collective-permute-start.13 = (bf16[384,128]{1,0:T(8,128)(2,1)S(1)}, bf16[384,128]{1,0:T(8,128)(2,1)S(1)}, u32[]{:S(2)}, u32[]{:S(2)}) collective-permute-start(bf16[384,128]{1,0:T(8,128)(2,1)S(1)} %pad_maximum_fusion.r_0_), channel_id=1, source_target_pairs={{0,1},{1,0},{2,3},{3,2},{4,5},{5,4},{6,7},{7,6},{8,9},{9,8},{10,11... | collective-permute-start | bytes 294920 | tf_op jit(solution)/shard_map/ppermute | solution.py:18
  36.8 1.3 %collective-permute-start.14 = (bf16[384,128]{1,0:T(8,128)(2,1)S(1)}, bf16[384,128]{1,0:T(8,128)(2,1)S(1)}, u32[]{:S(2)}, u32[]{:S(2)}) collective-permute-start(bf16[384,128]{1,0:T(8,128)(2,1)S(1)} %collective-permute-done.12.r_1_), channel_id=1, source_target_pairs={{0,1},{1,0},{2,3},{3,2},{4,5},{5,4},{6,7},{7,6},{8,9},{9,8},{10,11... | collective-permute-start | bytes 294920 | tf_op jit(solution)/shard_map/ppermute | solution.py:18

commit v3 on v2

v3 whole, which is shorter than its diff:
```python
import math

import jax
import jax.numpy as jnp
from jax import lax
from jax.experimental import pallas as pl
from jax.experimental.pallas import tpu as pltpu
from jax.sharding import PartitionSpec as P

BF16 = jnp.bfloat16
F32 = jnp.float32
LANES = 128
VMEM = pl.BlockSpec(memory_space=pltpu.VMEM)


def swap(x, axis, bits):
    n = lax.axis_size(axis)
    return lax.ppermute(x, axis, [(i, i ^ bits) for i in range(n)])


def near(x):
    return pltpu.with_memory_space_constraint(x, pltpu.VMEM)


def call(kernel, outs, *args, scratch=()):
    return pl.pallas_call(
        kernel,
        out_shape=[pltpu.VMEM(o.shape, o.dtype) for o in outs],
        in_specs=[VMEM] * len(args),
        out_specs=[VMEM] * len(outs),
        scratch_shapes=list(scratch),
    )(*[near(x) for x in args])


def prepare_kernel(points_ref, centers_ref, points_out, centers_out, square_out):
    points_out[...] = points_ref[...]
    centers_out[...] = centers_ref[...]
    wide = points_ref[...].astype(F32)
    square_out[...] = jnp.sum((wide * wide).T, axis=0, keepdims=True)


def dist_kernel(order, points_ref, square_ref, *refs):
    tiles, (part_ref, centers) = refs[: len(order)], refs[len(order) :]
    rows = tiles[0].shape[0]
    blk = lax.axis_index("blk")
    for k, tile in zip(order, tiles):
        at = pl.multiple_of((blk ^ k) * rows, rows)
        centers[pl.ds(at, rows), :] = tile[...]
    cross = lax.dot_general(
        centers[...], points_ref[...], (((1,), (1,)), ((), ())), preferred_element_type=F32
    )
    wide = centers[...].astype(F32)
    center_sq = jnp.sum(wide * wide, axis=1, keepdims=True)
    part_ref[...] = square_ref[...] + center_sq - 2.0 * cross


def send_kernel(features, a_ref, b_ref, coefs_ref, others_ref, out_ref):
    all_rows, rows = a_ref.shape[0], coefs_ref.shape[0]
    out_ref[:all_rows, :] = jnp.exp(-(a_ref[...] + b_ref[...]) / features).astype(BF16)
    core = lax.axis_index("feat") % 2
    pieces = coefs_ref.shape[1] // LANES
    for half, ref in ((core, coefs_ref), (1 - core, others_ref)):
        for i in range(pieces):
            at = pl.multiple_of(all_rows + (half * pieces + i) * rows, rows)
            out_ref[pl.ds(at, rows), :] = ref[:, i * LANES : (i + 1) * LANES]


def product_kernel(mine_order, other_order, rows, scale, *refs):
    n, m = len(mine_order[0]), len(other_order[0])
    tiles, (out_ref, kernel, coefs) = refs[: n + m], refs[n + m :]
    all_rows = kernel.shape[0]
    blk = lax.axis_index("blk")
    core = lax.axis_index("feat") % 2
    pieces = coefs.shape[1] // LANES
    for i, tile in enumerate(tiles):
        a, b = (mine_order[0][i], mine_order[1][i]) if i < n else (other_order[0][i - n], other_order[1][i - n])
        kernel[:, i * LANES : (i + 1) * LANES] = tile[:all_rows, :]
        at = pl.multiple_of((blk ^ jnp.where(core == 0, a, b)) * rows, rows)
        for j in range(pieces):
            top = pl.multiple_of(all_rows + (core * pieces + j) * rows, rows)
            coefs[pl.ds(at, rows), j * LANES : (j + 1) * LANES] = tile[pl.ds(top, rows), :]
    fitted = lax.dot_general(
        coefs[...].T, kernel[...], (((1,), (0,)), ((), ())), preferred_element_type=F32
    ).astype(BF16)
    own = kernel[pl.ds(pl.multiple_of(blk * rows, rows), rows), :]
    out_ref[...] = scale * lax.dot_general(
        own, fitted, (((1,), (1,)), ((), ())), preferred_element_type=F32
    )


def swap_by_core(x, even, odd):
    feats, blks = lax.axis_size("feat"), lax.axis_size("blk")
    pairs = [
        (b * feats + f, (b ^ (odd if f % 2 else even)) * feats + f)
        for b in range(blks)
        for f in range(feats)
    ]
    return lax.ppermute(x, ("blk", "feat"), pairs)


def on_device(points, centers, coefs):
    blks = lax.axis_size("blk")
    rows, local_points = centers.shape[0], points.shape[0]
    features = points.shape[1] * lax.axis_size("feat")
    all_rows = rows * blks
    line = [k for k in (4, 6, 2) if k < blks]

    tiles = {}
    for k in line:
        tiles[k] = swap(centers, "blk", k)
    tiles[1] = swap(centers, "blk", 1)
    for k in line:
        tiles[k ^ 1] = swap(tiles[k], "blk", 1)
    points, tiles[0], square = pl.pallas_call(
        prepare_kernel,
        out_shape=[pltpu.VMEM(points.shape, BF16), pltpu.VMEM(centers.shape, BF16), pltpu.VMEM((1, local_points), F32)],
        in_specs=[VMEM] * 2,
        out_specs=[VMEM] * 3,
        cost_estimate=pl.CostEstimate(flops=2 * points.size, bytes_accessed=2 * points.size, transcendentals=0),
    )(points, centers)
    others = swap(coefs, "feat", 1)
    order = sorted(tiles)
    (part,) = call(
        lambda *r: dist_kernel(order, *r),
        [jax.ShapeDtypeStruct((all_rows, local_points), F32)],
        points,
        square,
        *[tiles[k] for k in order],
        scratch=[pltpu.VMEM((all_rows, points.shape[1]), BF16)],
    )
    part = part + swap(part, "feat", 1)
    far = swap(part, "feat", 2)
    pieces = coefs.shape[1] // LANES
    (tile,) = call(
        lambda *r: send_kernel(float(features), *r),
        [jax.ShapeDtypeStruct((all_rows + 2 * pieces * rows, local_points), BF16)],
        part,
        far,
        coefs,
        others,
    )
    mine_order = ([0, 4, 5, 3, 2], [0, 6, 7, 1, 2])
    mine = [tile] + [swap_by_core(tile, a, b) for a, b in list(zip(*mine_order))[1:]]
    other_order = (mine_order[1][1:-1], mine_order[0][1:-1])
    other = [swap(x, "feat", 1) for x in mine[1:-1]]
    scale = 1.0 / math.sqrt(local_points * blks)
    (out,) = call(
        lambda *r: product_kernel(mine_order, other_order, rows, scale, *r),
        [jax.ShapeDtypeStruct((rows, coefs.shape[1]), F32)],
        *mine,
        *other,
        scratch=[pltpu.VMEM((all_rows, local_points * blks), BF16), pltpu.VMEM((all_rows, coefs.shape[1]), BF16)],
    )
    return out


def on_device_large(points, centers, coefs):
    features = points.shape[1] * lax.axis_size("feat")
    point_sq = jnp.einsum("nf,nf->n", points, points, preferred_element_type=F32)
    center_piece = lax.all_gather(centers, "blk", axis=0, tiled=True)
    center_sq = jnp.einsum("mf,mf->m", center_piece, center_piece, preferred_element_type=F32)
    cross_dot = lax.dot_general(
        points, center_piece, (((1,), (1,)), ((), ())), preferred_element_type=F32
    )
    dist_tile = point_sq[:, None] + center_sq[None, :] - 2.0 * cross_dot
    all_coefs = lax.all_gather(coefs, "blk", axis=0, tiled=True)
    dist = lax.psum(dist_tile, "feat")
    kernel = jnp.exp(-dist / features).astype(BF16)
    fitted = jnp.dot(kernel, all_coefs, preferred_element_type=F32).astype(BF16)
    summed = lax.psum_scatter(
        lax.dot_general(kernel, fitted, (((0,), (0,)), ((), ())), preferred_element_type=F32),
        "blk",
        scatter_dimension=0,
        tiled=True,
    )
    return summed * (1.0 / math.sqrt(points.shape[0] * lax.axis_size("blk")))


def solution(mesh):
    small = mesh.shape["blk"] == 8 and mesh.shape["feat"] == 4
    in_specs = (P("blk", "feat"), P("blk", "feat"), P("blk", "feat"))
    return jax.shard_map(
        on_device if small else on_device_large,
        mesh=mesh,
        in_specs=in_specs,
        out_specs=P("blk", "feat"),
        check_vma=False,
    )
```

time: 39.5 us -> 34 us (0.86)
  waiting for transfers between devices: 17.1 us -> 12.6 us
  local copies, waits for them, and re-layouts: 2.56 us -> 0.68 us
  Pallas kernels: 1.01 us -> 2.34 us
  starting transfers between devices: 18.6 us -> 18.1 us
    ppermute x15 -> x13, waiting for transfers between devices: 17.1 us -> 9.49 us  [swap(): return lax.ppermute(x, axis, [(i, i ^ bits) for i in range(n)])]
    ppermute x15 -> x13, starting transfers between devices: 18.6 us -> 12.2 us  [swap(): return lax.ppermute(x, axis, [(i, i ^ bits) for i in range(n)])]
    ppermute x0 -> x4, starting transfers between devices: none -> 5.91 us  [swap_by_core(): return lax.ppermute(x, ('blk', 'feat'), pairs)]
    ppermute x0 -> x4, waiting for transfers between devices: none -> 3.09 us  [swap_by_core(): return lax.ppermute(x, ('blk', 'feat'), pairs)]
    unnamed x7 -> x3, local copies, waits for them, and re-layouts: 2.56 us -> 0.68 us
    pallas_call x0 -> x1, Pallas kernels: none -> 1.41 us  [on_device(): pl.pallas_call(prepare_kernel, out_shape=[pltpu.VMEM(points.shape, BF16),...]
  transfers between devices with their start and end apart: 15 -> 17, of which waited for: 9 -> 9; matrix products, arithmetic and copies ran while one was open for 0% -> 0% of each run, Pallas kernels for 0% -> 4%
where the time goes in v3:
time: 34 us; the launch traced here: 33.8 us
  starting transfers between devices  18.1 us (53%)
  waiting for transfers between devices  12.6 us (37%)
  Pallas kernels  2.34 us (7%)
  local copies, waits for them, and re-layouts  0.68 us (2%)
    ppermute x13, starting transfers between devices, swap(): return lax.ppermute(x, axis, [(i, i ^ bits) for i in range(n)])  12.2 us
    ppermute x13, waiting for transfers between devices, swap(): return lax.ppermute(x, axis, [(i, i ^ bits) for i in range(n)])  9.49 us
    ppermute x4, starting transfers between devices, swap_by_core(): return lax.ppermute(x, ('blk', 'feat'), pairs)  5.91 us
    ppermute x4, waiting for transfers between devices, swap_by_core(): return lax.ppermute(x, ('blk', 'feat'), pairs)  3.09 us
    pallas_call x1, Pallas kernels, on_device(): pl.pallas_call(prepare_kernel, out_shape=[pltpu.VMEM(points.shape, BF16),...  1.41 us
    pallas_call x3, Pallas kernels, call(): pl.pallas_call(kernel, out_shape=[pltpu.VMEM(o.shape, o.dtype) for o in o...  0.93 us
  transfers between devices with their start and end apart: 17, of which 9 were waited for; matrix products, arithmetic and copies ran while one was open for 0% of the time, Pallas kernels for 4%

profile of v3, /device:TPU:0, one launch (start us, length us, event | category | flops | bytes accessed | tf_op | source)
XLA Modules:
  0.0 33.8 jit_solution(921505836610708173)
XLA Ops:
  0.0 3.0 %collective-permute-start.1 = (bf16[16,2048]{1,0:T(8,128)(2,1)}, bf16[16,2048]{1,0:T(8,128)(2,1)S(1)}, u32[]{:S(2)}, u32[]{:S(2)}) collective-permute-start(bf16[16,2048]{1,0:T(8,128)(2,1)} %centers_ref.1), channel_id=1, source_target_pairs={{0,8},{4,12},{8,0},{12,4},{16,24},{20,28},{24,16},{28,20},{1,9},{5... | collective-permute-start | bytes 196616 | tf_op jit(solution)/shard_map/ppermute | solution.py:18
  3.0 2.6 %collective-permute-start.3 = (bf16[16,2048]{1,0:T(8,128)(2,1)}, bf16[16,2048]{1,0:T(8,128)(2,1)S(1)}, u32[]{:S(2)}, u32[]{:S(2)}) collective-permute-start(bf16[16,2048]{1,0:T(8,128)(2,1)} %centers_ref.1), channel_id=1, source_target_pairs={{0,16},{4,20},{8,24},{12,28},{16,0},{20,4},{24,8},{28,12},{1,17},{... | collective-permute-start | bytes 196616 | tf_op jit(solution)/shard_map/ppermute | solution.py:18
  5.6 1.7 %collective-permute-start = (bf16[16,2048]{1,0:T(8,128)(2,1)}, bf16[16,2048]{1,0:T(8,128)(2,1)S(1)}, u32[]{:S(2)}, u32[]{:S(2)}) collective-permute-start(bf16[16,2048]{1,0:T(8,128)(2,1)} %centers_ref.1), channel_id=1, source_target_pairs={{0,4},{4,0},{8,12},{12,8},{16,20},{20,16},{24,28},{28,24},{1,5},{5... | collective-permute-start | bytes 196616 | tf_op jit(solution)/shard_map/ppermute | solution.py:18
  7.3 0.3 collective-permute-start.2
  7.6 2.9 %collective-permute-done.3.r_6_ = bf16[16,2048]{1,0:T(8,128)(2,1)S(1)} collective-permute-done((bf16[16,2048]{1,0:T(8,128)(2,1)}, bf16[16,2048]{1,0:T(8,128)(2,1)S(1)}, u32[]{:S(2)}, u32[]{:S(2)}) %collective-permute-start.3) | collective-permute-done | bytes 65568 | tf_op jit(solution)/shard_map/ppermute | solution.py:18
  10.5 1.5 %collective-permute-start.4 = (bf16[16,2048]{1,0:T(8,128)(2,1)S(1)}, bf16[16,2048]{1,0:T(8,128)(2,1)S(1)}, u32[]{:S(2)}, u32[]{:S(2)}) collective-permute-start(bf16[16,2048]{1,0:T(8,128)(2,1)S(1)} %collective-permute-done.3.r_6_), channel_id=1, source_target_pairs={{0,4},{4,0},{8,12},{12,8},{16,20},{20,16},{24,28},{28,24},{1,5},{5... | collective-permute-start | bytes 196616 | tf_op jit(solution)/shard_map/ppermute | solution.py:18
  12.0 1.4 %collective-permute-start.6 = (bf16[16,2048]{1,0:T(8,128)(2,1)S(1)}, bf16[16,2048]{1,0:T(8,128)(2,1)S(1)}, u32[]{:S(2)}, u32[]{:S(2)}) collective-permute-start(bf16[16,2048]{1,0:T(8,128)(2,1)S(1)} %collective-permute-done.5.r_8_), channel_id=1, source_target_pairs={{0,4},{4,0},{8,12},{12,8},{16,20},{20,16},{24,28},{28,24},{1,5},{5... | collective-permute-start | bytes 196616 | tf_op jit(solution)/shard_map/ppermute | solution.py:18
  13.4 1.4 %shard_map.37 = (bf16[128,2048]{1,0:T(8,128)(2,1)S(1)}, bf16[16,2048]{1,0:T(8,128)(2,1)S(1)}, f32[1,128]{1,0:T(1,128)S(1)}) custom-call(bf16[128,2048]{1,0:T(8,128)(2,1)} %points_ref.1, bf16[16,2048]{1,0:T(8,128)(2,1)} %centers_ref.1), custom_call_target="tpu_custom_call" | custom-call | flops 524288 | bytes 524288 | tf_op jit(solution)/shard_map/pallas_call | solution.py:114
  14.8 1.4 %collective-permute-done.6.r_9_ = bf16[16,2048]{1,0:T(8,128)(2,1)S(1)} collective-permute-done((bf16[16,2048]{1,0:T(8,128)(2,1)S(1)}, bf16[16,2048]{1,0:T(8,128)(2,1)S(1)}, u32[]{:S(2)}, u32[]{:S(2)}) %collective-permute-start.6) | collective-permute-done | bytes 65568 | tf_op jit(solution)/shard_map/ppermute | solution.py:18
  16.3 0.3 shard_map.38
  16.7 1.2 %collective-permute-done.7 = f32[128,128]{1,0:T(8,128)S(1)} collective-permute-done((f32[128,128]{1,0:T(8,128)S(1)}, f32[128,128]{1,0:T(8,128)S(1)}, u32[]{:S(2)}, u32[]{:S(2)}) %collective-permute-start.7) | collective-permute-done | bytes 65568 | tf_op jit(solution)/shard_map/ppermute | solution.py:18
  18.0 1.6 %collective-permute-start.8 = (f32[128,128]{1,0:T(8,128)S(1)}, f32[128,128]{1,0:T(8,128)S(1)}, u32[]{:S(2)}, u32[]{:S(2)}) collective-permute-start(f32[128,128]{1,0:T(8,128)S(1)} %add.3.r_0_), channel_id=1, source_target_pairs={{0,2},{1,3},{2,0},{3,1},{4,6},{5,7},{6,4},{7,5},{8,10},{9,11},{10,... | collective-permute-start | bytes 196616 | tf_op jit(solution)/shard_map/ppermute | solution.py:18
  19.6 1.2 %collective-permute-done.9.r_3_ = bf16[16,256]{1,0:T(8,128)(2,1)S(1)} collective-permute-done((bf16[16,256]{1,0:T(8,128)(2,1)S(1)}, bf16[16,256]{1,0:T(8,128)(2,1)S(1)}, u32[]{:S(2)}, u32[]{:S(2)}) %collective-permute-start.9) | collective-permute-done | bytes 8224 | tf_op jit(solution)/shard_map/ppermute | solution.py:18
  20.7 1.6 %collective-permute-done.8.r_1_ = f32[128,128]{1,0:T(8,128)S(1)} collective-permute-done((f32[128,128]{1,0:T(8,128)S(1)}, f32[128,128]{1,0:T(8,128)S(1)}, u32[]{:S(2)}, u32[]{:S(2)}) %collective-permute-start.8) | collective-permute-done | bytes 65568 | tf_op jit(solution)/shard_map/ppermute | solution.py:18
  22.3 1.5 %collective-permute-start.10 = (bf16[192,128]{1,0:T(8,128)(2,1)S(1)}, bf16[192,128]{1,0:T(8,128)(2,1)S(1)}, u32[]{:S(2)}, u32[]{:S(2)}) collective-permute-start(bf16[192,128]{1,0:T(8,128)(2,1)S(1)} %shard_map.39.r_0_), channel_id=1, source_target_pairs={{0,16},{1,25},{2,18},{3,27},{4,20},{5,29},{6,22},{7,31},{8,24},{9,... | collective-permute-start | bytes 147464 | tf_op jit(solution)/shard_map/ppermute | solution.py:98
  23.9 2.3 %collective-permute-start.11 = (bf16[192,128]{1,0:T(8,128)(2,1)S(1)}, bf16[192,128]{1,0:T(8,128)(2,1)S(1)}, u32[]{:S(2)}, u32[]{:S(2)}) collective-permute-start(bf16[192,128]{1,0:T(8,128)(2,1)S(1)} %shard_map.39.r_0_), channel_id=1, source_target_pairs={{0,20},{1,29},{2,22},{3,31},{4,16},{5,25},{6,18},{7,27},{8,28},{9,... | collective-permute-start | bytes 147464 | tf_op jit(solution)/shard_map/ppermute | solution.py:98
  26.2 0.9 %collective-permute-start.12 = (bf16[192,128]{1,0:T(8,128)(2,1)S(1)}, bf16[192,128]{1,0:T(8,128)(2,1)S(1)}, u32[]{:S(2)}, u32[]{:S(2)}) collective-permute-start(bf16[192,128]{1,0:T(8,128)(2,1)S(1)} %shard_map.39.r_0_), channel_id=1, source_target_pairs={{0,12},{1,5},{2,14},{3,7},{4,8},{5,1},{6,10},{7,3},{8,4},{9,13},{1... | collective-permute-start | bytes 147464 | tf_op jit(solution)/shard_map/ppermute | solution.py:98
  27.1 1.1 %collective-permute-start.13 = (bf16[192,128]{1,0:T(8,128)(2,1)S(1)}, bf16[192,128]{1,0:T(8,128)(2,1)S(1)}, u32[]{:S(2)}, u32[]{:S(2)}) collective-permute-start(bf16[192,128]{1,0:T(8,128)(2,1)S(1)} %shard_map.39.r_0_), channel_id=1, source_target_pairs={{0,8},{1,9},{2,10},{3,11},{4,12},{5,13},{6,14},{7,15},{8,0},{9,1},... | collective-permute-start | bytes 147464 | tf_op jit(solution)/shard_map/ppermute | solution.py:98
  28.2 2.1 %collective-permute-done.11.r_2_ = bf16[192,128]{1,0:T(8,128)(2,1)S(1)} collective-permute-done((bf16[192,128]{1,0:T(8,128)(2,1)S(1)}, bf16[192,128]{1,0:T(8,128)(2,1)S(1)}, u32[]{:S(2)}, u32[]{:S(2)}) %collective-permute-start.11) | collective-permute-done | bytes 49184 | tf_op jit(solution)/shard_map/ppermute | solution.py:98
  30.4 0.9 %collective-permute-done.12.r_3_ = bf16[192,128]{1,0:T(8,128)(2,1)S(1)} collective-permute-done((bf16[192,128]{1,0:T(8,128)(2,1)S(1)}, bf16[192,128]{1,0:T(8,128)(2,1)S(1)}, u32[]{:S(2)}, u32[]{:S(2)}) %collective-permute-start.12) | collective-permute-done | bytes 49184 | tf_op jit(solution)/shard_map/ppermute | solution.py:98
  31.3 0.3 collective-permute-done.15.r_6_
  31.6 0.9 %collective-permute-done.16.r_7_ = bf16[192,128]{1,0:T(8,128)(2,1)S(1)} collective-permute-done((bf16[192,128]{1,0:T(8,128)(2,1)S(1)}, bf16[192,128]{1,0:T(8,128)(2,1)S(1)}, u32[]{:S(2)}, u32[]{:S(2)}) %collective-permute-start.16) | collective-permute-done | bytes 49184 | tf_op jit(solution)/shard_map/ppermute | solution.py:18
  32.6 0.6 %shard_map.40 = f32[16,256]{1,0:T(8,128)S(1)} custom-call(bf16[192,128]{1,0:T(8,128)(2,1)S(1)} %shard_map.39.r_0_, bf16[192,128]{1,0:T(8,128)(2,1)S(1)} %collective-permute-done.10.r_1_, bf16[192,128]{1,0:T(8,128)(2,1)S(1)} %collective-permute-done.11.r_2_, bf16[192,128]{1,0:T(8,128)(2,1)S(1)} %collective-permute-done.12.r_3_, ...), custom_call_target="tpu_custom_call" | custom-call | tf_op jit(solution)/shard_map/pallas_call | solution.py:26
  33.1 0.7 %copy.4 = f32[16,256]{1,0:T(8,128)} copy(f32[16,256]{1,0:T(8,128)S(1)} %shard_map.40) | data formatting | bytes 32768
  (18 shorter events, 0.1 us)
Async XLA Ops:
  0.0 7.3 %collective-permute-start.1 = (bf16[16,2048]{1,0:T(8,128)(2,1)}, bf16[16,2048]{1,0:T(8,128)(2,1)S(1)}, u32[]{:S(2)}, u32[]{:S(2)}) collective-permute-start(bf16[16,2048]{1,0:T(8,128)(2,1)} %centers_ref.1), channel_id=1, source_target_pairs={{0,8},{4,12},{8,0},{12,4},{16,24},{20,28},{24,16},{28,20},{1,9},{5... | collective-permute-start | bytes 196616 | tf_op jit(solution)/shard_map/ppermute | solution.py:18
  3.0 7.5 %collective-permute-start.3 = (bf16[16,2048]{1,0:T(8,128)(2,1)}, bf16[16,2048]{1,0:T(8,128)(2,1)S(1)}, u32[]{:S(2)}, u32[]{:S(2)}) collective-permute-start(bf16[16,2048]{1,0:T(8,128)(2,1)} %centers_ref.1), channel_id=1, source_target_pairs={{0,16},{4,20},{8,24},{12,28},{16,0},{20,4},{24,8},{28,12},{1,17},{... | collective-permute-start | bytes 196616 | tf_op jit(solution)/shard_map/ppermute | solution.py:18
  5.6 6.4 %collective-permute-start.5 = (bf16[16,2048]{1,0:T(8,128)(2,1)}, bf16[16,2048]{1,0:T(8,128)(2,1)S(1)}, u32[]{:S(2)}, u32[]{:S(2)}) collective-permute-start(bf16[16,2048]{1,0:T(8,128)(2,1)} %centers_ref.1), channel_id=1, source_target_pairs={{0,24},{4,28},{8,16},{12,20},{16,8},{20,12},{24,0},{28,4},{1,25},{... | collective-permute-start | bytes 196616 | tf_op jit(solution)/shard_map/ppermute | solution.py:18
  5.6 9.2 %collective-permute-start = (bf16[16,2048]{1,0:T(8,128)(2,1)}, bf16[16,2048]{1,0:T(8,128)(2,1)S(1)}, u32[]{:S(2)}, u32[]{:S(2)}) collective-permute-start(bf16[16,2048]{1,0:T(8,128)(2,1)} %centers_ref.1), channel_id=1, source_target_pairs={{0,4},{4,0},{8,12},{12,8},{16,20},{20,16},{24,28},{28,24},{1,5},{5... | collective-permute-start | bytes 196616 | tf_op jit(solution)/shard_map/ppermute | solution.py:18
  7.3 7.5 %collective-permute-start.2 = (bf16[16,2048]{1,0:T(8,128)(2,1)S(1)}, bf16[16,2048]{1,0:T(8,128)(2,1)S(1)}, u32[]{:S(2)}, u32[]{:S(2)}) collective-permute-start(bf16[16,2048]{1,0:T(8,128)(2,1)S(1)} %collective-permute-done.1.r_4_), channel_id=1, source_target_pairs={{0,4},{4,0},{8,12},{12,8},{16,20},{20,16},{24,28},{28,24},{1,5},{5... | collective-permute-start | bytes 196616 | tf_op jit(solution)/shard_map/ppermute | solution.py:18
  10.5 4.3 %collective-permute-start.4 = (bf16[16,2048]{1,0:T(8,128)(2,1)S(1)}, bf16[16,2048]{1,0:T(8,128)(2,1)S(1)}, u32[]{:S(2)}, u32[]{:S(2)}) collective-permute-start(bf16[16,2048]{1,0:T(8,128)(2,1)S(1)} %collective-permute-done.3.r_6_), channel_id=1, source_target_pairs={{0,4},{4,0},{8,12},{12,8},{16,20},{20,16},{24,28},{28,24},{1,5},{5... | collective-permute-start | bytes 196616 | tf_op jit(solution)/shard_map/ppermute | solution.py:18
  12.0 4.3 %collective-permute-start.6 = (bf16[16,2048]{1,0:T(8,128)(2,1)S(1)}, bf16[16,2048]{1,0:T(8,128)(2,1)S(1)}, u32[]{:S(2)}, u32[]{:S(2)}) collective-permute-start(bf16[16,2048]{1,0:T(8,128)(2,1)S(1)} %collective-permute-done.5.r_8_), channel_id=1, source_target_pairs={{0,4},{4,0},{8,12},{12,8},{16,20},{20,16},{24,28},{28,24},{1,5},{5... | collective-permute-start | bytes 196616 | tf_op jit(solution)/shard_map/ppermute | solution.py:18
  16.6 3.0 %copy-start = (bf16[16,256]{1,0:T(8,128)(2,1)S(1)}, bf16[16,256]{1,0:T(8,128)(2,1)}, u32[]{:S(2)}) copy-start(bf16[16,256]{1,0:T(8,128)(2,1)} %r_2_.1) | copy-start | bytes 24580
  16.6 1.3 %collective-permute-start.7 = (f32[128,128]{1,0:T(8,128)S(1)}, f32[128,128]{1,0:T(8,128)S(1)}, u32[]{:S(2)}, u32[]{:S(2)}) collective-permute-start(f32[128,128]{1,0:T(8,128)S(1)} %shard_map.38), channel_id=1, source_target_pairs={{0,1},{1,0},{2,3},{3,2},{4,5},{5,4},{6,7},{7,6},{8,9},{9,8},{10,11... | collective-permute-start | bytes 196616 | tf_op jit(solution)/shard_map/ppermute | solution.py:18
  18.0 4.3 %collective-permute-start.8 = (f32[128,128]{1,0:T(8,128)S(1)}, f32[128,128]{1,0:T(8,128)S(1)}, u32[]{:S(2)}, u32[]{:S(2)}) collective-permute-start(f32[128,128]{1,0:T(8,128)S(1)} %add.3.r_0_), channel_id=1, source_target_pairs={{0,2},{1,3},{2,0},{3,1},{4,6},{5,7},{6,4},{7,5},{8,10},{9,11},{10,... | collective-permute-start | bytes 196616 | tf_op jit(solution)/shard_map/ppermute | solution.py:18
  19.6 1.2 %collective-permute-start.9 = (bf16[16,256]{1,0:T(8,128)(2,1)S(1)}, bf16[16,256]{1,0:T(8,128)(2,1)S(1)}, u32[]{:S(2)}, u32[]{:S(2)}) collective-permute-start(bf16[16,256]{1,0:T(8,128)(2,1)S(1)} %copy-done), channel_id=1, source_target_pairs={{0,1},{1,0},{2,3},{3,2},{4,5},{5,4},{6,7},{7,6},{8,9},{9,8},{10,11... | collective-permute-start | bytes 24584 | tf_op jit(solution)/shard_map/ppermute | solution.py:18
  22.3 5.9 %collective-permute-start.10 = (bf16[192,128]{1,0:T(8,128)(2,1)S(1)}, bf16[192,128]{1,0:T(8,128)(2,1)S(1)}, u32[]{:S(2)}, u32[]{:S(2)}) collective-permute-start(bf16[192,128]{1,0:T(8,128)(2,1)S(1)} %shard_map.39.r_0_), channel_id=1, source_target_pairs={{0,16},{1,25},{2,18},{3,27},{4,20},{5,29},{6,22},{7,31},{8,24},{9,... | collective-permute-start | bytes 147464 | tf_op jit(solution)/shard_map/ppermute | solution.py:98
  23.9 6.5 %collective-permute-start.11 = (bf16[192,128]{1,0:T(8,128)(2,1)S(1)}, bf16[192,128]{1,0:T(8,128)(2,1)S(1)}, u32[]{:S(2)}, u32[]{:S(2)}) collective-permute-start(bf16[192,128]{1,0:T(8,128)(2,1)S(1)} %shard_map.39.r_0_), channel_id=1, source_target_pairs={{0,20},{1,29},{2,22},{3,31},{4,16},{5,25},{6,18},{7,27},{8,28},{9,... | collective-permute-start | bytes 147464 | tf_op jit(solution)/shard_map/ppermute | solution.py:98
  26.2 5.2 %collective-permute-start.12 = (bf16[192,128]{1,0:T(8,128)(2,1)S(1)}, bf16[192,128]{1,0:T(8,128)(2,1)S(1)}, u32[]{:S(2)}, u32[]{:S(2)}) collective-permute-start(bf16[192,128]{1,0:T(8,128)(2,1)S(1)} %shard_map.39.r_0_), channel_id=1, source_target_pairs={{0,12},{1,5},{2,14},{3,7},{4,8},{5,1},{6,10},{7,3},{8,4},{9,13},{1... | collective-permute-start | bytes 147464 | tf_op jit(solution)/shard_map/ppermute | solution.py:98
  27.1 4.2 %collective-permute-start.13 = (bf16[192,128]{1,0:T(8,128)(2,1)S(1)}, bf16[192,128]{1,0:T(8,128)(2,1)S(1)}, u32[]{:S(2)}, u32[]{:S(2)}) collective-permute-start(bf16[192,128]{1,0:T(8,128)(2,1)S(1)} %shard_map.39.r_0_), channel_id=1, source_target_pairs={{0,8},{1,9},{2,10},{3,11},{4,12},{5,13},{6,14},{7,15},{8,0},{9,1},... | collective-permute-start | bytes 147464 | tf_op jit(solution)/shard_map/ppermute | solution.py:98
  28.2 3.1 %collective-permute-start.14 = (bf16[192,128]{1,0:T(8,128)(2,1)S(1)}, bf16[192,128]{1,0:T(8,128)(2,1)S(1)}, u32[]{:S(2)}, u32[]{:S(2)}) collective-permute-start(bf16[192,128]{1,0:T(8,128)(2,1)S(1)} %collective-permute-done.10.r_1_), channel_id=1, source_target_pairs={{0,1},{1,0},{2,3},{3,2},{4,5},{5,4},{6,7},{7,6},{8,9},{9,8},{10,11... | collective-permute-start | bytes 147464 | tf_op jit(solution)/shard_map/ppermute | solution.py:18
  30.4 1.2 %collective-permute-start.15 = (bf16[192,128]{1,0:T(8,128)(2,1)S(1)}, bf16[192,128]{1,0:T(8,128)(2,1)S(1)}, u32[]{:S(2)}, u32[]{:S(2)}) collective-permute-start(bf16[192,128]{1,0:T(8,128)(2,1)S(1)} %collective-permute-done.11.r_2_), channel_id=1, source_target_pairs={{0,1},{1,0},{2,3},{3,2},{4,5},{5,4},{6,7},{7,6},{8,9},{9,8},{10,11... | collective-permute-start | bytes 147464 | tf_op jit(solution)/shard_map/ppermute | solution.py:18
  31.3 1.2 %collective-permute-start.16 = (bf16[192,128]{1,0:T(8,128)(2,1)S(1)}, bf16[192,128]{1,0:T(8,128)(2,1)S(1)}, u32[]{:S(2)}, u32[]{:S(2)}) collective-permute-start(bf16[192,128]{1,0:T(8,128)(2,1)S(1)} %collective-permute-done.12.r_3_), channel_id=1, source_target_pairs={{0,1},{1,0},{2,3},{3,2},{4,5},{5,4},{6,7},{7,6},{8,9},{9,8},{10,11... | collective-permute-start | bytes 147464 | tf_op jit(solution)/shard_map/ppermute | solution.py:18

commit v4 on v3

--- a/solution.py
+++ b/solution.py
@@ -9,6 +9,8 @@
 
 BF16 = jnp.bfloat16
 F32 = jnp.float32
+GATHER = ((0, 1), (0, 4), (1, 4), (0, 2), (1, 2), (0, 6), (6, 1))
+SPREAD = ((0, 6, 7), (0, 4, 5), (0, 2, 3), (0, 1, 1))
 LANES = 128
 VMEM = pl.BlockSpec(memory_space=pltpu.VMEM)
 
@@ -65,17 +67,15 @@
             out_ref[pl.ds(at, rows), :] = ref[:, i * LANES : (i + 1) * LANES]
 
 
-def product_kernel(mine_order, other_order, rows, scale, *refs):
-    n, m = len(mine_order[0]), len(other_order[0])
-    tiles, (out_ref, kernel, coefs) = refs[: n + m], refs[n + m :]
+def product_kernel(sources, rows, scale, *refs):
+    tiles, (out_ref, kernel, coefs) = refs[: len(sources)], refs[len(sources) :]
     all_rows = kernel.shape[0]
     blk = lax.axis_index("blk")
     core = lax.axis_index("feat") % 2
     pieces = coefs.shape[1] // LANES
-    for i, tile in enumerate(tiles):
-        a, b = (mine_order[0][i], mine_order[1][i]) if i < n else (other_order[0][i - n], other_order[1][i - n])
+    for i, (tile, (even, odd)) in enumerate(zip(tiles, sources)):
         kernel[:, i * LANES : (i + 1) * LANES] = tile[:all_rows, :]
-        at = pl.multiple_of((blk ^ jnp.where(core == 0, a, b)) * rows, rows)
+        at = pl.multiple_of((blk ^ jnp.where(core == 0, even, odd)) * rows, rows)
         for j in range(pieces):
             top = pl.multiple_of(all_rows + (core * pieces + j) * rows, rows)
             coefs[pl.ds(at, rows), j * LANES : (j + 1) * LANES] = tile[pl.ds(top, rows), :]
@@ -103,14 +103,9 @@
     rows, local_points = centers.shape[0], points.shape[0]
     features = points.shape[1] * lax.axis_size("feat")
     all_rows = rows * blks
-    line = [k for k in (4, 6, 2) if k < blks]
-
-    tiles = {}
-    for k in line:
-        tiles[k] = swap(centers, "blk", k)
-    tiles[1] = swap(centers, "blk", 1)
-    for k in line:
-        tiles[k ^ 1] = swap(tiles[k], "blk", 1)
+    tiles = {0: centers}
+    for held, bits in GATHER:
+        tiles[held ^ bits] = swap(tiles[held], "blk", bits)
     points, tiles[0], square = pl.pallas_call(
         prepare_kernel,
         out_shape=[pltpu.VMEM(points.shape, BF16), pltpu.VMEM(centers.shape, BF16), pltpu.VMEM((1, local_points), F32)],
@@ -139,16 +134,18 @@
         coefs,
         others,
     )
-    mine_order = ([0, 4, 5, 3, 2], [0, 6, 7, 1, 2])
-    mine = [tile] + [swap_by_core(tile, a, b) for a, b in list(zip(*mine_order))[1:]]
-    other_order = (mine_order[1][1:-1], mine_order[0][1:-1])
-    other = [swap(x, "feat", 1) for x in mine[1:-1]]
+    held, sources = [tile], [(0, 0)]
+    for at, even, odd in SPREAD:
+        held.append(swap_by_core(held[at], even, odd))
+        sources.append((sources[at][0] ^ even, sources[at][1] ^ odd))
+    passed = [i for i, (even, odd) in enumerate(sources) if even != odd]
+    held += [swap(held[i], "feat", 1) for i in passed]
+    sources += [sources[i][::-1] for i in passed]
     scale = 1.0 / math.sqrt(local_points * blks)
     (out,) = call(
-        lambda *r: product_kernel(mine_order, other_order, rows, scale, *r),
+        lambda *r: product_kernel(sources, rows, scale, *r),
         [jax.ShapeDtypeStruct((rows, coefs.shape[1]), F32)],
-        *mine,
-        *other,
+        *held,
         scratch=[pltpu.VMEM((all_rows, local_points * blks), BF16), pltpu.VMEM((all_rows, coefs.shape[1]), BF16)],
     )
     return out

time: 34 us -> 32.1 us (0.944)
  waiting for transfers between devices: 12.6 us -> 9.65 us
  starting transfers between devices: 18.1 us -> 19.2 us
    ppermute x13, waiting for transfers between devices: 9.49 us -> 6.6 us  [swap(): return lax.ppermute(x, axis, [(i, i ^ bits) for i in range(n)])]
    ppermute x13, starting transfers between devices: 12.2 us -> 14.2 us  [swap(): return lax.ppermute(x, axis, [(i, i ^ bits) for i in range(n)])]
    ppermute x4, starting transfers between devices: 5.91 us -> 4.98 us  [swap_by_core(): return lax.ppermute(x, ('blk', 'feat'), pairs)]
  transfers between devices with their start and end apart: 17 -> 17, of which waited for: 9 -> 11; matrix products, arithmetic and copies ran while one was open for 0% -> 0% of each run, Pallas kernels for 4% -> 4%
where the time goes in v4:
time: 32.1 us; the launch traced here: 31.9 us
  starting transfers between devices  19.2 us (60%)
  waiting for transfers between devices  9.65 us (30%)
  Pallas kernels  2.35 us (7%)
  local copies, waits for them, and re-layouts  0.68 us (2%)
    ppermute x13, starting transfers between devices, swap(): return lax.ppermute(x, axis, [(i, i ^ bits) for i in range(n)])  14.2 us
    ppermute x13, waiting for transfers between devices, swap(): return lax.ppermute(x, axis, [(i, i ^ bits) for i in range(n)])  6.6 us
    ppermute x4, starting transfers between devices, swap_by_core(): return lax.ppermute(x, ('blk', 'feat'), pairs)  4.98 us
    ppermute x4, waiting for transfers between devices, swap_by_core(): return lax.ppermute(x, ('blk', 'feat'), pairs)  3.04 us
    pallas_call x1, Pallas kernels, on_device(): pl.pallas_call(prepare_kernel, out_shape=[pltpu.VMEM(points.shape, BF16),...  1.41 us
    pallas_call x3, Pallas kernels, call(): pl.pallas_call(kernel, out_shape=[pltpu.VMEM(o.shape, o.dtype) for o in o...  0.95 us
    unnamed x3, local copies, waits for them, and re-layouts  0.68 us
  transfers between devices with their start and end apart: 17, of which 11 were waited for; matrix products, arithmetic and copies ran while one was open for 0% of the time, Pallas kernels for 4%

profile of v4, /device:TPU:0, one launch (start us, length us, event | category | flops | bytes accessed | tf_op | source)
XLA Modules:
  0.0 31.9 jit_solution(4524119188610420330)
XLA Ops:
  0.0 2.9 %collective-permute-start = (bf16[16,2048]{1,0:T(8,128)(2,1)}, bf16[16,2048]{1,0:T(8,128)(2,1)S(1)}, u32[]{:S(2)}, u32[]{:S(2)}) collective-permute-start(bf16[16,2048]{1,0:T(8,128)(2,1)} %centers_ref.1), channel_id=1, source_target_pairs={{0,4},{4,0},{8,12},{12,8},{16,20},{20,16},{24,28},{28,24},{1,5},{5... | collective-permute-start | bytes 196616 | tf_op jit(solution)/shard_map/ppermute | solution.py:20
  2.9 3.6 %collective-permute-start.5 = (bf16[16,2048]{1,0:T(8,128)(2,1)}, bf16[16,2048]{1,0:T(8,128)(2,1)S(1)}, u32[]{:S(2)}, u32[]{:S(2)}) collective-permute-start(bf16[16,2048]{1,0:T(8,128)(2,1)} %centers_ref.1), channel_id=1, source_target_pairs={{0,24},{4,28},{8,16},{12,20},{16,8},{20,12},{24,0},{28,4},{1,25},{... | collective-permute-start | bytes 196616 | tf_op jit(solution)/shard_map/ppermute | solution.py:20
  6.5 0.8 %collective-permute-start.3 = (bf16[16,2048]{1,0:T(8,128)(2,1)}, bf16[16,2048]{1,0:T(8,128)(2,1)S(1)}, u32[]{:S(2)}, u32[]{:S(2)}) collective-permute-start(bf16[16,2048]{1,0:T(8,128)(2,1)} %centers_ref.1), channel_id=1, source_target_pairs={{0,16},{4,20},{8,24},{12,28},{16,0},{20,4},{24,8},{28,12},{1,17},{... | collective-permute-start | bytes 196616 | tf_op jit(solution)/shard_map/ppermute | solution.py:20
  7.3 1.2 %collective-permute-start.2 = (bf16[16,2048]{1,0:T(8,128)(2,1)S(1)}, bf16[16,2048]{1,0:T(8,128)(2,1)S(1)}, u32[]{:S(2)}, u32[]{:S(2)}) collective-permute-start(bf16[16,2048]{1,0:T(8,128)(2,1)S(1)} %collective-permute-done.r_3_), channel_id=1, source_target_pairs={{0,8},{4,12},{8,0},{12,4},{16,24},{20,28},{24,16},{28,20},{1,9},{5... | collective-permute-start | bytes 196616 | tf_op jit(solution)/shard_map/ppermute | solution.py:20
  8.6 2.9 %collective-permute-start.4 = (bf16[16,2048]{1,0:T(8,128)(2,1)S(1)}, bf16[16,2048]{1,0:T(8,128)(2,1)S(1)}, u32[]{:S(2)}, u32[]{:S(2)}) collective-permute-start(bf16[16,2048]{1,0:T(8,128)(2,1)S(1)} %collective-permute-done.r_3_), channel_id=1, source_target_pairs={{0,16},{4,20},{8,24},{12,28},{16,0},{20,4},{24,8},{28,12},{1,17},{... | collective-permute-start | bytes 196616 | tf_op jit(solution)/shard_map/ppermute | solution.py:20
  11.5 0.5 %collective-permute-start.6 = (bf16[16,2048]{1,0:T(8,128)(2,1)S(1)}, bf16[16,2048]{1,0:T(8,128)(2,1)S(1)}, u32[]{:S(2)}, u32[]{:S(2)}) collective-permute-start(bf16[16,2048]{1,0:T(8,128)(2,1)S(1)} %collective-permute-done.5.r_8_), channel_id=1, source_target_pairs={{0,4},{4,0},{8,12},{12,8},{16,20},{20,16},{24,28},{28,24},{1,5},{5... | collective-permute-start | bytes 196616 | tf_op jit(solution)/shard_map/ppermute | solution.py:20
  12.0 1.4 %shard_map.37 = (bf16[128,2048]{1,0:T(8,128)(2,1)S(1)}, bf16[16,2048]{1,0:T(8,128)(2,1)S(1)}, f32[1,128]{1,0:T(1,128)S(1)}) custom-call(bf16[128,2048]{1,0:T(8,128)(2,1)} %points_ref.1, bf16[16,2048]{1,0:T(8,128)(2,1)} %centers_ref.1), custom_call_target="tpu_custom_call" | custom-call | flops 524288 | bytes 524288 | tf_op jit(solution)/shard_map/pallas_call | solution.py:109
  13.5 0.8 %collective-permute-done.3.r_6_ = bf16[16,2048]{1,0:T(8,128)(2,1)S(1)} collective-permute-done((bf16[16,2048]{1,0:T(8,128)(2,1)}, bf16[16,2048]{1,0:T(8,128)(2,1)S(1)}, u32[]{:S(2)}, u32[]{:S(2)}) %collective-permute-start.3) | collective-permute-done | bytes 65568 | tf_op jit(solution)/shard_map/ppermute | solution.py:20
  14.2 1.4 %collective-permute-done.4.r_7_ = bf16[16,2048]{1,0:T(8,128)(2,1)S(1)} collective-permute-done((bf16[16,2048]{1,0:T(8,128)(2,1)S(1)}, bf16[16,2048]{1,0:T(8,128)(2,1)S(1)}, u32[]{:S(2)}, u32[]{:S(2)}) %collective-permute-start.4) | collective-permute-done | bytes 65568 | tf_op jit(solution)/shard_map/ppermute | solution.py:20
  15.8 0.4 %shard_map.38 = f32[128,128]{1,0:T(8,128)S(1)} custom-call(bf16[128,2048]{1,0:T(8,128)(2,1)S(1)} %get-tuple-element.8.r_0_, f32[1,128]{1,0:T(1,128)S(1)} %get-tuple-element.9.r_1_, bf16[16,2048]{1,0:T(8,128)(2,1)S(1)} %get-tuple-element.10.r_2_, bf16[16,2048]{1,0:T(8,128)(2,1)S(1)} %collective-permute-done.r_3_, ...), custom_call_target="tpu_custom_call" | custom-call | tf_op jit(solution)/shard_map/pallas_call | solution.py:28
  16.2 1.2 %collective-permute-done.7 = f32[128,128]{1,0:T(8,128)S(1)} collective-permute-done((f32[128,128]{1,0:T(8,128)S(1)}, f32[128,128]{1,0:T(8,128)S(1)}, u32[]{:S(2)}, u32[]{:S(2)}) %collective-permute-start.7) | collective-permute-done | bytes 65568 | tf_op jit(solution)/shard_map/ppermute | solution.py:20
  17.5 1.6 %collective-permute-start.8 = (f32[128,128]{1,0:T(8,128)S(1)}, f32[128,128]{1,0:T(8,128)S(1)}, u32[]{:S(2)}, u32[]{:S(2)}) collective-permute-start(f32[128,128]{1,0:T(8,128)S(1)} %add.3.r_0_), channel_id=1, source_target_pairs={{0,2},{1,3},{2,0},{3,1},{4,6},{5,7},{6,4},{7,5},{8,10},{9,11},{10,... | collective-permute-start | bytes 196616 | tf_op jit(solution)/shard_map/ppermute | solution.py:20
  19.1 1.2 %collective-permute-done.9.r_3_ = bf16[16,256]{1,0:T(8,128)(2,1)S(1)} collective-permute-done((bf16[16,256]{1,0:T(8,128)(2,1)S(1)}, bf16[16,256]{1,0:T(8,128)(2,1)S(1)}, u32[]{:S(2)}, u32[]{:S(2)}) %collective-permute-start.9) | collective-permute-done | bytes 8224 | tf_op jit(solution)/shard_map/ppermute | solution.py:20
  20.2 1.6 %collective-permute-done.8.r_1_ = f32[128,128]{1,0:T(8,128)S(1)} collective-permute-done((f32[128,128]{1,0:T(8,128)S(1)}, f32[128,128]{1,0:T(8,128)S(1)}, u32[]{:S(2)}, u32[]{:S(2)}) %collective-permute-start.8) | collective-permute-done | bytes 65568 | tf_op jit(solution)/shard_map/ppermute | solution.py:20
  21.8 2.2 %collective-permute-start.10 = (bf16[192,128]{1,0:T(8,128)(2,1)S(1)}, bf16[192,128]{1,0:T(8,128)(2,1)S(1)}, u32[]{:S(2)}, u32[]{:S(2)}) collective-permute-start(bf16[192,128]{1,0:T(8,128)(2,1)S(1)} %shard_map.39.r_0_), channel_id=1, source_target_pairs={{0,24},{1,29},{2,26},{3,31},{4,28},{5,25},{6,30},{7,27},{8,16},{9,... | collective-permute-start | bytes 147464 | tf_op jit(solution)/shard_map/ppermute | solution.py:98
  24.1 2.2 %collective-permute-start.12 = (bf16[192,128]{1,0:T(8,128)(2,1)S(1)}, bf16[192,128]{1,0:T(8,128)(2,1)S(1)}, u32[]{:S(2)}, u32[]{:S(2)}) collective-permute-start(bf16[192,128]{1,0:T(8,128)(2,1)S(1)} %shard_map.39.r_0_), channel_id=1, source_target_pairs={{0,8},{1,13},{2,10},{3,15},{4,12},{5,9},{6,14},{7,11},{8,0},{9,5},... | collective-permute-start | bytes 147464 | tf_op jit(solution)/shard_map/ppermute | solution.py:98
  26.3 0.5 %collective-permute-start.13 = (bf16[192,128]{1,0:T(8,128)(2,1)S(1)}, bf16[192,128]{1,0:T(8,128)(2,1)S(1)}, u32[]{:S(2)}, u32[]{:S(2)}) collective-permute-start(bf16[192,128]{1,0:T(8,128)(2,1)S(1)} %shard_map.39.r_0_), channel_id=1, source_target_pairs={{0,4},{1,5},{2,6},{3,7},{4,0},{5,1},{6,2},{7,3},{8,12},{9,13},{10,... | collective-permute-start | bytes 147464 | tf_op jit(solution)/shard_map/ppermute | solution.py:98
  26.8 1.1 %collective-permute-done.10.r_1_ = bf16[192,128]{1,0:T(8,128)(2,1)S(1)} collective-permute-done((bf16[192,128]{1,0:T(8,128)(2,1)S(1)}, bf16[192,128]{1,0:T(8,128)(2,1)S(1)}, u32[]{:S(2)}, u32[]{:S(2)}) %collective-permute-start.10) | collective-permute-done | bytes 49184 | tf_op jit(solution)/shard_map/ppermute | solution.py:98
  27.9 1.4 %collective-permute-done.11.r_2_ = bf16[192,128]{1,0:T(8,128)(2,1)S(1)} collective-permute-done((bf16[192,128]{1,0:T(8,128)(2,1)S(1)}, bf16[192,128]{1,0:T(8,128)(2,1)S(1)}, u32[]{:S(2)}, u32[]{:S(2)}) %collective-permute-start.11) | collective-permute-done | bytes 49184 | tf_op jit(solution)/shard_map/ppermute | solution.py:98
  29.3 0.5 %collective-permute-start.16 = (bf16[192,128]{1,0:T(8,128)(2,1)S(1)}, bf16[192,128]{1,0:T(8,128)(2,1)S(1)}, u32[]{:S(2)}, u32[]{:S(2)}) collective-permute-start(bf16[192,128]{1,0:T(8,128)(2,1)S(1)} %collective-permute-done.12.r_3_), channel_id=1, source_target_pairs={{0,1},{1,0},{2,3},{3,2},{4,5},{5,4},{6,7},{7,6},{8,9},{9,8},{10,11... | collective-permute-start | bytes 147464 | tf_op jit(solution)/shard_map/ppermute | solution.py:20
  29.8 0.6 %collective-permute-done.13.r_4_ = bf16[192,128]{1,0:T(8,128)(2,1)S(1)} collective-permute-done((bf16[192,128]{1,0:T(8,128)(2,1)S(1)}, bf16[192,128]{1,0:T(8,128)(2,1)S(1)}, u32[]{:S(2)}, u32[]{:S(2)}) %collective-permute-start.13) | collective-permute-done | bytes 49184 | tf_op jit(solution)/shard_map/ppermute | solution.py:98
  30.5 0.2 collective-permute-done.16.r_7_
  30.7 0.6 %shard_map.40 = f32[16,256]{1,0:T(8,128)S(1)} custom-call(bf16[192,128]{1,0:T(8,128)(2,1)S(1)} %shard_map.39.r_0_, bf16[192,128]{1,0:T(8,128)(2,1)S(1)} %collective-permute-done.10.r_1_, bf16[192,128]{1,0:T(8,128)(2,1)S(1)} %collective-permute-done.11.r_2_, bf16[192,128]{1,0:T(8,128)(2,1)S(1)} %collective-permute-done.12.r_3_, ...), custom_call_target="tpu_custom_call" | custom-call | tf_op jit(solution)/shard_map/pallas_call | solution.py:28
  31.2 0.7 %copy.4 = f32[16,256]{1,0:T(8,128)} copy(f32[16,256]{1,0:T(8,128)S(1)} %shard_map.40) | data formatting | bytes 32768
  (18 shorter events, 0.4 us)
Async XLA Ops:
  0.0 7.3 %collective-permute-start = (bf16[16,2048]{1,0:T(8,128)(2,1)}, bf16[16,2048]{1,0:T(8,128)(2,1)S(1)}, u32[]{:S(2)}, u32[]{:S(2)}) collective-permute-start(bf16[16,2048]{1,0:T(8,128)(2,1)} %centers_ref.1), channel_id=1, source_target_pairs={{0,4},{4,0},{8,12},{12,8},{16,20},{20,16},{24,28},{28,24},{1,5},{5... | collective-permute-start | bytes 196616 | tf_op jit(solution)/shard_map/ppermute | solution.py:20
  2.9 8.6 %collective-permute-start.5 = (bf16[16,2048]{1,0:T(8,128)(2,1)}, bf16[16,2048]{1,0:T(8,128)(2,1)S(1)}, u32[]{:S(2)}, u32[]{:S(2)}) collective-permute-start(bf16[16,2048]{1,0:T(8,128)(2,1)} %centers_ref.1), channel_id=1, source_target_pairs={{0,24},{4,28},{8,16},{12,20},{16,8},{20,12},{24,0},{28,4},{1,25},{... | collective-permute-start | bytes 196616 | tf_op jit(solution)/shard_map/ppermute | solution.py:20
  6.5 6.9 %collective-permute-start.1 = (bf16[16,2048]{1,0:T(8,128)(2,1)}, bf16[16,2048]{1,0:T(8,128)(2,1)S(1)}, u32[]{:S(2)}, u32[]{:S(2)}) collective-permute-start(bf16[16,2048]{1,0:T(8,128)(2,1)} %centers_ref.1), channel_id=1, source_target_pairs={{0,8},{4,12},{8,0},{12,4},{16,24},{20,28},{24,16},{28,20},{1,9},{5... | collective-permute-start | bytes 196616 | tf_op jit(solution)/shard_map/ppermute | solution.py:20
  6.5 7.7 %collective-permute-start.3 = (bf16[16,2048]{1,0:T(8,128)(2,1)}, bf16[16,2048]{1,0:T(8,128)(2,1)S(1)}, u32[]{:S(2)}, u32[]{:S(2)}) collective-permute-start(bf16[16,2048]{1,0:T(8,128)(2,1)} %centers_ref.1), channel_id=1, source_target_pairs={{0,16},{4,20},{8,24},{12,28},{16,0},{20,4},{24,8},{28,12},{1,17},{... | collective-permute-start | bytes 196616 | tf_op jit(solution)/shard_map/ppermute | solution.py:20
  7.3 6.9 %collective-permute-start.2 = (bf16[16,2048]{1,0:T(8,128)(2,1)S(1)}, bf16[16,2048]{1,0:T(8,128)(2,1)S(1)}, u32[]{:S(2)}, u32[]{:S(2)}) collective-permute-start(bf16[16,2048]{1,0:T(8,128)(2,1)S(1)} %collective-permute-done.r_3_), channel_id=1, source_target_pairs={{0,8},{4,12},{8,0},{12,4},{16,24},{20,28},{24,16},{28,20},{1,9},{5... | collective-permute-start | bytes 196616 | tf_op jit(solution)/shard_map/ppermute | solution.py:20
  8.6 7.0 %collective-permute-start.4 = (bf16[16,2048]{1,0:T(8,128)(2,1)S(1)}, bf16[16,2048]{1,0:T(8,128)(2,1)S(1)}, u32[]{:S(2)}, u32[]{:S(2)}) collective-permute-start(bf16[16,2048]{1,0:T(8,128)(2,1)S(1)} %collective-permute-done.r_3_), channel_id=1, source_target_pairs={{0,16},{4,20},{8,24},{12,28},{16,0},{20,4},{24,8},{28,12},{1,17},{... | collective-permute-start | bytes 196616 | tf_op jit(solution)/shard_map/ppermute | solution.py:20
  11.5 4.3 %collective-permute-start.6 = (bf16[16,2048]{1,0:T(8,128)(2,1)S(1)}, bf16[16,2048]{1,0:T(8,128)(2,1)S(1)}, u32[]{:S(2)}, u32[]{:S(2)}) collective-permute-start(bf16[16,2048]{1,0:T(8,128)(2,1)S(1)} %collective-permute-done.5.r_8_), channel_id=1, source_target_pairs={{0,4},{4,0},{8,12},{12,8},{16,20},{20,16},{24,28},{28,24},{1,5},{5... | collective-permute-start | bytes 196616 | tf_op jit(solution)/shard_map/ppermute | solution.py:20
  16.1 2.9 %copy-start = (bf16[16,256]{1,0:T(8,128)(2,1)S(1)}, bf16[16,256]{1,0:T(8,128)(2,1)}, u32[]{:S(2)}) copy-start(bf16[16,256]{1,0:T(8,128)(2,1)} %r_2_.1) | copy-start | bytes 24580
  16.1 1.3 %collective-permute-start.7 = (f32[128,128]{1,0:T(8,128)S(1)}, f32[128,128]{1,0:T(8,128)S(1)}, u32[]{:S(2)}, u32[]{:S(2)}) collective-permute-start(f32[128,128]{1,0:T(8,128)S(1)} %shard_map.38), channel_id=1, source_target_pairs={{0,1},{1,0},{2,3},{3,2},{4,5},{5,4},{6,7},{7,6},{8,9},{9,8},{10,11... | collective-permute-start | bytes 196616 | tf_op jit(solution)/shard_map/ppermute | solution.py:20
  17.5 4.3 %collective-permute-start.8 = (f32[128,128]{1,0:T(8,128)S(1)}, f32[128,128]{1,0:T(8,128)S(1)}, u32[]{:S(2)}, u32[]{:S(2)}) collective-permute-start(f32[128,128]{1,0:T(8,128)S(1)} %add.3.r_0_), channel_id=1, source_target_pairs={{0,2},{1,3},{2,0},{3,1},{4,6},{5,7},{6,4},{7,5},{8,10},{9,11},{10,... | collective-permute-start | bytes 196616 | tf_op jit(solution)/shard_map/ppermute | solution.py:20
  19.1 1.2 %collective-permute-start.9 = (bf16[16,256]{1,0:T(8,128)(2,1)S(1)}, bf16[16,256]{1,0:T(8,128)(2,1)S(1)}, u32[]{:S(2)}, u32[]{:S(2)}) collective-permute-start(bf16[16,256]{1,0:T(8,128)(2,1)S(1)} %copy-done), channel_id=1, source_target_pairs={{0,1},{1,0},{2,3},{3,2},{4,5},{5,4},{6,7},{7,6},{8,9},{9,8},{10,11... | collective-permute-start | bytes 24584 | tf_op jit(solution)/shard_map/ppermute | solution.py:20
  21.8 6.1 %collective-permute-start.10 = (bf16[192,128]{1,0:T(8,128)(2,1)S(1)}, bf16[192,128]{1,0:T(8,128)(2,1)S(1)}, u32[]{:S(2)}, u32[]{:S(2)}) collective-permute-start(bf16[192,128]{1,0:T(8,128)(2,1)S(1)} %shard_map.39.r_0_), channel_id=1, source_target_pairs={{0,24},{1,29},{2,26},{3,31},{4,28},{5,25},{6,30},{7,27},{8,16},{9,... | collective-permute-start | bytes 147464 | tf_op jit(solution)/shard_map/ppermute | solution.py:98
  24.0 5.2 %collective-permute-start.11 = (bf16[192,128]{1,0:T(8,128)(2,1)S(1)}, bf16[192,128]{1,0:T(8,128)(2,1)S(1)}, u32[]{:S(2)}, u32[]{:S(2)}) collective-permute-start(bf16[192,128]{1,0:T(8,128)(2,1)S(1)} %shard_map.39.r_0_), channel_id=1, source_target_pairs={{0,16},{1,21},{2,18},{3,23},{4,20},{5,17},{6,22},{7,19},{8,24},{9,... | collective-permute-start | bytes 147464 | tf_op jit(solution)/shard_map/ppermute | solution.py:98
  24.1 5.2 %collective-permute-start.12 = (bf16[192,128]{1,0:T(8,128)(2,1)S(1)}, bf16[192,128]{1,0:T(8,128)(2,1)S(1)}, u32[]{:S(2)}, u32[]{:S(2)}) collective-permute-start(bf16[192,128]{1,0:T(8,128)(2,1)S(1)} %shard_map.39.r_0_), channel_id=1, source_target_pairs={{0,8},{1,13},{2,10},{3,15},{4,12},{5,9},{6,14},{7,11},{8,0},{9,5},... | collective-permute-start | bytes 147464 | tf_op jit(solution)/shard_map/ppermute | solution.py:98
  26.3 4.1 %collective-permute-start.13 = (bf16[192,128]{1,0:T(8,128)(2,1)S(1)}, bf16[192,128]{1,0:T(8,128)(2,1)S(1)}, u32[]{:S(2)}, u32[]{:S(2)}) collective-permute-start(bf16[192,128]{1,0:T(8,128)(2,1)S(1)} %shard_map.39.r_0_), channel_id=1, source_target_pairs={{0,4},{1,5},{2,6},{3,7},{4,0},{5,1},{6,2},{7,3},{8,12},{9,13},{10,... | collective-permute-start | bytes 147464 | tf_op jit(solution)/shard_map/ppermute | solution.py:98
  27.9 2.5 %collective-permute-start.14 = (bf16[192,128]{1,0:T(8,128)(2,1)S(1)}, bf16[192,128]{1,0:T(8,128)(2,1)S(1)}, u32[]{:S(2)}, u32[]{:S(2)}) collective-permute-start(bf16[192,128]{1,0:T(8,128)(2,1)S(1)} %collective-permute-done.10.r_1_), channel_id=1, source_target_pairs={{0,1},{1,0},{2,3},{3,2},{4,5},{5,4},{6,7},{7,6},{8,9},{9,8},{10,11... | collective-permute-start | bytes 147464 | tf_op jit(solution)/shard_map/ppermute | solution.py:20
  29.3 1.2 %collective-permute-start.15 = (bf16[192,128]{1,0:T(8,128)(2,1)S(1)}, bf16[192,128]{1,0:T(8,128)(2,1)S(1)}, u32[]{:S(2)}, u32[]{:S(2)}) collective-permute-start(bf16[192,128]{1,0:T(8,128)(2,1)S(1)} %collective-permute-done.11.r_2_), channel_id=1, source_target_pairs={{0,1},{1,0},{2,3},{3,2},{4,5},{5,4},{6,7},{7,6},{8,9},{9,8},{10,11... | collective-permute-start | bytes 147464 | tf_op jit(solution)/shard_map/ppermute | solution.py:20
  29.3 1.4 %collective-permute-start.16 = (bf16[192,128]{1,0:T(8,128)(2,1)S(1)}, bf16[192,128]{1,0:T(8,128)(2,1)S(1)}, u32[]{:S(2)}, u32[]{:S(2)}) collective-permute-start(bf16[192,128]{1,0:T(8,128)(2,1)S(1)} %collective-permute-done.12.r_3_), channel_id=1, source_target_pairs={{0,1},{1,0},{2,3},{3,2},{4,5},{5,4},{6,7},{7,6},{8,9},{9,8},{10,11... | collective-permute-start | bytes 147464 | tf_op jit(solution)/shard_map/ppermute | solution.py:20

commit v5 on v4

--- a/solution.py
+++ b/solution.py
@@ -9,8 +9,8 @@
 
 BF16 = jnp.bfloat16
 F32 = jnp.float32
-GATHER = ((0, 1), (0, 4), (1, 4), (0, 2), (1, 2), (0, 6), (6, 1))
-SPREAD = ((0, 6, 7), (0, 4, 5), (0, 2, 3), (0, 1, 1))
+GATHER = ((0, 2, 5), (0, 1, 2), (0, 4, 1), (2, 2, 1), (0, 6, 6), (2, 4, 6), (5, 1, 1))
+SPREAD = ((0, 4, 5), (0, 6, 7), (0, 2, 3), (0, 1, 1))
 LANES = 128
 VMEM = pl.BlockSpec(memory_space=pltpu.VMEM)
 
@@ -41,12 +41,13 @@
     square_out[...] = jnp.sum((wide * wide).T, axis=0, keepdims=True)
 
 
-def dist_kernel(order, points_ref, square_ref, *refs):
-    tiles, (part_ref, centers) = refs[: len(order)], refs[len(order) :]
+def dist_kernel(sources, points_ref, square_ref, *refs):
+    tiles, (part_ref, centers) = refs[: len(sources)], refs[len(sources) :]
     rows = tiles[0].shape[0]
     blk = lax.axis_index("blk")
-    for k, tile in zip(order, tiles):
-        at = pl.multiple_of((blk ^ k) * rows, rows)
+    core = lax.axis_index("feat") % 2
+    for (even, odd), tile in zip(sources, tiles):
+        at = pl.multiple_of((blk ^ jnp.where(core == 0, even, odd)) * rows, rows)
         centers[pl.ds(at, rows), :] = tile[...]
     cross = lax.dot_general(
         centers[...], points_ref[...], (((1,), (1,)), ((), ())), preferred_element_type=F32
@@ -98,14 +99,20 @@
     return lax.ppermute(x, ("blk", "feat"), pairs)
 
 
+def gather(x, steps):
+    held, sources = [x], [(0, 0)]
+    for at, even, odd in steps:
+        held.append(swap_by_core(held[at], even, odd))
+        sources.append((sources[at][0] ^ even, sources[at][1] ^ odd))
+    return held, sources
+
+
 def on_device(points, centers, coefs):
     blks = lax.axis_size("blk")
     rows, local_points = centers.shape[0], points.shape[0]
     features = points.shape[1] * lax.axis_size("feat")
     all_rows = rows * blks
-    tiles = {0: centers}
-    for held, bits in GATHER:
-        tiles[held ^ bits] = swap(tiles[held], "blk", bits)
+    tiles, sources = gather(centers, GATHER)
     points, tiles[0], square = pl.pallas_call(
         prepare_kernel,
         out_shape=[pltpu.VMEM(points.shape, BF16), pltpu.VMEM(centers.shape, BF16), pltpu.VMEM((1, local_points), F32)],
@@ -114,13 +121,12 @@
         cost_estimate=pl.CostEstimate(flops=2 * points.size, bytes_accessed=2 * points.size, transcendentals=0),
     )(points, centers)
     others = swap(coefs, "feat", 1)
-    order = sorted(tiles)
     (part,) = call(
-        lambda *r: dist_kernel(order, *r),
+        lambda *r: dist_kernel(sources, *r),
         [jax.ShapeDtypeStruct((all_rows, local_points), F32)],
         points,
         square,
-        *[tiles[k] for k in order],
+        *tiles,
         scratch=[pltpu.VMEM((all_rows, points.shape[1]), BF16)],
     )
     part = part + swap(part, "feat", 1)
@@ -134,10 +140,7 @@
         coefs,
         others,
     )
-    held, sources = [tile], [(0, 0)]
-    for at, even, odd in SPREAD:
-        held.append(swap_by_core(held[at], even, odd))
-        sources.append((sources[at][0] ^ even, sources[at][1] ^ odd))
+    held, sources = gather(tile, SPREAD)
     passed = [i for i, (even, odd) in enumerate(sources) if even != odd]
     held += [swap(held[i], "feat", 1) for i in passed]
     sources += [sources[i][::-1] for i in passed]

time: 32.1 us -> 31.6 us (0.984)
  starting transfers between devices: 19.2 us -> 18.2 us
  waiting for transfers between devices: 9.65 us -> 10.2 us
    ppermute x13 -> x6, starting transfers between devices: 14.2 us -> 2.05 us  [swap(): return lax.ppermute(x, axis, [(i, i ^ bits) for i in range(n)])]
    ppermute x4 -> x11, starting transfers between devices: 4.98 us -> 16.1 us  [swap_by_core(): return lax.ppermute(x, ('blk', 'feat'), pairs)]
    ppermute x4 -> x11, waiting for transfers between devices: 3.04 us -> 5.47 us  [swap_by_core(): return lax.ppermute(x, ('blk', 'feat'), pairs)]
    ppermute x13 -> x6, waiting for transfers between devices: 6.6 us -> 4.76 us  [swap(): return lax.ppermute(x, axis, [(i, i ^ bits) for i in range(n)])]
  transfers between devices with their start and end apart: 17 -> 17, of which waited for: 11 -> 12; matrix products, arithmetic and copies ran while one was open for 0% -> 0% of each run, Pallas kernels for 4% -> 4%
where the time goes in v5:
time: 31.6 us; the launch traced here: 31.5 us
  starting transfers between devices  18.2 us (58%)
  waiting for transfers between devices  10.2 us (32%)
  Pallas kernels  2.35 us (7%)
  local copies, waits for them, and re-layouts  0.68 us (2%)
    ppermute x11, starting transfers between devices, swap_by_core(): return lax.ppermute(x, ('blk', 'feat'), pairs)  16.1 us
    ppermute x11, waiting for transfers between devices, swap_by_core(): return lax.ppermute(x, ('blk', 'feat'), pairs)  5.47 us
    ppermute x6, waiting for transfers between devices, swap(): return lax.ppermute(x, axis, [(i, i ^ bits) for i in range(n)])  4.76 us
    ppermute x6, starting transfers between devices, swap(): return lax.ppermute(x, axis, [(i, i ^ bits) for i in range(n)])  2.05 us
    pallas_call x1, Pallas kernels, on_device(): pl.pallas_call(prepare_kernel, out_shape=[pltpu.VMEM(points.shape, BF16),...  1.41 us
    pallas_call x3, Pallas kernels, call(): pl.pallas_call(kernel, out_shape=[pltpu.VMEM(o.shape, o.dtype) for o in o...  0.94 us
    unnamed x3, local copies, waits for them, and re-layouts  0.68 us
  transfers between devices with their start and end apart: 17, of which 12 were waited for; matrix products, arithmetic and copies ran while one was open for 0% of the time, Pallas kernels for 4%

profile of v5, /device:TPU:0, one launch (start us, length us, event | category | flops | bytes accessed | tf_op | source)
XLA Modules:
  0.0 31.5 jit_solution(12890154535388785956)
XLA Ops:
  0.0 2.9 %collective-permute-start.1 = (bf16[16,2048]{1,0:T(8,128)(2,1)}, bf16[16,2048]{1,0:T(8,128)(2,1)S(1)}, u32[]{:S(2)}, u32[]{:S(2)}) collective-permute-start(bf16[16,2048]{1,0:T(8,128)(2,1)} %centers_ref.1), channel_id=1, source_target_pairs={{0,4},{1,9},{2,6},{3,11},{4,0},{5,13},{6,2},{7,15},{8,12},{9,1},{1... | collective-permute-start | bytes 196616 | tf_op jit(solution)/shard_map/ppermute | solution.py:99
  2.9 3.6 %collective-permute-start.4 = (bf16[16,2048]{1,0:T(8,128)(2,1)}, bf16[16,2048]{1,0:T(8,128)(2,1)S(1)}, u32[]{:S(2)}, u32[]{:S(2)}) collective-permute-start(bf16[16,2048]{1,0:T(8,128)(2,1)} %centers_ref.1), channel_id=1, source_target_pairs={{0,24},{1,25},{2,26},{3,27},{4,28},{5,29},{6,30},{7,31},{8,16},{9,... | collective-permute-start | bytes 196616 | tf_op jit(solution)/shard_map/ppermute | solution.py:99
  6.5 0.8 %collective-permute-start.2 = (bf16[16,2048]{1,0:T(8,128)(2,1)}, bf16[16,2048]{1,0:T(8,128)(2,1)S(1)}, u32[]{:S(2)}, u32[]{:S(2)}) collective-permute-start(bf16[16,2048]{1,0:T(8,128)(2,1)} %centers_ref.1), channel_id=1, source_target_pairs={{0,16},{1,5},{2,18},{3,7},{4,20},{5,1},{6,22},{7,3},{8,24},{9,13},... | collective-permute-start | bytes 196616 | tf_op jit(solution)/shard_map/ppermute | solution.py:99
  7.3 1.2 %collective-permute-start.3 = (bf16[16,2048]{1,0:T(8,128)(2,1)S(1)}, bf16[16,2048]{1,0:T(8,128)(2,1)S(1)}, u32[]{:S(2)}, u32[]{:S(2)}) collective-permute-start(bf16[16,2048]{1,0:T(8,128)(2,1)S(1)} %collective-permute-done.1.r_4_), channel_id=1, source_target_pairs={{0,8},{1,5},{2,10},{3,7},{4,12},{5,1},{6,14},{7,3},{8,0},{9,13},{1... | collective-permute-start | bytes 196616 | tf_op jit(solution)/shard_map/ppermute | solution.py:99
  8.6 2.9 %collective-permute-start.5 = (bf16[16,2048]{1,0:T(8,128)(2,1)S(1)}, bf16[16,2048]{1,0:T(8,128)(2,1)S(1)}, u32[]{:S(2)}, u32[]{:S(2)}) collective-permute-start(bf16[16,2048]{1,0:T(8,128)(2,1)S(1)} %collective-permute-done.1.r_4_), channel_id=1, source_target_pairs={{0,16},{1,25},{2,18},{3,27},{4,20},{5,29},{6,22},{7,31},{8,24},{9,... | collective-permute-start | bytes 196616 | tf_op jit(solution)/shard_map/ppermute | solution.py:99
  11.5 0.5 %collective-permute-start.6 = (bf16[16,2048]{1,0:T(8,128)(2,1)S(1)}, bf16[16,2048]{1,0:T(8,128)(2,1)S(1)}, u32[]{:S(2)}, u32[]{:S(2)}) collective-permute-start(bf16[16,2048]{1,0:T(8,128)(2,1)S(1)} %collective-permute-done.4.r_7_), channel_id=1, source_target_pairs={{0,4},{1,5},{2,6},{3,7},{4,0},{5,1},{6,2},{7,3},{8,12},{9,13},{10,... | collective-permute-start | bytes 196616 | tf_op jit(solution)/shard_map/ppermute | solution.py:99
  12.0 1.4 %shard_map.37 = (bf16[128,2048]{1,0:T(8,128)(2,1)S(1)}, bf16[16,2048]{1,0:T(8,128)(2,1)S(1)}, f32[1,128]{1,0:T(1,128)S(1)}) custom-call(bf16[128,2048]{1,0:T(8,128)(2,1)} %points_ref.1, bf16[16,2048]{1,0:T(8,128)(2,1)} %centers_ref.1), custom_call_target="tpu_custom_call" | custom-call | flops 524288 | bytes 524288 | tf_op jit(solution)/shard_map/pallas_call | solution.py:116
  13.6 1.4 %collective-permute-done.5.r_8_ = bf16[16,2048]{1,0:T(8,128)(2,1)S(1)} collective-permute-done((bf16[16,2048]{1,0:T(8,128)(2,1)S(1)}, bf16[16,2048]{1,0:T(8,128)(2,1)S(1)}, u32[]{:S(2)}, u32[]{:S(2)}) %collective-permute-start.5) | collective-permute-done | bytes 65568 | tf_op jit(solution)/shard_map/ppermute | solution.py:99
  15.0 0.7 %collective-permute-done.6.r_9_ = bf16[16,2048]{1,0:T(8,128)(2,1)S(1)} collective-permute-done((bf16[16,2048]{1,0:T(8,128)(2,1)S(1)}, bf16[16,2048]{1,0:T(8,128)(2,1)S(1)}, u32[]{:S(2)}, u32[]{:S(2)}) %collective-permute-start.6) | collective-permute-done | bytes 65568 | tf_op jit(solution)/shard_map/ppermute | solution.py:99
  15.8 0.3 %shard_map.38 = f32[128,128]{1,0:T(8,128)S(1)} custom-call(bf16[128,2048]{1,0:T(8,128)(2,1)S(1)} %get-tuple-element.8.r_0_, f32[1,128]{1,0:T(1,128)S(1)} %get-tuple-element.9.r_1_, bf16[16,2048]{1,0:T(8,128)(2,1)S(1)} %get-tuple-element.10.r_2_, bf16[16,2048]{1,0:T(8,128)(2,1)S(1)} %collective-permute-done.r_3_, ...), custom_call_target="tpu_custom_call" | custom-call | tf_op jit(solution)/shard_map/pallas_call | solution.py:28
  16.2 1.2 %collective-permute-done.7 = f32[128,128]{1,0:T(8,128)S(1)} collective-permute-done((f32[128,128]{1,0:T(8,128)S(1)}, f32[128,128]{1,0:T(8,128)S(1)}, u32[]{:S(2)}, u32[]{:S(2)}) %collective-permute-start.7) | collective-permute-done | bytes 65568 | tf_op jit(solution)/shard_map/ppermute | solution.py:20
  17.5 1.6 %collective-permute-start.8 = (f32[128,128]{1,0:T(8,128)S(1)}, f32[128,128]{1,0:T(8,128)S(1)}, u32[]{:S(2)}, u32[]{:S(2)}) collective-permute-start(f32[128,128]{1,0:T(8,128)S(1)} %add.3.r_0_), channel_id=1, source_target_pairs={{0,2},{1,3},{2,0},{3,1},{4,6},{5,7},{6,4},{7,5},{8,10},{9,11},{10,... | collective-permute-start | bytes 196616 | tf_op jit(solution)/shard_map/ppermute | solution.py:20
  19.1 1.2 %collective-permute-done.9.r_3_ = bf16[16,256]{1,0:T(8,128)(2,1)S(1)} collective-permute-done((bf16[16,256]{1,0:T(8,128)(2,1)S(1)}, bf16[16,256]{1,0:T(8,128)(2,1)S(1)}, u32[]{:S(2)}, u32[]{:S(2)}) %collective-permute-start.9) | collective-permute-done | bytes 8224 | tf_op jit(solution)/shard_map/ppermute | solution.py:20
  20.2 1.6 %collective-permute-done.8.r_1_ = f32[128,128]{1,0:T(8,128)S(1)} collective-permute-done((f32[128,128]{1,0:T(8,128)S(1)}, f32[128,128]{1,0:T(8,128)S(1)}, u32[]{:S(2)}, u32[]{:S(2)}) %collective-permute-start.8) | collective-permute-done | bytes 65568 | tf_op jit(solution)/shard_map/ppermute | solution.py:20
  21.8 1.0 %collective-permute-start.10 = (bf16[192,128]{1,0:T(8,128)(2,1)S(1)}, bf16[192,128]{1,0:T(8,128)(2,1)S(1)}, u32[]{:S(2)}, u32[]{:S(2)}) collective-permute-start(bf16[192,128]{1,0:T(8,128)(2,1)S(1)} %shard_map.39.r_0_), channel_id=1, source_target_pairs={{0,16},{1,21},{2,18},{3,23},{4,20},{5,17},{6,22},{7,19},{8,24},{9,... | collective-permute-start | bytes 147464 | tf_op jit(solution)/shard_map/ppermute | solution.py:99
  22.8 1.5 %collective-permute-start.11 = (bf16[192,128]{1,0:T(8,128)(2,1)S(1)}, bf16[192,128]{1,0:T(8,128)(2,1)S(1)}, u32[]{:S(2)}, u32[]{:S(2)}) collective-permute-start(bf16[192,128]{1,0:T(8,128)(2,1)S(1)} %shard_map.39.r_0_), channel_id=1, source_target_pairs={{0,24},{1,29},{2,26},{3,31},{4,28},{5,25},{6,30},{7,27},{8,16},{9,... | collective-permute-start | bytes 147464 | tf_op jit(solution)/shard_map/ppermute | solution.py:99
  24.3 1.1 %collective-permute-start.12 = (bf16[192,128]{1,0:T(8,128)(2,1)S(1)}, bf16[192,128]{1,0:T(8,128)(2,1)S(1)}, u32[]{:S(2)}, u32[]{:S(2)}) collective-permute-start(bf16[192,128]{1,0:T(8,128)(2,1)S(1)} %shard_map.39.r_0_), channel_id=1, source_target_pairs={{0,8},{1,13},{2,10},{3,15},{4,12},{5,9},{6,14},{7,11},{8,0},{9,5},... | collective-permute-start | bytes 147464 | tf_op jit(solution)/shard_map/ppermute | solution.py:99
  25.4 0.5 %collective-permute-start.13 = (bf16[192,128]{1,0:T(8,128)(2,1)S(1)}, bf16[192,128]{1,0:T(8,128)(2,1)S(1)}, u32[]{:S(2)}, u32[]{:S(2)}) collective-permute-start(bf16[192,128]{1,0:T(8,128)(2,1)S(1)} %shard_map.39.r_0_), channel_id=1, source_target_pairs={{0,4},{1,5},{2,6},{3,7},{4,0},{5,1},{6,2},{7,3},{8,12},{9,13},{10,... | collective-permute-start | bytes 147464 | tf_op jit(solution)/shard_map/ppermute | solution.py:99
  25.9 1.7 %collective-permute-done.10.r_1_ = bf16[192,128]{1,0:T(8,128)(2,1)S(1)} collective-permute-done((bf16[192,128]{1,0:T(8,128)(2,1)S(1)}, bf16[192,128]{1,0:T(8,128)(2,1)S(1)}, u32[]{:S(2)}, u32[]{:S(2)}) %collective-permute-start.10) | collective-permute-done | bytes 49184 | tf_op jit(solution)/shard_map/ppermute | solution.py:99
  27.6 1.2 %collective-permute-done.11.r_2_ = bf16[192,128]{1,0:T(8,128)(2,1)S(1)} collective-permute-done((bf16[192,128]{1,0:T(8,128)(2,1)S(1)}, bf16[192,128]{1,0:T(8,128)(2,1)S(1)}, u32[]{:S(2)}, u32[]{:S(2)}) %collective-permute-start.11) | collective-permute-done | bytes 49184 | tf_op jit(solution)/shard_map/ppermute | solution.py:99
  29.0 0.4 %collective-permute-start.16 = (bf16[192,128]{1,0:T(8,128)(2,1)S(1)}, bf16[192,128]{1,0:T(8,128)(2,1)S(1)}, u32[]{:S(2)}, u32[]{:S(2)}) collective-permute-start(bf16[192,128]{1,0:T(8,128)(2,1)S(1)} %collective-permute-done.12.r_3_), channel_id=1, source_target_pairs={{0,1},{1,0},{2,3},{3,2},{4,5},{5,4},{6,7},{7,6},{8,9},{9,8},{10,11... | collective-permute-start | bytes 147464 | tf_op jit(solution)/shard_map/ppermute | solution.py:20
  29.5 0.6 %collective-permute-done.15.r_6_ = bf16[192,128]{1,0:T(8,128)(2,1)S(1)} collective-permute-done((bf16[192,128]{1,0:T(8,128)(2,1)S(1)}, bf16[192,128]{1,0:T(8,128)(2,1)S(1)}, u32[]{:S(2)}, u32[]{:S(2)}) %collective-permute-start.15) | collective-permute-done | bytes 49184 | tf_op jit(solution)/shard_map/ppermute | solution.py:20
  30.2 0.6 %shard_map.40 = f32[16,256]{1,0:T(8,128)S(1)} custom-call(bf16[192,128]{1,0:T(8,128)(2,1)S(1)} %shard_map.39.r_0_, bf16[192,128]{1,0:T(8,128)(2,1)S(1)} %collective-permute-done.10.r_1_, bf16[192,128]{1,0:T(8,128)(2,1)S(1)} %collective-permute-done.11.r_2_, bf16[192,128]{1,0:T(8,128)(2,1)S(1)} %collective-permute-done.12.r_3_, ...), custom_call_target="tpu_custom_call" | custom-call | tf_op jit(solution)/shard_map/pallas_call | solution.py:28
  30.8 0.7 %copy.4 = f32[16,256]{1,0:T(8,128)} copy(f32[16,256]{1,0:T(8,128)S(1)} %shard_map.40) | data formatting | bytes 32768
  (18 shorter events, 0.7 us)
Async XLA Ops:
  0.0 7.3 %collective-permute-start.1 = (bf16[16,2048]{1,0:T(8,128)(2,1)}, bf16[16,2048]{1,0:T(8,128)(2,1)S(1)}, u32[]{:S(2)}, u32[]{:S(2)}) collective-permute-start(bf16[16,2048]{1,0:T(8,128)(2,1)} %centers_ref.1), channel_id=1, source_target_pairs={{0,4},{1,9},{2,6},{3,11},{4,0},{5,13},{6,2},{7,15},{8,12},{9,1},{1... | collective-permute-start | bytes 196616 | tf_op jit(solution)/shard_map/ppermute | solution.py:99
  2.9 8.6 %collective-permute-start.4 = (bf16[16,2048]{1,0:T(8,128)(2,1)}, bf16[16,2048]{1,0:T(8,128)(2,1)S(1)}, u32[]{:S(2)}, u32[]{:S(2)}) collective-permute-start(bf16[16,2048]{1,0:T(8,128)(2,1)} %centers_ref.1), channel_id=1, source_target_pairs={{0,24},{1,25},{2,26},{3,27},{4,28},{5,29},{6,30},{7,31},{8,16},{9,... | collective-permute-start | bytes 196616 | tf_op jit(solution)/shard_map/ppermute | solution.py:99
  6.5 6.9 %collective-permute-start = (bf16[16,2048]{1,0:T(8,128)(2,1)}, bf16[16,2048]{1,0:T(8,128)(2,1)S(1)}, u32[]{:S(2)}, u32[]{:S(2)}) collective-permute-start(bf16[16,2048]{1,0:T(8,128)(2,1)} %centers_ref.1), channel_id=1, source_target_pairs={{0,8},{1,21},{2,10},{3,23},{4,12},{5,17},{6,14},{7,19},{8,0},{9,29... | collective-permute-start | bytes 196616 | tf_op jit(solution)/shard_map/ppermute | solution.py:99
  6.5 7.1 %collective-permute-start.2 = (bf16[16,2048]{1,0:T(8,128)(2,1)}, bf16[16,2048]{1,0:T(8,128)(2,1)S(1)}, u32[]{:S(2)}, u32[]{:S(2)}) collective-permute-start(bf16[16,2048]{1,0:T(8,128)(2,1)} %centers_ref.1), channel_id=1, source_target_pairs={{0,16},{1,5},{2,18},{3,7},{4,20},{5,1},{6,22},{7,3},{8,24},{9,13},... | collective-permute-start | bytes 196616 | tf_op jit(solution)/shard_map/ppermute | solution.py:99
  7.3 6.3 %collective-permute-start.3 = (bf16[16,2048]{1,0:T(8,128)(2,1)S(1)}, bf16[16,2048]{1,0:T(8,128)(2,1)S(1)}, u32[]{:S(2)}, u32[]{:S(2)}) collective-permute-start(bf16[16,2048]{1,0:T(8,128)(2,1)S(1)} %collective-permute-done.1.r_4_), channel_id=1, source_target_pairs={{0,8},{1,5},{2,10},{3,7},{4,12},{5,1},{6,14},{7,3},{8,0},{9,13},{1... | collective-permute-start | bytes 196616 | tf_op jit(solution)/shard_map/ppermute | solution.py:99
  8.6 6.5 %collective-permute-start.5 = (bf16[16,2048]{1,0:T(8,128)(2,1)S(1)}, bf16[16,2048]{1,0:T(8,128)(2,1)S(1)}, u32[]{:S(2)}, u32[]{:S(2)}) collective-permute-start(bf16[16,2048]{1,0:T(8,128)(2,1)S(1)} %collective-permute-done.1.r_4_), channel_id=1, source_target_pairs={{0,16},{1,25},{2,18},{3,27},{4,20},{5,29},{6,22},{7,31},{8,24},{9,... | collective-permute-start | bytes 196616 | tf_op jit(solution)/shard_map/ppermute | solution.py:99
  11.5 4.3 %collective-permute-start.6 = (bf16[16,2048]{1,0:T(8,128)(2,1)S(1)}, bf16[16,2048]{1,0:T(8,128)(2,1)S(1)}, u32[]{:S(2)}, u32[]{:S(2)}) collective-permute-start(bf16[16,2048]{1,0:T(8,128)(2,1)S(1)} %collective-permute-done.4.r_7_), channel_id=1, source_target_pairs={{0,4},{1,5},{2,6},{3,7},{4,0},{5,1},{6,2},{7,3},{8,12},{9,13},{10,... | collective-permute-start | bytes 196616 | tf_op jit(solution)/shard_map/ppermute | solution.py:99
  16.1 2.9 %copy-start = (bf16[16,256]{1,0:T(8,128)(2,1)S(1)}, bf16[16,256]{1,0:T(8,128)(2,1)}, u32[]{:S(2)}) copy-start(bf16[16,256]{1,0:T(8,128)(2,1)} %r_2_.1) | copy-start | bytes 24580
  16.1 1.3 %collective-permute-start.7 = (f32[128,128]{1,0:T(8,128)S(1)}, f32[128,128]{1,0:T(8,128)S(1)}, u32[]{:S(2)}, u32[]{:S(2)}) collective-permute-start(f32[128,128]{1,0:T(8,128)S(1)} %shard_map.38), channel_id=1, source_target_pairs={{0,1},{1,0},{2,3},{3,2},{4,5},{5,4},{6,7},{7,6},{8,9},{9,8},{10,11... | collective-permute-start | bytes 196616 | tf_op jit(solution)/shard_map/ppermute | solution.py:20
  17.5 4.3 %collective-permute-start.8 = (f32[128,128]{1,0:T(8,128)S(1)}, f32[128,128]{1,0:T(8,128)S(1)}, u32[]{:S(2)}, u32[]{:S(2)}) collective-permute-start(f32[128,128]{1,0:T(8,128)S(1)} %add.3.r_0_), channel_id=1, source_target_pairs={{0,2},{1,3},{2,0},{3,1},{4,6},{5,7},{6,4},{7,5},{8,10},{9,11},{10,... | collective-permute-start | bytes 196616 | tf_op jit(solution)/shard_map/ppermute | solution.py:20
  19.1 1.2 %collective-permute-start.9 = (bf16[16,256]{1,0:T(8,128)(2,1)S(1)}, bf16[16,256]{1,0:T(8,128)(2,1)S(1)}, u32[]{:S(2)}, u32[]{:S(2)}) collective-permute-start(bf16[16,256]{1,0:T(8,128)(2,1)S(1)} %copy-done), channel_id=1, source_target_pairs={{0,1},{1,0},{2,3},{3,2},{4,5},{5,4},{6,7},{7,6},{8,9},{9,8},{10,11... | collective-permute-start | bytes 24584 | tf_op jit(solution)/shard_map/ppermute | solution.py:20
  21.8 5.8 %collective-permute-start.10 = (bf16[192,128]{1,0:T(8,128)(2,1)S(1)}, bf16[192,128]{1,0:T(8,128)(2,1)S(1)}, u32[]{:S(2)}, u32[]{:S(2)}) collective-permute-start(bf16[192,128]{1,0:T(8,128)(2,1)S(1)} %shard_map.39.r_0_), channel_id=1, source_target_pairs={{0,16},{1,21},{2,18},{3,23},{4,20},{5,17},{6,22},{7,19},{8,24},{9,... | collective-permute-start | bytes 147464 | tf_op jit(solution)/shard_map/ppermute | solution.py:99
  22.8 6.1 %collective-permute-start.11 = (bf16[192,128]{1,0:T(8,128)(2,1)S(1)}, bf16[192,128]{1,0:T(8,128)(2,1)S(1)}, u32[]{:S(2)}, u32[]{:S(2)}) collective-permute-start(bf16[192,128]{1,0:T(8,128)(2,1)S(1)} %shard_map.39.r_0_), channel_id=1, source_target_pairs={{0,24},{1,29},{2,26},{3,31},{4,28},{5,25},{6,30},{7,27},{8,16},{9,... | collective-permute-start | bytes 147464 | tf_op jit(solution)/shard_map/ppermute | solution.py:99
  24.3 4.7 %collective-permute-start.12 = (bf16[192,128]{1,0:T(8,128)(2,1)S(1)}, bf16[192,128]{1,0:T(8,128)(2,1)S(1)}, u32[]{:S(2)}, u32[]{:S(2)}) collective-permute-start(bf16[192,128]{1,0:T(8,128)(2,1)S(1)} %shard_map.39.r_0_), channel_id=1, source_target_pairs={{0,8},{1,13},{2,10},{3,15},{4,12},{5,9},{6,14},{7,11},{8,0},{9,5},... | collective-permute-start | bytes 147464 | tf_op jit(solution)/shard_map/ppermute | solution.py:99
  25.4 4.1 %collective-permute-start.13 = (bf16[192,128]{1,0:T(8,128)(2,1)S(1)}, bf16[192,128]{1,0:T(8,128)(2,1)S(1)}, u32[]{:S(2)}, u32[]{:S(2)}) collective-permute-start(bf16[192,128]{1,0:T(8,128)(2,1)S(1)} %shard_map.39.r_0_), channel_id=1, source_target_pairs={{0,4},{1,5},{2,6},{3,7},{4,0},{5,1},{6,2},{7,3},{8,12},{9,13},{10,... | collective-permute-start | bytes 147464 | tf_op jit(solution)/shard_map/ppermute | solution.py:99
  27.6 1.8 %collective-permute-start.14 = (bf16[192,128]{1,0:T(8,128)(2,1)S(1)}, bf16[192,128]{1,0:T(8,128)(2,1)S(1)}, u32[]{:S(2)}, u32[]{:S(2)}) collective-permute-start(bf16[192,128]{1,0:T(8,128)(2,1)S(1)} %collective-permute-done.10.r_1_), channel_id=1, source_target_pairs={{0,1},{1,0},{2,3},{3,2},{4,5},{5,4},{6,7},{7,6},{8,9},{9,8},{10,11... | collective-permute-start | bytes 147464 | tf_op jit(solution)/shard_map/ppermute | solution.py:20
  28.8 1.2 %collective-permute-start.15 = (bf16[192,128]{1,0:T(8,128)(2,1)S(1)}, bf16[192,128]{1,0:T(8,128)(2,1)S(1)}, u32[]{:S(2)}, u32[]{:S(2)}) collective-permute-start(bf16[192,128]{1,0:T(8,128)(2,1)S(1)} %collective-permute-done.11.r_2_), channel_id=1, source_target_pairs={{0,1},{1,0},{2,3},{3,2},{4,5},{5,4},{6,7},{7,6},{8,9},{9,8},{10,11... | collective-permute-start | bytes 147464 | tf_op jit(solution)/shard_map/ppermute | solution.py:20
  29.0 1.3 %collective-permute-start.16 = (bf16[192,128]{1,0:T(8,128)(2,1)S(1)}, bf16[192,128]{1,0:T(8,128)(2,1)S(1)}, u32[]{:S(2)}, u32[]{:S(2)}) collective-permute-start(bf16[192,128]{1,0:T(8,128)(2,1)S(1)} %collective-permute-done.12.r_3_), channel_id=1, source_target_pairs={{0,1},{1,0},{2,3},{3,2},{4,5},{5,4},{6,7},{7,6},{8,9},{9,8},{10,11... | collective-permute-start | bytes 147464 | tf_op jit(solution)/shard_map/ppermute | solution.py:20

commit v6 on v5

v6 whole, which is shorter than its diff:
```python
import math

import jax
import jax.numpy as jnp
from jax import lax
from jax.experimental import pallas as pl
from jax.experimental.pallas import tpu as pltpu
from jax.sharding import PartitionSpec as P

BF16 = jnp.bfloat16
F32 = jnp.float32
VMEM = pl.BlockSpec(memory_space=pltpu.VMEM)

GATHER = ((0, 2, 5), (0, 1, 2), (0, 4, 1), (2, 2, 1), (0, 6, 6), (2, 4, 6), (5, 1, 1))
SPREAD = ((0, 4, 5), (0, 6, 7), (0, 2, 3), (0, 1, 1))


def near(x):
    return pltpu.with_memory_space_constraint(x, pltpu.VMEM)


def call(kernel, outs, *args, scratch=()):
    return pl.pallas_call(
        kernel,
        out_shape=[pltpu.VMEM(*o) for o in outs],
        in_specs=[VMEM] * len(args),
        out_specs=[VMEM] * len(outs),
        scratch_shapes=list(scratch),
    )(*[near(x) for x in args])


def place(bits, rows):
    even, odd = bits
    core = lax.axis_index("feat") % 2
    return pl.multiple_of((lax.axis_index("blk") ^ jnp.where(core == 0, even, odd)) * rows, rows)


def prepare_kernel(points_ref, centers_ref, points_out, centers_out, square_out):
    points_out[...] = points_ref[...]
    centers_out[...] = centers_ref[...]
    wide = points_ref[...].astype(F32)
    square_out[...] = jnp.sum((wide * wide).T, axis=0, keepdims=True)


def dist_kernel(sources, points_ref, square_ref, *refs):
    tiles, (part_ref, centers) = refs[: len(sources)], refs[len(sources) :]
    rows = tiles[0].shape[0]
    for bits, tile in zip(sources, tiles):
        centers[pl.ds(place(bits, rows), rows), :] = tile[...]
    cross = lax.dot_general(
        centers[...], points_ref[...], (((1,), (1,)), ((), ())), preferred_element_type=F32
    )
    wide = centers[...].astype(F32)
    center_sq = jnp.sum(wide * wide, axis=1, keepdims=True)
    part_ref[...] = square_ref[...] + center_sq - 2.0 * cross


def send_kernel(features, a_ref, b_ref, coefs_ref, others_ref, out_ref):
    all_rows, width = a_ref.shape
    rows, pieces = coefs_ref.shape[0], coefs_ref.shape[1] // width
    out_ref[:all_rows, :] = jnp.exp(-(a_ref[...] + b_ref[...]) / features).astype(BF16)
    core = lax.axis_index("feat") % 2
    for half, ref in ((core, coefs_ref), (1 - core, others_ref)):
        for i in range(pieces):
            at = pl.multiple_of(all_rows + (half * pieces + i) * rows, rows)
            out_ref[pl.ds(at, rows), :] = ref[:, i * width : (i + 1) * width]


def product_kernel(sources, rows, scale, *refs):
    tiles, (out_ref, kernel, coefs) = refs[: len(sources)], refs[len(sources) :]
    all_rows, width = kernel.shape[0], tiles[0].shape[1]
    pieces = coefs.shape[1] // width
    core = lax.axis_index("feat") % 2
    for i, (bits, tile) in enumerate(zip(sources, tiles)):
        kernel[:, i * width : (i + 1) * width] = tile[:all_rows, :]
        at = place(bits, rows)
        for j in range(pieces):
            top = pl.multiple_of(all_rows + (core * pieces + j) * rows, rows)
            coefs[pl.ds(at, rows), j * width : (j + 1) * width] = tile[pl.ds(top, rows), :]
    fitted = lax.dot_general(
        coefs[...].T, kernel[...], (((1,), (0,)), ((), ())), preferred_element_type=F32
    ).astype(BF16)
    own = kernel[pl.ds(place((0, 0), rows), rows), :]
    out_ref[...] = scale * lax.dot_general(
        own, fitted, (((1,), (1,)), ((), ())), preferred_element_type=F32
    )


def swap(x, bits):
    return lax.ppermute(x, "feat", [(f, f ^ bits) for f in range(lax.axis_size("feat"))])


def swap_by_core(x, even, odd):
    feats, blks = lax.axis_size("feat"), lax.axis_size("blk")
    pairs = [
        (b * feats + f, (b ^ (odd if f % 2 else even)) * feats + f)
        for b in range(blks)
        for f in range(feats)
    ]
    return lax.ppermute(x, ("blk", "feat"), pairs)


def gather(x, steps):
    held, sources = [x], [(0, 0)]
    for at, even, odd in steps:
        held.append(swap_by_core(held[at], even, odd))
        sources.append((sources[at][0] ^ even, sources[at][1] ^ odd))
    return held, sources


def on_device(points, centers, coefs):
    blks, feats = lax.axis_size("blk"), lax.axis_size("feat")
    rows, local_points = centers.shape[0], points.shape[0]
    all_rows = rows * blks
    features = points.shape[1] * feats

    tiles, sources = gather(centers, GATHER)
    points, tiles[0], square = pl.pallas_call(
        prepare_kernel,
        out_shape=[pltpu.VMEM(points.shape, BF16), pltpu.VMEM(centers.shape, BF16), pltpu.VMEM((1, local_points), F32)],
        in_specs=[VMEM] * 2,
        out_specs=[VMEM] * 3,
        cost_estimate=pl.CostEstimate(flops=2 * points.size, bytes_accessed=2 * points.size, transcendentals=0),
    )(points, centers)
    others = swap(coefs, 1)
    (part,) = call(
        lambda *r: dist_kernel(sources, *r),
        [((all_rows, local_points), F32)],
        points,
        square,
        *tiles,
        scratch=[pltpu.VMEM((all_rows, points.shape[1]), BF16)],
    )
    bits = 1
    while 2 * bits < feats:
        part = part + swap(part, bits)
        bits *= 2
    far = swap(part, bits)
    (tile,) = call(
        lambda *r: send_kernel(float(features), *r),
        [((all_rows + 2 * rows * (coefs.shape[1] // local_points), local_points), BF16)],
        part,
        far,
        coefs,
        others,
    )
    held, sources = gather(tile, SPREAD)
    passed = [i for i, (even, odd) in enumerate(sources) if even != odd]
    held += [swap(held[i], 1) for i in passed]
    sources += [sources[i][::-1] for i in passed]
    scale = 1.0 / math.sqrt(local_points * blks)
    (out,) = call(
        lambda *r: product_kernel(sources, rows, scale, *r),
        [((rows, coefs.shape[1]), F32)],
        *held,
        scratch=[pltpu.VMEM((all_rows, local_points * blks), BF16), pltpu.VMEM((all_rows, coefs.shape[1]), BF16)],
    )
    return out


def on_device_unplanned(points, centers, coefs):
    features = points.shape[1] * lax.axis_size("feat")
    point_sq = jnp.einsum("nf,nf->n", points, points, preferred_element_type=F32)
    center_piece = lax.all_gather(centers, "blk", axis=0, tiled=True)
    center_sq = jnp.einsum("mf,mf->m", center_piece, center_piece, preferred_element_type=F32)
    cross_dot = lax.dot_general(
        points, center_piece, (((1,), (1,)), ((), ())), preferred_element_type=F32
    )
    dist_tile = point_sq[:, None] + center_sq[None, :] - 2.0 * cross_dot
    all_coefs = lax.all_gather(coefs, "blk", axis=0, tiled=True)
    dist = lax.psum(dist_tile, "feat")
    kernel = jnp.exp(-dist / features).astype(BF16)
    fitted = jnp.dot(kernel, all_coefs, preferred_element_type=F32).astype(BF16)
    summed = lax.psum_scatter(
        lax.dot_general(kernel, fitted, (((0,), (0,)), ((), ())), preferred_element_type=F32),
        "blk",
        scatter_dimension=0,
        tiled=True,
    )
    return summed * (1.0 / math.sqrt(points.shape[0] * lax.axis_size("blk")))


def solution(mesh):
    blks, feats = mesh.shape["blk"], mesh.shape["feat"]
    planned = blks == len(GATHER) + 1 and feats % 2 == 0 and feats & (feats - 1) == 0
    return jax.shard_map(
        on_device if planned else on_device_unplanned,
        mesh=mesh,
        in_specs=(P("blk", "feat"),) * 3,
        out_specs=P("blk", "feat"),
        check_vma=False,
    )
```

time: 31.6 us -> 31.6 us (level)
  no operation moved by 1% of the time
where the time goes in v6:
time: 31.6 us; the launch traced here: 31.5 us
  starting transfers between devices  18.2 us (58%)
  waiting for transfers between devices  10.2 us (32%)
  Pallas kernels  2.34 us (7%)
  local copies, waits for them, and re-layouts  0.68 us (2%)
    ppermute x11, starting transfers between devices, swap_by_core(): return lax.ppermute(x, ('blk', 'feat'), pairs)  16.1 us
    ppermute x11, waiting for transfers between devices, swap_by_core(): return lax.ppermute(x, ('blk', 'feat'), pairs)  5.47 us
    ppermute x6, waiting for transfers between devices, swap(): lax.ppermute(x, 'feat', [(f, f ^ bits) for f in range(lax.axis_size('feat...  4.75 us
    ppermute x6, starting transfers between devices, swap(): lax.ppermute(x, 'feat', [(f, f ^ bits) for f in range(lax.axis_size('feat...  2.07 us
    pallas_call x1, Pallas kernels, on_device(): pl.pallas_call(prepare_kernel, out_shape=[pltpu.VMEM(points.shape, BF16),...  1.41 us
    pallas_call x3, Pallas kernels, call(): pl.pallas_call(kernel, out_shape=[pltpu.VMEM(*o) for o in outs], in_specs...  0.93 us
    unnamed x3, local copies, waits for them, and re-layouts  0.68 us
  transfers between devices with their start and end apart: 17, of which 12 were waited for; matrix products, arithmetic and copies ran while one was open for 0% of the time, Pallas kernels for 4%

profile of v6, /device:TPU:0, one launch (start us, length us, event | category | flops | bytes accessed | tf_op | source)
XLA Modules:
  0.0 31.5 jit_solution(8916472406621398524)
XLA Ops:
  0.0 2.9 %collective-permute-start.1 = (bf16[16,2048]{1,0:T(8,128)(2,1)}, bf16[16,2048]{1,0:T(8,128)(2,1)S(1)}, u32[]{:S(2)}, u32[]{:S(2)}) collective-permute-start(bf16[16,2048]{1,0:T(8,128)(2,1)} %centers_ref.1), channel_id=1, source_target_pairs={{0,4},{1,9},{2,6},{3,11},{4,0},{5,13},{6,2},{7,15},{8,12},{9,1},{1... | collective-permute-start | bytes 196616 | tf_op jit(solution)/shard_map/ppermute | solution.py:100
  2.9 3.6 %collective-permute-start.4 = (bf16[16,2048]{1,0:T(8,128)(2,1)}, bf16[16,2048]{1,0:T(8,128)(2,1)S(1)}, u32[]{:S(2)}, u32[]{:S(2)}) collective-permute-start(bf16[16,2048]{1,0:T(8,128)(2,1)} %centers_ref.1), channel_id=1, source_target_pairs={{0,24},{1,25},{2,26},{3,27},{4,28},{5,29},{6,30},{7,31},{8,16},{9,... | collective-permute-start | bytes 196616 | tf_op jit(solution)/shard_map/ppermute | solution.py:100
  6.5 0.8 %collective-permute-start.2 = (bf16[16,2048]{1,0:T(8,128)(2,1)}, bf16[16,2048]{1,0:T(8,128)(2,1)S(1)}, u32[]{:S(2)}, u32[]{:S(2)}) collective-permute-start(bf16[16,2048]{1,0:T(8,128)(2,1)} %centers_ref.1), channel_id=1, source_target_pairs={{0,16},{1,5},{2,18},{3,7},{4,20},{5,1},{6,22},{7,3},{8,24},{9,13},... | collective-permute-start | bytes 196616 | tf_op jit(solution)/shard_map/ppermute | solution.py:100
  7.3 1.2 %collective-permute-start.3 = (bf16[16,2048]{1,0:T(8,128)(2,1)S(1)}, bf16[16,2048]{1,0:T(8,128)(2,1)S(1)}, u32[]{:S(2)}, u32[]{:S(2)}) collective-permute-start(bf16[16,2048]{1,0:T(8,128)(2,1)S(1)} %collective-permute-done.1.r_4_), channel_id=1, source_target_pairs={{0,8},{1,5},{2,10},{3,7},{4,12},{5,1},{6,14},{7,3},{8,0},{9,13},{1... | collective-permute-start | bytes 196616 | tf_op jit(solution)/shard_map/ppermute | solution.py:100
  8.6 2.9 %collective-permute-start.5 = (bf16[16,2048]{1,0:T(8,128)(2,1)S(1)}, bf16[16,2048]{1,0:T(8,128)(2,1)S(1)}, u32[]{:S(2)}, u32[]{:S(2)}) collective-permute-start(bf16[16,2048]{1,0:T(8,128)(2,1)S(1)} %collective-permute-done.1.r_4_), channel_id=1, source_target_pairs={{0,16},{1,25},{2,18},{3,27},{4,20},{5,29},{6,22},{7,31},{8,24},{9,... | collective-permute-start | bytes 196616 | tf_op jit(solution)/shard_map/ppermute | solution.py:100
  11.5 0.5 %collective-permute-start.6 = (bf16[16,2048]{1,0:T(8,128)(2,1)S(1)}, bf16[16,2048]{1,0:T(8,128)(2,1)S(1)}, u32[]{:S(2)}, u32[]{:S(2)}) collective-permute-start(bf16[16,2048]{1,0:T(8,128)(2,1)S(1)} %collective-permute-done.4.r_7_), channel_id=1, source_target_pairs={{0,4},{1,5},{2,6},{3,7},{4,0},{5,1},{6,2},{7,3},{8,12},{9,13},{10,... | collective-permute-start | bytes 196616 | tf_op jit(solution)/shard_map/ppermute | solution.py:100
  12.0 1.4 %shard_map.37 = (bf16[128,2048]{1,0:T(8,128)(2,1)S(1)}, bf16[16,2048]{1,0:T(8,128)(2,1)S(1)}, f32[1,128]{1,0:T(1,128)S(1)}) custom-call(bf16[128,2048]{1,0:T(8,128)(2,1)} %points_ref.1, bf16[16,2048]{1,0:T(8,128)(2,1)} %centers_ref.1), custom_call_target="tpu_custom_call" | custom-call | flops 524288 | bytes 524288 | tf_op jit(solution)/shard_map/pallas_call | solution.py:118
  13.6 1.4 %collective-permute-done.5.r_8_ = bf16[16,2048]{1,0:T(8,128)(2,1)S(1)} collective-permute-done((bf16[16,2048]{1,0:T(8,128)(2,1)S(1)}, bf16[16,2048]{1,0:T(8,128)(2,1)S(1)}, u32[]{:S(2)}, u32[]{:S(2)}) %collective-permute-start.5) | collective-permute-done | bytes 65568 | tf_op jit(solution)/shard_map/ppermute | solution.py:100
  15.0 0.7 %collective-permute-done.6.r_9_ = bf16[16,2048]{1,0:T(8,128)(2,1)S(1)} collective-permute-done((bf16[16,2048]{1,0:T(8,128)(2,1)S(1)}, bf16[16,2048]{1,0:T(8,128)(2,1)S(1)}, u32[]{:S(2)}, u32[]{:S(2)}) %collective-permute-start.6) | collective-permute-done | bytes 65568 | tf_op jit(solution)/shard_map/ppermute | solution.py:100
  15.8 0.3 %shard_map.38 = f32[128,128]{1,0:T(8,128)S(1)} custom-call(bf16[128,2048]{1,0:T(8,128)(2,1)S(1)} %get-tuple-element.8.r_0_, f32[1,128]{1,0:T(1,128)S(1)} %get-tuple-element.9.r_1_, bf16[16,2048]{1,0:T(8,128)(2,1)S(1)} %get-tuple-element.10.r_2_, bf16[16,2048]{1,0:T(8,128)(2,1)S(1)} %collective-permute-done.r_3_, ...), custom_call_target="tpu_custom_call" | custom-call | tf_op jit(solution)/shard_map/pallas_call | solution.py:23
  16.2 1.2 %collective-permute-done.7 = f32[128,128]{1,0:T(8,128)S(1)} collective-permute-done((f32[128,128]{1,0:T(8,128)S(1)}, f32[128,128]{1,0:T(8,128)S(1)}, u32[]{:S(2)}, u32[]{:S(2)}) %collective-permute-start.7) | collective-permute-done | bytes 65568 | tf_op jit(solution)/shard_map/ppermute | solution.py:90
  17.5 1.6 %collective-permute-start.8 = (f32[128,128]{1,0:T(8,128)S(1)}, f32[128,128]{1,0:T(8,128)S(1)}, u32[]{:S(2)}, u32[]{:S(2)}) collective-permute-start(f32[128,128]{1,0:T(8,128)S(1)} %add.3.r_0_), channel_id=1, source_target_pairs={{0,2},{1,3},{2,0},{3,1},{4,6},{5,7},{6,4},{7,5},{8,10},{9,11},{10,... | collective-permute-start | bytes 196616 | tf_op jit(solution)/shard_map/ppermute | solution.py:90
  19.1 1.2 %collective-permute-done.9.r_3_ = bf16[16,256]{1,0:T(8,128)(2,1)S(1)} collective-permute-done((bf16[16,256]{1,0:T(8,128)(2,1)S(1)}, bf16[16,256]{1,0:T(8,128)(2,1)S(1)}, u32[]{:S(2)}, u32[]{:S(2)}) %collective-permute-start.9) | collective-permute-done | bytes 8224 | tf_op jit(solution)/shard_map/ppermute | solution.py:90
  20.2 1.6 %collective-permute-done.8.r_1_ = f32[128,128]{1,0:T(8,128)S(1)} collective-permute-done((f32[128,128]{1,0:T(8,128)S(1)}, f32[128,128]{1,0:T(8,128)S(1)}, u32[]{:S(2)}, u32[]{:S(2)}) %collective-permute-start.8) | collective-permute-done | bytes 65568 | tf_op jit(solution)/shard_map/ppermute | solution.py:90
  21.8 1.0 %collective-permute-start.10 = (bf16[192,128]{1,0:T(8,128)(2,1)S(1)}, bf16[192,128]{1,0:T(8,128)(2,1)S(1)}, u32[]{:S(2)}, u32[]{:S(2)}) collective-permute-start(bf16[192,128]{1,0:T(8,128)(2,1)S(1)} %shard_map.39.r_0_), channel_id=1, source_target_pairs={{0,16},{1,21},{2,18},{3,23},{4,20},{5,17},{6,22},{7,19},{8,24},{9,... | collective-permute-start | bytes 147464 | tf_op jit(solution)/shard_map/ppermute | solution.py:100
  22.8 1.5 %collective-permute-start.11 = (bf16[192,128]{1,0:T(8,128)(2,1)S(1)}, bf16[192,128]{1,0:T(8,128)(2,1)S(1)}, u32[]{:S(2)}, u32[]{:S(2)}) collective-permute-start(bf16[192,128]{1,0:T(8,128)(2,1)S(1)} %shard_map.39.r_0_), channel_id=1, source_target_pairs={{0,24},{1,29},{2,26},{3,31},{4,28},{5,25},{6,30},{7,27},{8,16},{9,... | collective-permute-start | bytes 147464 | tf_op jit(solution)/shard_map/ppermute | solution.py:100
  24.2 1.1 %collective-permute-start.12 = (bf16[192,128]{1,0:T(8,128)(2,1)S(1)}, bf16[192,128]{1,0:T(8,128)(2,1)S(1)}, u32[]{:S(2)}, u32[]{:S(2)}) collective-permute-start(bf16[192,128]{1,0:T(8,128)(2,1)S(1)} %shard_map.39.r_0_), channel_id=1, source_target_pairs={{0,8},{1,13},{2,10},{3,15},{4,12},{5,9},{6,14},{7,11},{8,0},{9,5},... | collective-permute-start | bytes 147464 | tf_op jit(solution)/shard_map/ppermute | solution.py:100
  25.4 0.5 %collective-permute-start.13 = (bf16[192,128]{1,0:T(8,128)(2,1)S(1)}, bf16[192,128]{1,0:T(8,128)(2,1)S(1)}, u32[]{:S(2)}, u32[]{:S(2)}) collective-permute-start(bf16[192,128]{1,0:T(8,128)(2,1)S(1)} %shard_map.39.r_0_), channel_id=1, source_target_pairs={{0,4},{1,5},{2,6},{3,7},{4,0},{5,1},{6,2},{7,3},{8,12},{9,13},{10,... | collective-permute-start | bytes 147464 | tf_op jit(solution)/shard_map/ppermute | solution.py:100
  25.9 1.7 %collective-permute-done.10.r_1_ = bf16[192,128]{1,0:T(8,128)(2,1)S(1)} collective-permute-done((bf16[192,128]{1,0:T(8,128)(2,1)S(1)}, bf16[192,128]{1,0:T(8,128)(2,1)S(1)}, u32[]{:S(2)}, u32[]{:S(2)}) %collective-permute-start.10) | collective-permute-done | bytes 49184 | tf_op jit(solution)/shard_map/ppermute | solution.py:100
  27.6 1.2 %collective-permute-done.11.r_2_ = bf16[192,128]{1,0:T(8,128)(2,1)S(1)} collective-permute-done((bf16[192,128]{1,0:T(8,128)(2,1)S(1)}, bf16[192,128]{1,0:T(8,128)(2,1)S(1)}, u32[]{:S(2)}, u32[]{:S(2)}) %collective-permute-start.11) | collective-permute-done | bytes 49184 | tf_op jit(solution)/shard_map/ppermute | solution.py:100
  29.0 0.4 %collective-permute-start.16 = (bf16[192,128]{1,0:T(8,128)(2,1)S(1)}, bf16[192,128]{1,0:T(8,128)(2,1)S(1)}, u32[]{:S(2)}, u32[]{:S(2)}) collective-permute-start(bf16[192,128]{1,0:T(8,128)(2,1)S(1)} %collective-permute-done.12.r_3_), channel_id=1, source_target_pairs={{0,1},{1,0},{2,3},{3,2},{4,5},{5,4},{6,7},{7,6},{8,9},{9,8},{10,11... | collective-permute-start | bytes 147464 | tf_op jit(solution)/shard_map/ppermute | solution.py:90
  29.5 0.6 %collective-permute-done.15.r_6_ = bf16[192,128]{1,0:T(8,128)(2,1)S(1)} collective-permute-done((bf16[192,128]{1,0:T(8,128)(2,1)S(1)}, bf16[192,128]{1,0:T(8,128)(2,1)S(1)}, u32[]{:S(2)}, u32[]{:S(2)}) %collective-permute-start.15) | collective-permute-done | bytes 49184 | tf_op jit(solution)/shard_map/ppermute | solution.py:90
  30.2 0.6 %shard_map.40 = f32[16,256]{1,0:T(8,128)S(1)} custom-call(bf16[192,128]{1,0:T(8,128)(2,1)S(1)} %shard_map.39.r_0_, bf16[192,128]{1,0:T(8,128)(2,1)S(1)} %collective-permute-done.10.r_1_, bf16[192,128]{1,0:T(8,128)(2,1)S(1)} %collective-permute-done.11.r_2_, bf16[192,128]{1,0:T(8,128)(2,1)S(1)} %collective-permute-done.12.r_3_, ...), custom_call_target="tpu_custom_call" | custom-call | tf_op jit(solution)/shard_map/pallas_call | solution.py:23
  30.8 0.7 %copy.4 = f32[16,256]{1,0:T(8,128)} copy(f32[16,256]{1,0:T(8,128)S(1)} %shard_map.40) | data formatting | bytes 32768
  (18 shorter events, 0.7 us)
Async XLA Ops:
  0.0 7.3 %collective-permute-start.1 = (bf16[16,2048]{1,0:T(8,128)(2,1)}, bf16[16,2048]{1,0:T(8,128)(2,1)S(1)}, u32[]{:S(2)}, u32[]{:S(2)}) collective-permute-start(bf16[16,2048]{1,0:T(8,128)(2,1)} %centers_ref.1), channel_id=1, source_target_pairs={{0,4},{1,9},{2,6},{3,11},{4,0},{5,13},{6,2},{7,15},{8,12},{9,1},{1... | collective-permute-start | bytes 196616 | tf_op jit(solution)/shard_map/ppermute | solution.py:100
  2.9 8.6 %collective-permute-start.4 = (bf16[16,2048]{1,0:T(8,128)(2,1)}, bf16[16,2048]{1,0:T(8,128)(2,1)S(1)}, u32[]{:S(2)}, u32[]{:S(2)}) collective-permute-start(bf16[16,2048]{1,0:T(8,128)(2,1)} %centers_ref.1), channel_id=1, source_target_pairs={{0,24},{1,25},{2,26},{3,27},{4,28},{5,29},{6,30},{7,31},{8,16},{9,... | collective-permute-start | bytes 196616 | tf_op jit(solution)/shard_map/ppermute | solution.py:100
  6.5 6.9 %collective-permute-start = (bf16[16,2048]{1,0:T(8,128)(2,1)}, bf16[16,2048]{1,0:T(8,128)(2,1)S(1)}, u32[]{:S(2)}, u32[]{:S(2)}) collective-permute-start(bf16[16,2048]{1,0:T(8,128)(2,1)} %centers_ref.1), channel_id=1, source_target_pairs={{0,8},{1,21},{2,10},{3,23},{4,12},{5,17},{6,14},{7,19},{8,0},{9,29... | collective-permute-start | bytes 196616 | tf_op jit(solution)/shard_map/ppermute | solution.py:100
  6.5 7.1 %collective-permute-start.2 = (bf16[16,2048]{1,0:T(8,128)(2,1)}, bf16[16,2048]{1,0:T(8,128)(2,1)S(1)}, u32[]{:S(2)}, u32[]{:S(2)}) collective-permute-start(bf16[16,2048]{1,0:T(8,128)(2,1)} %centers_ref.1), channel_id=1, source_target_pairs={{0,16},{1,5},{2,18},{3,7},{4,20},{5,1},{6,22},{7,3},{8,24},{9,13},... | collective-permute-start | bytes 196616 | tf_op jit(solution)/shard_map/ppermute | solution.py:100
  7.3 6.3 %collective-permute-start.3 = (bf16[16,2048]{1,0:T(8,128)(2,1)S(1)}, bf16[16,2048]{1,0:T(8,128)(2,1)S(1)}, u32[]{:S(2)}, u32[]{:S(2)}) collective-permute-start(bf16[16,2048]{1,0:T(8,128)(2,1)S(1)} %collective-permute-done.1.r_4_), channel_id=1, source_target_pairs={{0,8},{1,5},{2,10},{3,7},{4,12},{5,1},{6,14},{7,3},{8,0},{9,13},{1... | collective-permute-start | bytes 196616 | tf_op jit(solution)/shard_map/ppermute | solution.py:100
  8.6 6.5 %collective-permute-start.5 = (bf16[16,2048]{1,0:T(8,128)(2,1)S(1)}, bf16[16,2048]{1,0:T(8,128)(2,1)S(1)}, u32[]{:S(2)}, u32[]{:S(2)}) collective-permute-start(bf16[16,2048]{1,0:T(8,128)(2,1)S(1)} %collective-permute-done.1.r_4_), channel_id=1, source_target_pairs={{0,16},{1,25},{2,18},{3,27},{4,20},{5,29},{6,22},{7,31},{8,24},{9,... | collective-permute-start | bytes 196616 | tf_op jit(solution)/shard_map/ppermute | solution.py:100
  11.5 4.3 %collective-permute-start.6 = (bf16[16,2048]{1,0:T(8,128)(2,1)S(1)}, bf16[16,2048]{1,0:T(8,128)(2,1)S(1)}, u32[]{:S(2)}, u32[]{:S(2)}) collective-permute-start(bf16[16,2048]{1,0:T(8,128)(2,1)S(1)} %collective-permute-done.4.r_7_), channel_id=1, source_target_pairs={{0,4},{1,5},{2,6},{3,7},{4,0},{5,1},{6,2},{7,3},{8,12},{9,13},{10,... | collective-permute-start | bytes 196616 | tf_op jit(solution)/shard_map/ppermute | solution.py:100
  16.1 3.0 %copy-start = (bf16[16,256]{1,0:T(8,128)(2,1)S(1)}, bf16[16,256]{1,0:T(8,128)(2,1)}, u32[]{:S(2)}) copy-start(bf16[16,256]{1,0:T(8,128)(2,1)} %r_2_.1) | copy-start | bytes 24580
  16.1 1.3 %collective-permute-start.7 = (f32[128,128]{1,0:T(8,128)S(1)}, f32[128,128]{1,0:T(8,128)S(1)}, u32[]{:S(2)}, u32[]{:S(2)}) collective-permute-start(f32[128,128]{1,0:T(8,128)S(1)} %shard_map.38), channel_id=1, source_target_pairs={{0,1},{1,0},{2,3},{3,2},{4,5},{5,4},{6,7},{7,6},{8,9},{9,8},{10,11... | collective-permute-start | bytes 196616 | tf_op jit(solution)/shard_map/ppermute | solution.py:90
  17.5 4.3 %collective-permute-start.8 = (f32[128,128]{1,0:T(8,128)S(1)}, f32[128,128]{1,0:T(8,128)S(1)}, u32[]{:S(2)}, u32[]{:S(2)}) collective-permute-start(f32[128,128]{1,0:T(8,128)S(1)} %add.3.r_0_), channel_id=1, source_target_pairs={{0,2},{1,3},{2,0},{3,1},{4,6},{5,7},{6,4},{7,5},{8,10},{9,11},{10,... | collective-permute-start | bytes 196616 | tf_op jit(solution)/shard_map/ppermute | solution.py:90
  19.1 1.2 %collective-permute-start.9 = (bf16[16,256]{1,0:T(8,128)(2,1)S(1)}, bf16[16,256]{1,0:T(8,128)(2,1)S(1)}, u32[]{:S(2)}, u32[]{:S(2)}) collective-permute-start(bf16[16,256]{1,0:T(8,128)(2,1)S(1)} %copy-done), channel_id=1, source_target_pairs={{0,1},{1,0},{2,3},{3,2},{4,5},{5,4},{6,7},{7,6},{8,9},{9,8},{10,11... | collective-permute-start | bytes 24584 | tf_op jit(solution)/shard_map/ppermute | solution.py:90
  21.8 5.8 %collective-permute-start.10 = (bf16[192,128]{1,0:T(8,128)(2,1)S(1)}, bf16[192,128]{1,0:T(8,128)(2,1)S(1)}, u32[]{:S(2)}, u32[]{:S(2)}) collective-permute-start(bf16[192,128]{1,0:T(8,128)(2,1)S(1)} %shard_map.39.r_0_), channel_id=1, source_target_pairs={{0,16},{1,21},{2,18},{3,23},{4,20},{5,17},{6,22},{7,19},{8,24},{9,... | collective-permute-start | bytes 147464 | tf_op jit(solution)/shard_map/ppermute | solution.py:100
  22.8 6.1 %collective-permute-start.11 = (bf16[192,128]{1,0:T(8,128)(2,1)S(1)}, bf16[192,128]{1,0:T(8,128)(2,1)S(1)}, u32[]{:S(2)}, u32[]{:S(2)}) collective-permute-start(bf16[192,128]{1,0:T(8,128)(2,1)S(1)} %shard_map.39.r_0_), channel_id=1, source_target_pairs={{0,24},{1,29},{2,26},{3,31},{4,28},{5,25},{6,30},{7,27},{8,16},{9,... | collective-permute-start | bytes 147464 | tf_op jit(solution)/shard_map/ppermute | solution.py:100
  24.2 4.7 %collective-permute-start.12 = (bf16[192,128]{1,0:T(8,128)(2,1)S(1)}, bf16[192,128]{1,0:T(8,128)(2,1)S(1)}, u32[]{:S(2)}, u32[]{:S(2)}) collective-permute-start(bf16[192,128]{1,0:T(8,128)(2,1)S(1)} %shard_map.39.r_0_), channel_id=1, source_target_pairs={{0,8},{1,13},{2,10},{3,15},{4,12},{5,9},{6,14},{7,11},{8,0},{9,5},... | collective-permute-start | bytes 147464 | tf_op jit(solution)/shard_map/ppermute | solution.py:100
  25.4 4.1 %collective-permute-start.13 = (bf16[192,128]{1,0:T(8,128)(2,1)S(1)}, bf16[192,128]{1,0:T(8,128)(2,1)S(1)}, u32[]{:S(2)}, u32[]{:S(2)}) collective-permute-start(bf16[192,128]{1,0:T(8,128)(2,1)S(1)} %shard_map.39.r_0_), channel_id=1, source_target_pairs={{0,4},{1,5},{2,6},{3,7},{4,0},{5,1},{6,2},{7,3},{8,12},{9,13},{10,... | collective-permute-start | bytes 147464 | tf_op jit(solution)/shard_map/ppermute | solution.py:100
  27.6 1.8 %collective-permute-start.14 = (bf16[192,128]{1,0:T(8,128)(2,1)S(1)}, bf16[192,128]{1,0:T(8,128)(2,1)S(1)}, u32[]{:S(2)}, u32[]{:S(2)}) collective-permute-start(bf16[192,128]{1,0:T(8,128)(2,1)S(1)} %collective-permute-done.10.r_1_), channel_id=1, source_target_pairs={{0,1},{1,0},{2,3},{3,2},{4,5},{5,4},{6,7},{7,6},{8,9},{9,8},{10,11... | collective-permute-start | bytes 147464 | tf_op jit(solution)/shard_map/ppermute | solution.py:90
  28.8 1.2 %collective-permute-start.15 = (bf16[192,128]{1,0:T(8,128)(2,1)S(1)}, bf16[192,128]{1,0:T(8,128)(2,1)S(1)}, u32[]{:S(2)}, u32[]{:S(2)}) collective-permute-start(bf16[192,128]{1,0:T(8,128)(2,1)S(1)} %collective-permute-done.11.r_2_), channel_id=1, source_target_pairs={{0,1},{1,0},{2,3},{3,2},{4,5},{5,4},{6,7},{7,6},{8,9},{9,8},{10,11... | collective-permute-start | bytes 147464 | tf_op jit(solution)/shard_map/ppermute | solution.py:90
  29.0 1.3 %collective-permute-start.16 = (bf16[192,128]{1,0:T(8,128)(2,1)S(1)}, bf16[192,128]{1,0:T(8,128)(2,1)S(1)}, u32[]{:S(2)}, u32[]{:S(2)}) collective-permute-start(bf16[192,128]{1,0:T(8,128)(2,1)S(1)} %collective-permute-done.12.r_3_), channel_id=1, source_target_pairs={{0,1},{1,0},{2,3},{3,2},{4,5},{5,4},{6,7},{7,6},{8,9},{9,8},{10,11... | collective-permute-start | bytes 147464 | tf_op jit(solution)/shard_map/ppermute | solution.py:90

commit v7 on v6

--- a/solution.py
+++ b/solution.py
@@ -12,6 +12,7 @@
 VMEM = pl.BlockSpec(memory_space=pltpu.VMEM)
 
 GATHER = ((0, 2, 5), (0, 1, 2), (0, 4, 1), (2, 2, 1), (0, 6, 6), (2, 4, 6), (5, 1, 1))
+LATE = (6, 7)
 SPREAD = ((0, 4, 5), (0, 6, 7), (0, 2, 3), (0, 1, 1))
 
 
@@ -42,17 +43,26 @@
     square_out[...] = jnp.sum((wide * wide).T, axis=0, keepdims=True)
 
 
-def dist_kernel(sources, points_ref, square_ref, *refs):
-    tiles, (part_ref, centers) = refs[: len(sources)], refs[len(sources) :]
-    rows = tiles[0].shape[0]
-    for bits, tile in zip(sources, tiles):
-        centers[pl.ds(place(bits, rows), rows), :] = tile[...]
-    cross = lax.dot_general(
-        centers[...], points_ref[...], (((1,), (1,)), ((), ())), preferred_element_type=F32
-    )
-    wide = centers[...].astype(F32)
-    center_sq = jnp.sum(wide * wide, axis=1, keepdims=True)
-    part_ref[...] = square_ref[...] + center_sq - 2.0 * cross
+def part_of_dist(centers, points, square):
+    cross = lax.dot_general(centers, points, (((1,), (1,)), ((), ())), preferred_element_type=F32)
+    wide = centers.astype(F32)
+    return square + jnp.sum(wide * wide, axis=1, keepdims=True) - 2.0 * cross
+
+
+def early_kernel(points_ref, square_ref, *refs):
+    tiles, out_ref = refs[:-1], refs[-1]
+    centers = jnp.concatenate([tile[...] for tile in tiles], axis=0)
+    out_ref[...] = part_of_dist(centers, points_ref[...], square_ref[...])
+
+
+def dist_kernel(early, late, rows, points_ref, square_ref, early_ref, *refs):
+    tiles, part_ref = refs[:-1], refs[-1]
+    for i, bits in enumerate(early):
+        part_ref[pl.ds(place(bits, rows), rows), :] = early_ref[i * rows : (i + 1) * rows, :]
+    centers = jnp.concatenate([tile[...] for tile in tiles], axis=0)
+    part = part_of_dist(centers, points_ref[...], square_ref[...])
+    for i, bits in enumerate(late):
+        part_ref[pl.ds(place(bits, rows), rows), :] = part[i * rows : (i + 1) * rows]
 
 
 def send_kernel(features, a_ref, b_ref, coefs_ref, others_ref, out_ref):
@@ -123,13 +133,21 @@
         cost_estimate=pl.CostEstimate(flops=2 * points.size, bytes_accessed=2 * points.size, transcendentals=0),
     )(points, centers)
     others = swap(coefs, 1)
+    first = [i for i in range(len(tiles)) if i not in LATE]
+    (early,) = call(
+        early_kernel,
+        [((rows * len(first), local_points), F32)],
+        points,
+        square,
+        *[tiles[i] for i in first],
+    )
     (part,) = call(
-        lambda *r: dist_kernel(sources, *r),
+        lambda *r: dist_kernel([sources[i] for i in first], [sources[i] for i in LATE], rows, *r),
         [((all_rows, local_points), F32)],
         points,
         square,
-        *tiles,
-        scratch=[pltpu.VMEM((all_rows, points.shape[1]), BF16)],
+        early,
+        *[tiles[i] for i in LATE],
     )
     bits = 1
     while 2 * bits < feats:

time: 31.6 us -> 31.6 us (level)
    pallas_call x3 -> x4, Pallas kernels: 0.93 us -> 1.16 us  [call(): pl.pallas_call(kernel, out_shape=[pltpu.VMEM(*o) for o in outs], in_specs...]
  transfers between devices with their start and end apart: 17 -> 17, of which waited for: 12 -> 12; matrix products, arithmetic and copies ran while one was open for 0% -> 0% of each run, Pallas kernels for 4% -> 5%
where the time goes in v7:
time: 31.6 us; the launch traced here: 31.4 us
  starting transfers between devices  18.2 us (58%)
  waiting for transfers between devices  9.92 us (31%)
  Pallas kernels  2.57 us (8%)
  local copies, waits for them, and re-layouts  0.69 us (2%)
    ppermute x11, starting transfers between devices, swap_by_core(): return lax.ppermute(x, ('blk', 'feat'), pairs)  16.1 us
    ppermute x11, waiting for transfers between devices, swap_by_core(): return lax.ppermute(x, ('blk', 'feat'), pairs)  5.17 us
    ppermute x6, waiting for transfers between devices, swap(): lax.ppermute(x, 'feat', [(f, f ^ bits) for f in range(lax.axis_size('feat...  4.75 us
    ppermute x6, starting transfers between devices, swap(): lax.ppermute(x, 'feat', [(f, f ^ bits) for f in range(lax.axis_size('feat...  2.05 us
    pallas_call x1, Pallas kernels, on_device(): pl.pallas_call(prepare_kernel, out_shape=[pltpu.VMEM(points.shape, BF16),...  1.41 us
    pallas_call x4, Pallas kernels, call(): pl.pallas_call(kernel, out_shape=[pltpu.VMEM(*o) for o in outs], in_specs...  1.16 us
    unnamed x3, local copies, waits for them, and re-layouts  0.69 us
  transfers between devices with their start and end apart: 17, of which 12 were waited for; matrix products, arithmetic and copies ran while one was open for 0% of the time, Pallas kernels for 5%

profile of v7, /device:TPU:0, one launch (start us, length us, event | category | flops | bytes accessed | tf_op | source)
XLA Modules:
  0.0 31.4 jit_solution(14284248201198561495)
XLA Ops:
  0.0 2.9 %collective-permute-start.1 = (bf16[16,2048]{1,0:T(8,128)(2,1)}, bf16[16,2048]{1,0:T(8,128)(2,1)S(1)}, u32[]{:S(2)}, u32[]{:S(2)}) collective-permute-start(bf16[16,2048]{1,0:T(8,128)(2,1)} %centers_ref.1), channel_id=1, source_target_pairs={{0,4},{1,9},{2,6},{3,11},{4,0},{5,13},{6,2},{7,15},{8,12},{9,1},{1... | collective-permute-start | bytes 196616 | tf_op jit(solution)/shard_map/ppermute | solution.py:110
  2.9 3.6 %collective-permute-start.4 = (bf16[16,2048]{1,0:T(8,128)(2,1)}, bf16[16,2048]{1,0:T(8,128)(2,1)S(1)}, u32[]{:S(2)}, u32[]{:S(2)}) collective-permute-start(bf16[16,2048]{1,0:T(8,128)(2,1)} %centers_ref.1), channel_id=1, source_target_pairs={{0,24},{1,25},{2,26},{3,27},{4,28},{5,29},{6,30},{7,31},{8,16},{9,... | collective-permute-start | bytes 196616 | tf_op jit(solution)/shard_map/ppermute | solution.py:110
  6.5 0.8 %collective-permute-start.2 = (bf16[16,2048]{1,0:T(8,128)(2,1)}, bf16[16,2048]{1,0:T(8,128)(2,1)S(1)}, u32[]{:S(2)}, u32[]{:S(2)}) collective-permute-start(bf16[16,2048]{1,0:T(8,128)(2,1)} %centers_ref.1), channel_id=1, source_target_pairs={{0,16},{1,5},{2,18},{3,7},{4,20},{5,1},{6,22},{7,3},{8,24},{9,13},... | collective-permute-start | bytes 196616 | tf_op jit(solution)/shard_map/ppermute | solution.py:110
  7.3 1.2 %collective-permute-start.3 = (bf16[16,2048]{1,0:T(8,128)(2,1)S(1)}, bf16[16,2048]{1,0:T(8,128)(2,1)S(1)}, u32[]{:S(2)}, u32[]{:S(2)}) collective-permute-start(bf16[16,2048]{1,0:T(8,128)(2,1)S(1)} %collective-permute-done.1.refs_2_), channel_id=1, source_target_pairs={{0,8},{1,5},{2,10},{3,7},{4,12},{5,1},{6,14},{7,3},{8,0},{9,13},{1... | collective-permute-start | bytes 196616 | tf_op jit(solution)/shard_map/ppermute | solution.py:110
  8.6 2.9 %collective-permute-start.5 = (bf16[16,2048]{1,0:T(8,128)(2,1)S(1)}, bf16[16,2048]{1,0:T(8,128)(2,1)S(1)}, u32[]{:S(2)}, u32[]{:S(2)}) collective-permute-start(bf16[16,2048]{1,0:T(8,128)(2,1)S(1)} %collective-permute-done.1.refs_2_), channel_id=1, source_target_pairs={{0,16},{1,25},{2,18},{3,27},{4,20},{5,29},{6,22},{7,31},{8,24},{9,... | collective-permute-start | bytes 196616 | tf_op jit(solution)/shard_map/ppermute | solution.py:110
  11.5 0.5 %collective-permute-start.6 = (bf16[16,2048]{1,0:T(8,128)(2,1)S(1)}, bf16[16,2048]{1,0:T(8,128)(2,1)S(1)}, u32[]{:S(2)}, u32[]{:S(2)}) collective-permute-start(bf16[16,2048]{1,0:T(8,128)(2,1)S(1)} %collective-permute-done.4.refs_5_), channel_id=1, source_target_pairs={{0,4},{1,5},{2,6},{3,7},{4,0},{5,1},{6,2},{7,3},{8,12},{9,13},{10,... | collective-permute-start | bytes 196616 | tf_op jit(solution)/shard_map/ppermute | solution.py:110
  12.0 1.4 %shard_map.37 = (bf16[128,2048]{1,0:T(8,128)(2,1)S(1)}, bf16[16,2048]{1,0:T(8,128)(2,1)S(1)}, f32[1,128]{1,0:T(1,128)S(1)}) custom-call(bf16[128,2048]{1,0:T(8,128)(2,1)} %points_ref.1, bf16[16,2048]{1,0:T(8,128)(2,1)} %centers_ref.1), custom_call_target="tpu_custom_call" | custom-call | flops 524288 | bytes 524288 | tf_op jit(solution)/shard_map/pallas_call | solution.py:128
  13.6 0.3 shard_map.38.r_2_
  14.0 1.1 %collective-permute-done.5.r_3_ = bf16[16,2048]{1,0:T(8,128)(2,1)S(1)} collective-permute-done((bf16[16,2048]{1,0:T(8,128)(2,1)S(1)}, bf16[16,2048]{1,0:T(8,128)(2,1)S(1)}, u32[]{:S(2)}, u32[]{:S(2)}) %collective-permute-start.5) | collective-permute-done | bytes 65568 | tf_op jit(solution)/shard_map/ppermute | solution.py:110
  15.0 0.7 %collective-permute-done.6.r_4_ = bf16[16,2048]{1,0:T(8,128)(2,1)S(1)} collective-permute-done((bf16[16,2048]{1,0:T(8,128)(2,1)S(1)}, bf16[16,2048]{1,0:T(8,128)(2,1)S(1)}, u32[]{:S(2)}, u32[]{:S(2)}) %collective-permute-start.6) | collective-permute-done | bytes 65568 | tf_op jit(solution)/shard_map/ppermute | solution.py:110
  16.1 1.2 %collective-permute-done.7 = f32[128,128]{1,0:T(8,128)S(1)} collective-permute-done((f32[128,128]{1,0:T(8,128)S(1)}, f32[128,128]{1,0:T(8,128)S(1)}, u32[]{:S(2)}, u32[]{:S(2)}) %collective-permute-start.7) | collective-permute-done | bytes 65568 | tf_op jit(solution)/shard_map/ppermute | solution.py:100
  17.4 1.6 %collective-permute-start.8 = (f32[128,128]{1,0:T(8,128)S(1)}, f32[128,128]{1,0:T(8,128)S(1)}, u32[]{:S(2)}, u32[]{:S(2)}) collective-permute-start(f32[128,128]{1,0:T(8,128)S(1)} %add.3.r_0_), channel_id=1, source_target_pairs={{0,2},{1,3},{2,0},{3,1},{4,6},{5,7},{6,4},{7,5},{8,10},{9,11},{10,... | collective-permute-start | bytes 196616 | tf_op jit(solution)/shard_map/ppermute | solution.py:100
  19.0 1.2 %collective-permute-done.9.r_3_ = bf16[16,256]{1,0:T(8,128)(2,1)S(1)} collective-permute-done((bf16[16,256]{1,0:T(8,128)(2,1)S(1)}, bf16[16,256]{1,0:T(8,128)(2,1)S(1)}, u32[]{:S(2)}, u32[]{:S(2)}) %collective-permute-start.9) | collective-permute-done | bytes 8224 | tf_op jit(solution)/shard_map/ppermute | solution.py:100
  20.2 1.6 %collective-permute-done.8.r_1_ = f32[128,128]{1,0:T(8,128)S(1)} collective-permute-done((f32[128,128]{1,0:T(8,128)S(1)}, f32[128,128]{1,0:T(8,128)S(1)}, u32[]{:S(2)}, u32[]{:S(2)}) %collective-permute-start.8) | collective-permute-done | bytes 65568 | tf_op jit(solution)/shard_map/ppermute | solution.py:100
  21.8 1.0 %collective-permute-start.10 = (bf16[192,128]{1,0:T(8,128)(2,1)S(1)}, bf16[192,128]{1,0:T(8,128)(2,1)S(1)}, u32[]{:S(2)}, u32[]{:S(2)}) collective-permute-start(bf16[192,128]{1,0:T(8,128)(2,1)S(1)} %shard_map.40.r_0_), channel_id=1, source_target_pairs={{0,16},{1,21},{2,18},{3,23},{4,20},{5,17},{6,22},{7,19},{8,24},{9,... | collective-permute-start | bytes 147464 | tf_op jit(solution)/shard_map/ppermute | solution.py:110
  22.7 1.5 %collective-permute-start.11 = (bf16[192,128]{1,0:T(8,128)(2,1)S(1)}, bf16[192,128]{1,0:T(8,128)(2,1)S(1)}, u32[]{:S(2)}, u32[]{:S(2)}) collective-permute-start(bf16[192,128]{1,0:T(8,128)(2,1)S(1)} %shard_map.40.r_0_), channel_id=1, source_target_pairs={{0,24},{1,29},{2,26},{3,31},{4,28},{5,25},{6,30},{7,27},{8,16},{9,... | collective-permute-start | bytes 147464 | tf_op jit(solution)/shard_map/ppermute | solution.py:110
  24.2 1.1 %collective-permute-start.12 = (bf16[192,128]{1,0:T(8,128)(2,1)S(1)}, bf16[192,128]{1,0:T(8,128)(2,1)S(1)}, u32[]{:S(2)}, u32[]{:S(2)}) collective-permute-start(bf16[192,128]{1,0:T(8,128)(2,1)S(1)} %shard_map.40.r_0_), channel_id=1, source_target_pairs={{0,8},{1,13},{2,10},{3,15},{4,12},{5,9},{6,14},{7,11},{8,0},{9,5},... | collective-permute-start | bytes 147464 | tf_op jit(solution)/shard_map/ppermute | solution.py:110
  25.3 0.5 %collective-permute-start.13 = (bf16[192,128]{1,0:T(8,128)(2,1)S(1)}, bf16[192,128]{1,0:T(8,128)(2,1)S(1)}, u32[]{:S(2)}, u32[]{:S(2)}) collective-permute-start(bf16[192,128]{1,0:T(8,128)(2,1)S(1)} %shard_map.40.r_0_), channel_id=1, source_target_pairs={{0,4},{1,5},{2,6},{3,7},{4,0},{5,1},{6,2},{7,3},{8,12},{9,13},{10,... | collective-permute-start | bytes 147464 | tf_op jit(solution)/shard_map/ppermute | solution.py:110
  25.8 1.7 %collective-permute-done.10.r_1_ = bf16[192,128]{1,0:T(8,128)(2,1)S(1)} collective-permute-done((bf16[192,128]{1,0:T(8,128)(2,1)S(1)}, bf16[192,128]{1,0:T(8,128)(2,1)S(1)}, u32[]{:S(2)}, u32[]{:S(2)}) %collective-permute-start.10) | collective-permute-done | bytes 49184 | tf_op jit(solution)/shard_map/ppermute | solution.py:110
  27.6 1.2 %collective-permute-done.11.r_2_ = bf16[192,128]{1,0:T(8,128)(2,1)S(1)} collective-permute-done((bf16[192,128]{1,0:T(8,128)(2,1)S(1)}, bf16[192,128]{1,0:T(8,128)(2,1)S(1)}, u32[]{:S(2)}, u32[]{:S(2)}) %collective-permute-start.11) | collective-permute-done | bytes 49184 | tf_op jit(solution)/shard_map/ppermute | solution.py:110
  28.9 0.4 %collective-permute-start.16 = (bf16[192,128]{1,0:T(8,128)(2,1)S(1)}, bf16[192,128]{1,0:T(8,128)(2,1)S(1)}, u32[]{:S(2)}, u32[]{:S(2)}) collective-permute-start(bf16[192,128]{1,0:T(8,128)(2,1)S(1)} %collective-permute-done.12.r_3_), channel_id=1, source_target_pairs={{0,1},{1,0},{2,3},{3,2},{4,5},{5,4},{6,7},{7,6},{8,9},{9,8},{10,11... | collective-permute-start | bytes 147464 | tf_op jit(solution)/shard_map/ppermute | solution.py:100
  29.4 0.6 %collective-permute-done.15.r_6_ = bf16[192,128]{1,0:T(8,128)(2,1)S(1)} collective-permute-done((bf16[192,128]{1,0:T(8,128)(2,1)S(1)}, bf16[192,128]{1,0:T(8,128)(2,1)S(1)}, u32[]{:S(2)}, u32[]{:S(2)}) %collective-permute-start.15) | collective-permute-done | bytes 49184 | tf_op jit(solution)/shard_map/ppermute | solution.py:100
  30.2 0.6 %shard_map.41 = f32[16,256]{1,0:T(8,128)S(1)} custom-call(bf16[192,128]{1,0:T(8,128)(2,1)S(1)} %shard_map.40.r_0_, bf16[192,128]{1,0:T(8,128)(2,1)S(1)} %collective-permute-done.10.r_1_, bf16[192,128]{1,0:T(8,128)(2,1)S(1)} %collective-permute-done.11.r_2_, bf16[192,128]{1,0:T(8,128)(2,1)S(1)} %collective-permute-done.12.r_3_, ...), custom_call_target="tpu_custom_call" | custom-call | tf_op jit(solution)/shard_map/pallas_call | solution.py:24
  30.7 0.7 %copy.4 = f32[16,256]{1,0:T(8,128)} copy(f32[16,256]{1,0:T(8,128)S(1)} %shard_map.41) | data formatting | bytes 32768
  (19 shorter events, 1.0 us)
Async XLA Ops:
  0.0 7.3 %collective-permute-start.1 = (bf16[16,2048]{1,0:T(8,128)(2,1)}, bf16[16,2048]{1,0:T(8,128)(2,1)S(1)}, u32[]{:S(2)}, u32[]{:S(2)}) collective-permute-start(bf16[16,2048]{1,0:T(8,128)(2,1)} %centers_ref.1), channel_id=1, source_target_pairs={{0,4},{1,9},{2,6},{3,11},{4,0},{5,13},{6,2},{7,15},{8,12},{9,1},{1... | collective-permute-start | bytes 196616 | tf_op jit(solution)/shard_map/ppermute | solution.py:110
  2.9 8.6 %collective-permute-start.4 = (bf16[16,2048]{1,0:T(8,128)(2,1)}, bf16[16,2048]{1,0:T(8,128)(2,1)S(1)}, u32[]{:S(2)}, u32[]{:S(2)}) collective-permute-start(bf16[16,2048]{1,0:T(8,128)(2,1)} %centers_ref.1), channel_id=1, source_target_pairs={{0,24},{1,25},{2,26},{3,27},{4,28},{5,29},{6,30},{7,31},{8,16},{9,... | collective-permute-start | bytes 196616 | tf_op jit(solution)/shard_map/ppermute | solution.py:110
  6.5 6.9 %collective-permute-start = (bf16[16,2048]{1,0:T(8,128)(2,1)}, bf16[16,2048]{1,0:T(8,128)(2,1)S(1)}, u32[]{:S(2)}, u32[]{:S(2)}) collective-permute-start(bf16[16,2048]{1,0:T(8,128)(2,1)} %centers_ref.1), channel_id=1, source_target_pairs={{0,8},{1,21},{2,10},{3,23},{4,12},{5,17},{6,14},{7,19},{8,0},{9,29... | collective-permute-start | bytes 196616 | tf_op jit(solution)/shard_map/ppermute | solution.py:110
  6.5 7.1 %collective-permute-start.2 = (bf16[16,2048]{1,0:T(8,128)(2,1)}, bf16[16,2048]{1,0:T(8,128)(2,1)S(1)}, u32[]{:S(2)}, u32[]{:S(2)}) collective-permute-start(bf16[16,2048]{1,0:T(8,128)(2,1)} %centers_ref.1), channel_id=1, source_target_pairs={{0,16},{1,5},{2,18},{3,7},{4,20},{5,1},{6,22},{7,3},{8,24},{9,13},... | collective-permute-start | bytes 196616 | tf_op jit(solution)/shard_map/ppermute | solution.py:110
  7.3 6.3 %collective-permute-start.3 = (bf16[16,2048]{1,0:T(8,128)(2,1)S(1)}, bf16[16,2048]{1,0:T(8,128)(2,1)S(1)}, u32[]{:S(2)}, u32[]{:S(2)}) collective-permute-start(bf16[16,2048]{1,0:T(8,128)(2,1)S(1)} %collective-permute-done.1.refs_2_), channel_id=1, source_target_pairs={{0,8},{1,5},{2,10},{3,7},{4,12},{5,1},{6,14},{7,3},{8,0},{9,13},{1... | collective-permute-start | bytes 196616 | tf_op jit(solution)/shard_map/ppermute | solution.py:110
  8.6 6.5 %collective-permute-start.5 = (bf16[16,2048]{1,0:T(8,128)(2,1)S(1)}, bf16[16,2048]{1,0:T(8,128)(2,1)S(1)}, u32[]{:S(2)}, u32[]{:S(2)}) collective-permute-start(bf16[16,2048]{1,0:T(8,128)(2,1)S(1)} %collective-permute-done.1.refs_2_), channel_id=1, source_target_pairs={{0,16},{1,25},{2,18},{3,27},{4,20},{5,29},{6,22},{7,31},{8,24},{9,... | collective-permute-start | bytes 196616 | tf_op jit(solution)/shard_map/ppermute | solution.py:110
  11.5 4.3 %collective-permute-start.6 = (bf16[16,2048]{1,0:T(8,128)(2,1)S(1)}, bf16[16,2048]{1,0:T(8,128)(2,1)S(1)}, u32[]{:S(2)}, u32[]{:S(2)}) collective-permute-start(bf16[16,2048]{1,0:T(8,128)(2,1)S(1)} %collective-permute-done.4.refs_5_), channel_id=1, source_target_pairs={{0,4},{1,5},{2,6},{3,7},{4,0},{5,1},{6,2},{7,3},{8,12},{9,13},{10,... | collective-permute-start | bytes 196616 | tf_op jit(solution)/shard_map/ppermute | solution.py:110
  16.0 2.9 %copy-start = (bf16[16,256]{1,0:T(8,128)(2,1)S(1)}, bf16[16,256]{1,0:T(8,128)(2,1)}, u32[]{:S(2)}) copy-start(bf16[16,256]{1,0:T(8,128)(2,1)} %r_2_.1) | copy-start | bytes 24580
  16.1 1.3 %collective-permute-start.7 = (f32[128,128]{1,0:T(8,128)S(1)}, f32[128,128]{1,0:T(8,128)S(1)}, u32[]{:S(2)}, u32[]{:S(2)}) collective-permute-start(f32[128,128]{1,0:T(8,128)S(1)} %shard_map.39), channel_id=1, source_target_pairs={{0,1},{1,0},{2,3},{3,2},{4,5},{5,4},{6,7},{7,6},{8,9},{9,8},{10,11... | collective-permute-start | bytes 196616 | tf_op jit(solution)/shard_map/ppermute | solution.py:100
  17.4 4.3 %collective-permute-start.8 = (f32[128,128]{1,0:T(8,128)S(1)}, f32[128,128]{1,0:T(8,128)S(1)}, u32[]{:S(2)}, u32[]{:S(2)}) collective-permute-start(f32[128,128]{1,0:T(8,128)S(1)} %add.3.r_0_), channel_id=1, source_target_pairs={{0,2},{1,3},{2,0},{3,1},{4,6},{5,7},{6,4},{7,5},{8,10},{9,11},{10,... | collective-permute-start | bytes 196616 | tf_op jit(solution)/shard_map/ppermute | solution.py:100
  19.0 1.2 %collective-permute-start.9 = (bf16[16,256]{1,0:T(8,128)(2,1)S(1)}, bf16[16,256]{1,0:T(8,128)(2,1)S(1)}, u32[]{:S(2)}, u32[]{:S(2)}) collective-permute-start(bf16[16,256]{1,0:T(8,128)(2,1)S(1)} %copy-done), channel_id=1, source_target_pairs={{0,1},{1,0},{2,3},{3,2},{4,5},{5,4},{6,7},{7,6},{8,9},{9,8},{10,11... | collective-permute-start | bytes 24584 | tf_op jit(solution)/shard_map/ppermute | solution.py:100
  21.8 5.8 %collective-permute-start.10 = (bf16[192,128]{1,0:T(8,128)(2,1)S(1)}, bf16[192,128]{1,0:T(8,128)(2,1)S(1)}, u32[]{:S(2)}, u32[]{:S(2)}) collective-permute-start(bf16[192,128]{1,0:T(8,128)(2,1)S(1)} %shard_map.40.r_0_), channel_id=1, source_target_pairs={{0,16},{1,21},{2,18},{3,23},{4,20},{5,17},{6,22},{7,19},{8,24},{9,... | collective-permute-start | bytes 147464 | tf_op jit(solution)/shard_map/ppermute | solution.py:110
  22.7 6.1 %collective-permute-start.11 = (bf16[192,128]{1,0:T(8,128)(2,1)S(1)}, bf16[192,128]{1,0:T(8,128)(2,1)S(1)}, u32[]{:S(2)}, u32[]{:S(2)}) collective-permute-start(bf16[192,128]{1,0:T(8,128)(2,1)S(1)} %shard_map.40.r_0_), channel_id=1, source_target_pairs={{0,24},{1,29},{2,26},{3,31},{4,28},{5,25},{6,30},{7,27},{8,16},{9,... | collective-permute-start | bytes 147464 | tf_op jit(solution)/shard_map/ppermute | solution.py:110
  24.2 4.7 %collective-permute-start.12 = (bf16[192,128]{1,0:T(8,128)(2,1)S(1)}, bf16[192,128]{1,0:T(8,128)(2,1)S(1)}, u32[]{:S(2)}, u32[]{:S(2)}) collective-permute-start(bf16[192,128]{1,0:T(8,128)(2,1)S(1)} %shard_map.40.r_0_), channel_id=1, source_target_pairs={{0,8},{1,13},{2,10},{3,15},{4,12},{5,9},{6,14},{7,11},{8,0},{9,5},... | collective-permute-start | bytes 147464 | tf_op jit(solution)/shard_map/ppermute | solution.py:110
  25.3 4.1 %collective-permute-start.13 = (bf16[192,128]{1,0:T(8,128)(2,1)S(1)}, bf16[192,128]{1,0:T(8,128)(2,1)S(1)}, u32[]{:S(2)}, u32[]{:S(2)}) collective-permute-start(bf16[192,128]{1,0:T(8,128)(2,1)S(1)} %shard_map.40.r_0_), channel_id=1, source_target_pairs={{0,4},{1,5},{2,6},{3,7},{4,0},{5,1},{6,2},{7,3},{8,12},{9,13},{10,... | collective-permute-start | bytes 147464 | tf_op jit(solution)/shard_map/ppermute | solution.py:110
  27.6 1.8 %collective-permute-start.14 = (bf16[192,128]{1,0:T(8,128)(2,1)S(1)}, bf16[192,128]{1,0:T(8,128)(2,1)S(1)}, u32[]{:S(2)}, u32[]{:S(2)}) collective-permute-start(bf16[192,128]{1,0:T(8,128)(2,1)S(1)} %collective-permute-done.10.r_1_), channel_id=1, source_target_pairs={{0,1},{1,0},{2,3},{3,2},{4,5},{5,4},{6,7},{7,6},{8,9},{9,8},{10,11... | collective-permute-start | bytes 147464 | tf_op jit(solution)/shard_map/ppermute | solution.py:100
  28.8 1.2 %collective-permute-start.15 = (bf16[192,128]{1,0:T(8,128)(2,1)S(1)}, bf16[192,128]{1,0:T(8,128)(2,1)S(1)}, u32[]{:S(2)}, u32[]{:S(2)}) collective-permute-start(bf16[192,128]{1,0:T(8,128)(2,1)S(1)} %collective-permute-done.11.r_2_), channel_id=1, source_target_pairs={{0,1},{1,0},{2,3},{3,2},{4,5},{5,4},{6,7},{7,6},{8,9},{9,8},{10,11... | collective-permute-start | bytes 147464 | tf_op jit(solution)/shard_map/ppermute | solution.py:100
  28.9 1.3 %collective-permute-start.16 = (bf16[192,128]{1,0:T(8,128)(2,1)S(1)}, bf16[192,128]{1,0:T(8,128)(2,1)S(1)}, u32[]{:S(2)}, u32[]{:S(2)}) collective-permute-start(bf16[192,128]{1,0:T(8,128)(2,1)S(1)} %collective-permute-done.12.r_3_), channel_id=1, source_target_pairs={{0,1},{1,0},{2,3},{3,2},{4,5},{5,4},{6,7},{7,6},{8,9},{9,8},{10,11... | collective-permute-start | bytes 147464 | tf_op jit(solution)/shard_map/ppermute | solution.py:100

commit v8 on v7

--- a/solution.py
+++ b/solution.py
@@ -13,7 +13,7 @@
 
 GATHER = ((0, 2, 5), (0, 1, 2), (0, 4, 1), (2, 2, 1), (0, 6, 6), (2, 4, 6), (5, 1, 1))
 LATE = (6, 7)
-SPREAD = ((0, 4, 5), (0, 6, 7), (0, 2, 3), (0, 1, 1))
+SPREAD = ((0, 3, 5), (0, 1, 7), (0, 2, 2), (0, 4, 6))
 
 
 def near(x):

time: 31.6 us -> 31.5 us (level)
  waiting for transfers between devices: 9.92 us -> 8.59 us
  starting transfers between devices: 18.2 us -> 19.4 us
    ppermute x6, starting transfers between devices: 2.05 us -> 2.97 us  [swap(): lax.ppermute(x, 'feat', [(f, f ^ bits) for f in range(lax.axis_size('feat...]
    ppermute x11, waiting for transfers between devices: 5.17 us -> 4.37 us  [swap_by_core(): return lax.ppermute(x, ('blk', 'feat'), pairs)]
    ppermute x6, waiting for transfers between devices: 4.75 us -> 4.22 us  [swap(): lax.ppermute(x, 'feat', [(f, f ^ bits) for f in range(lax.axis_size('feat...]
    ppermute x11, starting transfers between devices: 16.1 us -> 16.5 us  [swap_by_core(): return lax.ppermute(x, ('blk', 'feat'), pairs)]
  transfers between devices with their start and end apart: 17 -> 17, of which waited for: 12 -> 10; matrix products, arithmetic and copies ran while one was open for 0% -> 0% of each run, Pallas kernels for 5% -> 5%
where the time goes in v8:
time: 31.5 us; the launch traced here: 31.4 us
  starting transfers between devices  19.4 us (62%)
  waiting for transfers between devices  8.59 us (27%)
  Pallas kernels  2.57 us (8%)
  local copies, waits for them, and re-layouts  0.69 us (2%)
    ppermute x11, starting transfers between devices, swap_by_core(): return lax.ppermute(x, ('blk', 'feat'), pairs)  16.5 us
    ppermute x11, waiting for transfers between devices, swap_by_core(): return lax.ppermute(x, ('blk', 'feat'), pairs)  4.37 us
    ppermute x6, waiting for transfers between devices, swap(): lax.ppermute(x, 'feat', [(f, f ^ bits) for f in range(lax.axis_size('feat...  4.22 us
    ppermute x6, starting transfers between devices, swap(): lax.ppermute(x, 'feat', [(f, f ^ bits) for f in range(lax.axis_size('feat...  2.97 us
    pallas_call x1, Pallas kernels, on_device(): pl.pallas_call(prepare_kernel, out_shape=[pltpu.VMEM(points.shape, BF16),...  1.41 us
    pallas_call x4, Pallas kernels, call(): pl.pallas_call(kernel, out_shape=[pltpu.VMEM(*o) for o in outs], in_specs...  1.16 us
    unnamed x3, local copies, waits for them, and re-layouts  0.69 us
  transfers between devices with their start and end apart: 17, of which 10 were waited for; matrix products, arithmetic and copies ran while one was open for 0% of the time, Pallas kernels for 5%

profile of v8, /device:TPU:0, one launch (start us, length us, event | category | flops | bytes accessed | tf_op | source)
XLA Modules:
  0.0 31.4 jit_solution(9940188905371078203)
XLA Ops:
  0.0 2.9 %collective-permute-start.1 = (bf16[16,2048]{1,0:T(8,128)(2,1)}, bf16[16,2048]{1,0:T(8,128)(2,1)S(1)}, u32[]{:S(2)}, u32[]{:S(2)}) collective-permute-start(bf16[16,2048]{1,0:T(8,128)(2,1)} %centers_ref.1), channel_id=1, source_target_pairs={{0,4},{1,9},{2,6},{3,11},{4,0},{5,13},{6,2},{7,15},{8,12},{9,1},{1... | collective-permute-start | bytes 196616 | tf_op jit(solution)/shard_map/ppermute | solution.py:110
  2.9 3.6 %collective-permute-start.4 = (bf16[16,2048]{1,0:T(8,128)(2,1)}, bf16[16,2048]{1,0:T(8,128)(2,1)S(1)}, u32[]{:S(2)}, u32[]{:S(2)}) collective-permute-start(bf16[16,2048]{1,0:T(8,128)(2,1)} %centers_ref.1), channel_id=1, source_target_pairs={{0,24},{1,25},{2,26},{3,27},{4,28},{5,29},{6,30},{7,31},{8,16},{9,... | collective-permute-start | bytes 196616 | tf_op jit(solution)/shard_map/ppermute | solution.py:110
  6.5 0.8 %collective-permute-start.2 = (bf16[16,2048]{1,0:T(8,128)(2,1)}, bf16[16,2048]{1,0:T(8,128)(2,1)S(1)}, u32[]{:S(2)}, u32[]{:S(2)}) collective-permute-start(bf16[16,2048]{1,0:T(8,128)(2,1)} %centers_ref.1), channel_id=1, source_target_pairs={{0,16},{1,5},{2,18},{3,7},{4,20},{5,1},{6,22},{7,3},{8,24},{9,13},... | collective-permute-start | bytes 196616 | tf_op jit(solution)/shard_map/ppermute | solution.py:110
  7.3 1.2 %collective-permute-start.3 = (bf16[16,2048]{1,0:T(8,128)(2,1)S(1)}, bf16[16,2048]{1,0:T(8,128)(2,1)S(1)}, u32[]{:S(2)}, u32[]{:S(2)}) collective-permute-start(bf16[16,2048]{1,0:T(8,128)(2,1)S(1)} %collective-permute-done.1.refs_2_), channel_id=1, source_target_pairs={{0,8},{1,5},{2,10},{3,7},{4,12},{5,1},{6,14},{7,3},{8,0},{9,13},{1... | collective-permute-start | bytes 196616 | tf_op jit(solution)/shard_map/ppermute | solution.py:110
  8.6 2.9 %collective-permute-start.5 = (bf16[16,2048]{1,0:T(8,128)(2,1)S(1)}, bf16[16,2048]{1,0:T(8,128)(2,1)S(1)}, u32[]{:S(2)}, u32[]{:S(2)}) collective-permute-start(bf16[16,2048]{1,0:T(8,128)(2,1)S(1)} %collective-permute-done.1.refs_2_), channel_id=1, source_target_pairs={{0,16},{1,25},{2,18},{3,27},{4,20},{5,29},{6,22},{7,31},{8,24},{9,... | collective-permute-start | bytes 196616 | tf_op jit(solution)/shard_map/ppermute | solution.py:110
  11.5 0.5 %collective-permute-start.6 = (bf16[16,2048]{1,0:T(8,128)(2,1)S(1)}, bf16[16,2048]{1,0:T(8,128)(2,1)S(1)}, u32[]{:S(2)}, u32[]{:S(2)}) collective-permute-start(bf16[16,2048]{1,0:T(8,128)(2,1)S(1)} %collective-permute-done.4.refs_5_), channel_id=1, source_target_pairs={{0,4},{1,5},{2,6},{3,7},{4,0},{5,1},{6,2},{7,3},{8,12},{9,13},{10,... | collective-permute-start | bytes 196616 | tf_op jit(solution)/shard_map/ppermute | solution.py:110
  12.0 1.4 %shard_map.37 = (bf16[128,2048]{1,0:T(8,128)(2,1)S(1)}, bf16[16,2048]{1,0:T(8,128)(2,1)S(1)}, f32[1,128]{1,0:T(1,128)S(1)}) custom-call(bf16[128,2048]{1,0:T(8,128)(2,1)} %points_ref.1, bf16[16,2048]{1,0:T(8,128)(2,1)} %centers_ref.1), custom_call_target="tpu_custom_call" | custom-call | flops 524288 | bytes 524288 | tf_op jit(solution)/shard_map/pallas_call | solution.py:128
  13.6 0.3 shard_map.38.r_2_
  14.0 1.1 %collective-permute-done.5.r_3_ = bf16[16,2048]{1,0:T(8,128)(2,1)S(1)} collective-permute-done((bf16[16,2048]{1,0:T(8,128)(2,1)S(1)}, bf16[16,2048]{1,0:T(8,128)(2,1)S(1)}, u32[]{:S(2)}, u32[]{:S(2)}) %collective-permute-start.5) | collective-permute-done | bytes 65568 | tf_op jit(solution)/shard_map/ppermute | solution.py:110
  15.0 0.7 %collective-permute-done.6.r_4_ = bf16[16,2048]{1,0:T(8,128)(2,1)S(1)} collective-permute-done((bf16[16,2048]{1,0:T(8,128)(2,1)S(1)}, bf16[16,2048]{1,0:T(8,128)(2,1)S(1)}, u32[]{:S(2)}, u32[]{:S(2)}) %collective-permute-start.6) | collective-permute-done | bytes 65568 | tf_op jit(solution)/shard_map/ppermute | solution.py:110
  15.8 0.3 shard_map.39
  16.1 1.2 %collective-permute-done.7 = f32[128,128]{1,0:T(8,128)S(1)} collective-permute-done((f32[128,128]{1,0:T(8,128)S(1)}, f32[128,128]{1,0:T(8,128)S(1)}, u32[]{:S(2)}, u32[]{:S(2)}) %collective-permute-start.7) | collective-permute-done | bytes 65568 | tf_op jit(solution)/shard_map/ppermute | solution.py:100
  17.4 1.6 %collective-permute-start.8 = (f32[128,128]{1,0:T(8,128)S(1)}, f32[128,128]{1,0:T(8,128)S(1)}, u32[]{:S(2)}, u32[]{:S(2)}) collective-permute-start(f32[128,128]{1,0:T(8,128)S(1)} %add.3.r_0_), channel_id=1, source_target_pairs={{0,2},{1,3},{2,0},{3,1},{4,6},{5,7},{6,4},{7,5},{8,10},{9,11},{10,... | collective-permute-start | bytes 196616 | tf_op jit(solution)/shard_map/ppermute | solution.py:100
  19.0 1.2 %collective-permute-done.9.r_3_ = bf16[16,256]{1,0:T(8,128)(2,1)S(1)} collective-permute-done((bf16[16,256]{1,0:T(8,128)(2,1)S(1)}, bf16[16,256]{1,0:T(8,128)(2,1)S(1)}, u32[]{:S(2)}, u32[]{:S(2)}) %collective-permute-start.9) | collective-permute-done | bytes 8224 | tf_op jit(solution)/shard_map/ppermute | solution.py:100
  20.2 1.6 %collective-permute-done.8.r_1_ = f32[128,128]{1,0:T(8,128)S(1)} collective-permute-done((f32[128,128]{1,0:T(8,128)S(1)}, f32[128,128]{1,0:T(8,128)S(1)}, u32[]{:S(2)}, u32[]{:S(2)}) %collective-permute-start.8) | collective-permute-done | bytes 65568 | tf_op jit(solution)/shard_map/ppermute | solution.py:100
  22.0 1.3 %collective-permute-start.11 = (bf16[192,128]{1,0:T(8,128)(2,1)S(1)}, bf16[192,128]{1,0:T(8,128)(2,1)S(1)}, u32[]{:S(2)}, u32[]{:S(2)}) collective-permute-start(bf16[192,128]{1,0:T(8,128)(2,1)S(1)} %shard_map.40.r_0_), channel_id=1, source_target_pairs={{0,4},{1,29},{2,6},{3,31},{4,0},{5,25},{6,2},{7,27},{8,12},{9,21},... | collective-permute-start | bytes 147464 | tf_op jit(solution)/shard_map/ppermute | solution.py:110
  23.3 2.0 %collective-permute-start.13 = (bf16[192,128]{1,0:T(8,128)(2,1)S(1)}, bf16[192,128]{1,0:T(8,128)(2,1)S(1)}, u32[]{:S(2)}, u32[]{:S(2)}) collective-permute-start(bf16[192,128]{1,0:T(8,128)(2,1)S(1)} %shard_map.40.r_0_), channel_id=1, source_target_pairs={{0,16},{1,25},{2,18},{3,27},{4,20},{5,29},{6,22},{7,31},{8,24},{9,... | collective-permute-start | bytes 147464 | tf_op jit(solution)/shard_map/ppermute | solution.py:110
  25.3 0.9 %collective-permute-start.12 = (bf16[192,128]{1,0:T(8,128)(2,1)S(1)}, bf16[192,128]{1,0:T(8,128)(2,1)S(1)}, u32[]{:S(2)}, u32[]{:S(2)}) collective-permute-start(bf16[192,128]{1,0:T(8,128)(2,1)S(1)} %shard_map.40.r_0_), channel_id=1, source_target_pairs={{0,8},{1,9},{2,10},{3,11},{4,12},{5,13},{6,14},{7,15},{8,0},{9,1},... | collective-permute-start | bytes 147464 | tf_op jit(solution)/shard_map/ppermute | solution.py:110
  26.2 0.6 %collective-permute-done.10.r_1_ = bf16[192,128]{1,0:T(8,128)(2,1)S(1)} collective-permute-done((bf16[192,128]{1,0:T(8,128)(2,1)S(1)}, bf16[192,128]{1,0:T(8,128)(2,1)S(1)}, u32[]{:S(2)}, u32[]{:S(2)}) %collective-permute-start.10) | collective-permute-done | bytes 49184 | tf_op jit(solution)/shard_map/ppermute | solution.py:110
  26.8 1.3 %collective-permute-start.15 = (bf16[192,128]{1,0:T(8,128)(2,1)S(1)}, bf16[192,128]{1,0:T(8,128)(2,1)S(1)}, u32[]{:S(2)}, u32[]{:S(2)}) collective-permute-start(bf16[192,128]{1,0:T(8,128)(2,1)S(1)} %collective-permute-done.11.r_2_), channel_id=1, source_target_pairs={{0,1},{1,0},{2,3},{3,2},{4,5},{5,4},{6,7},{7,6},{8,9},{9,8},{10,11... | collective-permute-start | bytes 147464 | tf_op jit(solution)/shard_map/ppermute | solution.py:100
  28.1 0.8 %collective-permute-done.13.r_4_ = bf16[192,128]{1,0:T(8,128)(2,1)S(1)} collective-permute-done((bf16[192,128]{1,0:T(8,128)(2,1)S(1)}, bf16[192,128]{1,0:T(8,128)(2,1)S(1)}, u32[]{:S(2)}, u32[]{:S(2)}) %collective-permute-start.13) | collective-permute-done | bytes 49184 | tf_op jit(solution)/shard_map/ppermute | solution.py:110
  28.9 1.0 %collective-permute-done.12.r_3_ = bf16[192,128]{1,0:T(8,128)(2,1)S(1)} collective-permute-done((bf16[192,128]{1,0:T(8,128)(2,1)S(1)}, bf16[192,128]{1,0:T(8,128)(2,1)S(1)}, u32[]{:S(2)}, u32[]{:S(2)}) %collective-permute-start.12) | collective-permute-done | bytes 49184 | tf_op jit(solution)/shard_map/ppermute | solution.py:110
  30.1 0.6 %shard_map.41 = f32[16,256]{1,0:T(8,128)S(1)} custom-call(bf16[192,128]{1,0:T(8,128)(2,1)S(1)} %shard_map.40.r_0_, bf16[192,128]{1,0:T(8,128)(2,1)S(1)} %collective-permute-done.10.r_1_, bf16[192,128]{1,0:T(8,128)(2,1)S(1)} %collective-permute-done.11.r_2_, bf16[192,128]{1,0:T(8,128)(2,1)S(1)} %collective-permute-done.12.r_3_, ...), custom_call_target="tpu_custom_call" | custom-call | tf_op jit(solution)/shard_map/pallas_call | solution.py:24
  30.7 0.7 %copy.4 = f32[16,256]{1,0:T(8,128)} copy(f32[16,256]{1,0:T(8,128)S(1)} %shard_map.41) | data formatting | bytes 32768
  (19 shorter events, 0.8 us)
Async XLA Ops:
  0.0 7.3 %collective-permute-start.1 = (bf16[16,2048]{1,0:T(8,128)(2,1)}, bf16[16,2048]{1,0:T(8,128)(2,1)S(1)}, u32[]{:S(2)}, u32[]{:S(2)}) collective-permute-start(bf16[16,2048]{1,0:T(8,128)(2,1)} %centers_ref.1), channel_id=1, source_target_pairs={{0,4},{1,9},{2,6},{3,11},{4,0},{5,13},{6,2},{7,15},{8,12},{9,1},{1... | collective-permute-start | bytes 196616 | tf_op jit(solution)/shard_map/ppermute | solution.py:110
  2.9 8.6 %collective-permute-start.4 = (bf16[16,2048]{1,0:T(8,128)(2,1)}, bf16[16,2048]{1,0:T(8,128)(2,1)S(1)}, u32[]{:S(2)}, u32[]{:S(2)}) collective-permute-start(bf16[16,2048]{1,0:T(8,128)(2,1)} %centers_ref.1), channel_id=1, source_target_pairs={{0,24},{1,25},{2,26},{3,27},{4,28},{5,29},{6,30},{7,31},{8,16},{9,... | collective-permute-start | bytes 196616 | tf_op jit(solution)/shard_map/ppermute | solution.py:110
  6.5 6.9 %collective-permute-start = (bf16[16,2048]{1,0:T(8,128)(2,1)}, bf16[16,2048]{1,0:T(8,128)(2,1)S(1)}, u32[]{:S(2)}, u32[]{:S(2)}) collective-permute-start(bf16[16,2048]{1,0:T(8,128)(2,1)} %centers_ref.1), channel_id=1, source_target_pairs={{0,8},{1,21},{2,10},{3,23},{4,12},{5,17},{6,14},{7,19},{8,0},{9,29... | collective-permute-start | bytes 196616 | tf_op jit(solution)/shard_map/ppermute | solution.py:110
  6.5 7.1 %collective-permute-start.2 = (bf16[16,2048]{1,0:T(8,128)(2,1)}, bf16[16,2048]{1,0:T(8,128)(2,1)S(1)}, u32[]{:S(2)}, u32[]{:S(2)}) collective-permute-start(bf16[16,2048]{1,0:T(8,128)(2,1)} %centers_ref.1), channel_id=1, source_target_pairs={{0,16},{1,5},{2,18},{3,7},{4,20},{5,1},{6,22},{7,3},{8,24},{9,13},... | collective-permute-start | bytes 196616 | tf_op jit(solution)/shard_map/ppermute | solution.py:110
  7.3 6.3 %collective-permute-start.3 = (bf16[16,2048]{1,0:T(8,128)(2,1)S(1)}, bf16[16,2048]{1,0:T(8,128)(2,1)S(1)}, u32[]{:S(2)}, u32[]{:S(2)}) collective-permute-start(bf16[16,2048]{1,0:T(8,128)(2,1)S(1)} %collective-permute-done.1.refs_2_), channel_id=1, source_target_pairs={{0,8},{1,5},{2,10},{3,7},{4,12},{5,1},{6,14},{7,3},{8,0},{9,13},{1... | collective-permute-start | bytes 196616 | tf_op jit(solution)/shard_map/ppermute | solution.py:110
  8.6 6.5 %collective-permute-start.5 = (bf16[16,2048]{1,0:T(8,128)(2,1)S(1)}, bf16[16,2048]{1,0:T(8,128)(2,1)S(1)}, u32[]{:S(2)}, u32[]{:S(2)}) collective-permute-start(bf16[16,2048]{1,0:T(8,128)(2,1)S(1)} %collective-permute-done.1.refs_2_), channel_id=1, source_target_pairs={{0,16},{1,25},{2,18},{3,27},{4,20},{5,29},{6,22},{7,31},{8,24},{9,... | collective-permute-start | bytes 196616 | tf_op jit(solution)/shard_map/ppermute | solution.py:110
  11.5 4.3 %collective-permute-start.6 = (bf16[16,2048]{1,0:T(8,128)(2,1)S(1)}, bf16[16,2048]{1,0:T(8,128)(2,1)S(1)}, u32[]{:S(2)}, u32[]{:S(2)}) collective-permute-start(bf16[16,2048]{1,0:T(8,128)(2,1)S(1)} %collective-permute-done.4.refs_5_), channel_id=1, source_target_pairs={{0,4},{1,5},{2,6},{3,7},{4,0},{5,1},{6,2},{7,3},{8,12},{9,13},{10,... | collective-permute-start | bytes 196616 | tf_op jit(solution)/shard_map/ppermute | solution.py:110
  16.0 2.9 %copy-start = (bf16[16,256]{1,0:T(8,128)(2,1)S(1)}, bf16[16,256]{1,0:T(8,128)(2,1)}, u32[]{:S(2)}) copy-start(bf16[16,256]{1,0:T(8,128)(2,1)} %r_2_.1) | copy-start | bytes 24580
  16.1 1.3 %collective-permute-start.7 = (f32[128,128]{1,0:T(8,128)S(1)}, f32[128,128]{1,0:T(8,128)S(1)}, u32[]{:S(2)}, u32[]{:S(2)}) collective-permute-start(f32[128,128]{1,0:T(8,128)S(1)} %shard_map.39), channel_id=1, source_target_pairs={{0,1},{1,0},{2,3},{3,2},{4,5},{5,4},{6,7},{7,6},{8,9},{9,8},{10,11... | collective-permute-start | bytes 196616 | tf_op jit(solution)/shard_map/ppermute | solution.py:100
  17.4 4.3 %collective-permute-start.8 = (f32[128,128]{1,0:T(8,128)S(1)}, f32[128,128]{1,0:T(8,128)S(1)}, u32[]{:S(2)}, u32[]{:S(2)}) collective-permute-start(f32[128,128]{1,0:T(8,128)S(1)} %add.3.r_0_), channel_id=1, source_target_pairs={{0,2},{1,3},{2,0},{3,1},{4,6},{5,7},{6,4},{7,5},{8,10},{9,11},{10,... | collective-permute-start | bytes 196616 | tf_op jit(solution)/shard_map/ppermute | solution.py:100
  19.0 1.2 %collective-permute-start.9 = (bf16[16,256]{1,0:T(8,128)(2,1)S(1)}, bf16[16,256]{1,0:T(8,128)(2,1)S(1)}, u32[]{:S(2)}, u32[]{:S(2)}) collective-permute-start(bf16[16,256]{1,0:T(8,128)(2,1)S(1)} %copy-done), channel_id=1, source_target_pairs={{0,1},{1,0},{2,3},{3,2},{4,5},{5,4},{6,7},{7,6},{8,9},{9,8},{10,11... | collective-permute-start | bytes 24584 | tf_op jit(solution)/shard_map/ppermute | solution.py:100
  21.8 5.1 %collective-permute-start.10 = (bf16[192,128]{1,0:T(8,128)(2,1)S(1)}, bf16[192,128]{1,0:T(8,128)(2,1)S(1)}, u32[]{:S(2)}, u32[]{:S(2)}) collective-permute-start(bf16[192,128]{1,0:T(8,128)(2,1)S(1)} %shard_map.40.r_0_), channel_id=1, source_target_pairs={{0,12},{1,21},{2,14},{3,23},{4,8},{5,17},{6,10},{7,19},{8,4},{9,29... | collective-permute-start | bytes 147464 | tf_op jit(solution)/shard_map/ppermute | solution.py:110
  22.0 4.8 %collective-permute-start.11 = (bf16[192,128]{1,0:T(8,128)(2,1)S(1)}, bf16[192,128]{1,0:T(8,128)(2,1)S(1)}, u32[]{:S(2)}, u32[]{:S(2)}) collective-permute-start(bf16[192,128]{1,0:T(8,128)(2,1)S(1)} %shard_map.40.r_0_), channel_id=1, source_target_pairs={{0,4},{1,29},{2,6},{3,31},{4,0},{5,25},{6,2},{7,27},{8,12},{9,21},... | collective-permute-start | bytes 147464 | tf_op jit(solution)/shard_map/ppermute | solution.py:110
  23.3 5.6 %collective-permute-start.13 = (bf16[192,128]{1,0:T(8,128)(2,1)S(1)}, bf16[192,128]{1,0:T(8,128)(2,1)S(1)}, u32[]{:S(2)}, u32[]{:S(2)}) collective-permute-start(bf16[192,128]{1,0:T(8,128)(2,1)S(1)} %shard_map.40.r_0_), channel_id=1, source_target_pairs={{0,16},{1,25},{2,18},{3,27},{4,20},{5,29},{6,22},{7,31},{8,24},{9,... | collective-permute-start | bytes 147464 | tf_op jit(solution)/shard_map/ppermute | solution.py:110
  25.3 4.6 %collective-permute-start.12 = (bf16[192,128]{1,0:T(8,128)(2,1)S(1)}, bf16[192,128]{1,0:T(8,128)(2,1)S(1)}, u32[]{:S(2)}, u32[]{:S(2)}) collective-permute-start(bf16[192,128]{1,0:T(8,128)(2,1)S(1)} %shard_map.40.r_0_), channel_id=1, source_target_pairs={{0,8},{1,9},{2,10},{3,11},{4,12},{5,13},{6,14},{7,15},{8,0},{9,1},... | collective-permute-start | bytes 147464 | tf_op jit(solution)/shard_map/ppermute | solution.py:110
  26.8 3.1 %collective-permute-start.14 = (bf16[192,128]{1,0:T(8,128)(2,1)S(1)}, bf16[192,128]{1,0:T(8,128)(2,1)S(1)}, u32[]{:S(2)}, u32[]{:S(2)}) collective-permute-start(bf16[192,128]{1,0:T(8,128)(2,1)S(1)} %collective-permute-done.10.r_1_), channel_id=1, source_target_pairs={{0,1},{1,0},{2,3},{3,2},{4,5},{5,4},{6,7},{7,6},{8,9},{9,8},{10,11... | collective-permute-start | bytes 147464 | tf_op jit(solution)/shard_map/ppermute | solution.py:100
  26.8 3.1 %collective-permute-start.15 = (bf16[192,128]{1,0:T(8,128)(2,1)S(1)}, bf16[192,128]{1,0:T(8,128)(2,1)S(1)}, u32[]{:S(2)}, u32[]{:S(2)}) collective-permute-start(bf16[192,128]{1,0:T(8,128)(2,1)S(1)} %collective-permute-done.11.r_2_), channel_id=1, source_target_pairs={{0,1},{1,0},{2,3},{3,2},{4,5},{5,4},{6,7},{7,6},{8,9},{9,8},{10,11... | collective-permute-start | bytes 147464 | tf_op jit(solution)/shard_map/ppermute | solution.py:100
  28.9 1.2 %collective-permute-start.16 = (bf16[192,128]{1,0:T(8,128)(2,1)S(1)}, bf16[192,128]{1,0:T(8,128)(2,1)S(1)}, u32[]{:S(2)}, u32[]{:S(2)}) collective-permute-start(bf16[192,128]{1,0:T(8,128)(2,1)S(1)} %collective-permute-done.13.r_4_), channel_id=1, source_target_pairs={{0,1},{1,0},{2,3},{3,2},{4,5},{5,4},{6,7},{7,6},{8,9},{9,8},{10,11... | collective-permute-start | bytes 147464 | tf_op jit(solution)/shard_map/ppermute | solution.py:100

commit v9 on v8

--- a/solution.py
+++ b/solution.py
@@ -12,7 +12,7 @@
 VMEM = pl.BlockSpec(memory_space=pltpu.VMEM)
 
 GATHER = ((0, 2, 5), (0, 1, 2), (0, 4, 1), (2, 2, 1), (0, 6, 6), (2, 4, 6), (5, 1, 1))
-LATE = (6, 7)
+LATE = (7,)
 SPREAD = ((0, 3, 5), (0, 1, 7), (0, 2, 2), (0, 4, 6))
 
 

time: 31.5 us -> 31.4 us (level)
  waiting for transfers between devices: 8.59 us -> 8.18 us
  starting transfers between devices: 19.4 us -> 19.8 us
    ppermute x11, waiting for transfers between devices: 4.37 us -> 3.98 us  [swap_by_core(): return lax.ppermute(x, ('blk', 'feat'), pairs)]
    ppermute x11, starting transfers between devices: 16.5 us -> 16.8 us  [swap_by_core(): return lax.ppermute(x, ('blk', 'feat'), pairs)]
where the time goes in v9:
time: 31.4 us; the launch traced here: 31.2 us
  starting transfers between devices  19.8 us (63%)
  waiting for transfers between devices  8.18 us (26%)
  Pallas kernels  2.54 us (8%)
  local copies, waits for them, and re-layouts  0.68 us (2%)
    ppermute x11, starting transfers between devices, swap_by_core(): return lax.ppermute(x, ('blk', 'feat'), pairs)  16.8 us
    ppermute x6, waiting for transfers between devices, swap(): lax.ppermute(x, 'feat', [(f, f ^ bits) for f in range(lax.axis_size('feat...  4.2 us
    ppermute x11, waiting for transfers between devices, swap_by_core(): return lax.ppermute(x, ('blk', 'feat'), pairs)  3.98 us
    ppermute x6, starting transfers between devices, swap(): lax.ppermute(x, 'feat', [(f, f ^ bits) for f in range(lax.axis_size('feat...  2.97 us
    pallas_call x1, Pallas kernels, on_device(): pl.pallas_call(prepare_kernel, out_shape=[pltpu.VMEM(points.shape, BF16),...  1.41 us
    pallas_call x4, Pallas kernels, call(): pl.pallas_call(kernel, out_shape=[pltpu.VMEM(*o) for o in outs], in_specs...  1.13 us
    unnamed x3, local copies, waits for them, and re-layouts  0.68 us
  transfers between devices with their start and end apart: 17, of which 10 were waited for; matrix products, arithmetic and copies ran while one was open for 0% of the time, Pallas kernels for 5%

profile of v9, /device:TPU:0, one launch (start us, length us, event | category | flops | bytes accessed | tf_op | source)
XLA Modules:
  0.0 31.2 jit_solution(5259314064777027881)
XLA Ops:
  0.0 2.9 %collective-permute-start.1 = (bf16[16,2048]{1,0:T(8,128)(2,1)}, bf16[16,2048]{1,0:T(8,128)(2,1)S(1)}, u32[]{:S(2)}, u32[]{:S(2)}) collective-permute-start(bf16[16,2048]{1,0:T(8,128)(2,1)} %centers_ref.1), channel_id=1, source_target_pairs={{0,4},{1,9},{2,6},{3,11},{4,0},{5,13},{6,2},{7,15},{8,12},{9,1},{1... | collective-permute-start | bytes 196616 | tf_op jit(solution)/shard_map/ppermute | solution.py:110
  2.9 3.6 %collective-permute-start.4 = (bf16[16,2048]{1,0:T(8,128)(2,1)}, bf16[16,2048]{1,0:T(8,128)(2,1)S(1)}, u32[]{:S(2)}, u32[]{:S(2)}) collective-permute-start(bf16[16,2048]{1,0:T(8,128)(2,1)} %centers_ref.1), channel_id=1, source_target_pairs={{0,24},{1,25},{2,26},{3,27},{4,28},{5,29},{6,30},{7,31},{8,16},{9,... | collective-permute-start | bytes 196616 | tf_op jit(solution)/shard_map/ppermute | solution.py:110
  6.5 0.8 %collective-permute-start.2 = (bf16[16,2048]{1,0:T(8,128)(2,1)}, bf16[16,2048]{1,0:T(8,128)(2,1)S(1)}, u32[]{:S(2)}, u32[]{:S(2)}) collective-permute-start(bf16[16,2048]{1,0:T(8,128)(2,1)} %centers_ref.1), channel_id=1, source_target_pairs={{0,16},{1,5},{2,18},{3,7},{4,20},{5,1},{6,22},{7,3},{8,24},{9,13},... | collective-permute-start | bytes 196616 | tf_op jit(solution)/shard_map/ppermute | solution.py:110
  7.3 1.2 %collective-permute-start.3 = (bf16[16,2048]{1,0:T(8,128)(2,1)S(1)}, bf16[16,2048]{1,0:T(8,128)(2,1)S(1)}, u32[]{:S(2)}, u32[]{:S(2)}) collective-permute-start(bf16[16,2048]{1,0:T(8,128)(2,1)S(1)} %collective-permute-done.1.refs_2_), channel_id=1, source_target_pairs={{0,8},{1,5},{2,10},{3,7},{4,12},{5,1},{6,14},{7,3},{8,0},{9,13},{1... | collective-permute-start | bytes 196616 | tf_op jit(solution)/shard_map/ppermute | solution.py:110
  8.6 2.9 %collective-permute-start.5 = (bf16[16,2048]{1,0:T(8,128)(2,1)S(1)}, bf16[16,2048]{1,0:T(8,128)(2,1)S(1)}, u32[]{:S(2)}, u32[]{:S(2)}) collective-permute-start(bf16[16,2048]{1,0:T(8,128)(2,1)S(1)} %collective-permute-done.1.refs_2_), channel_id=1, source_target_pairs={{0,16},{1,25},{2,18},{3,27},{4,20},{5,29},{6,22},{7,31},{8,24},{9,... | collective-permute-start | bytes 196616 | tf_op jit(solution)/shard_map/ppermute | solution.py:110
  11.5 0.5 %collective-permute-start.6 = (bf16[16,2048]{1,0:T(8,128)(2,1)S(1)}, bf16[16,2048]{1,0:T(8,128)(2,1)S(1)}, u32[]{:S(2)}, u32[]{:S(2)}) collective-permute-start(bf16[16,2048]{1,0:T(8,128)(2,1)S(1)} %collective-permute-done.4.refs_5_), channel_id=1, source_target_pairs={{0,4},{1,5},{2,6},{3,7},{4,0},{5,1},{6,2},{7,3},{8,12},{9,13},{10,... | collective-permute-start | bytes 196616 | tf_op jit(solution)/shard_map/ppermute | solution.py:110
  12.0 1.4 %shard_map.37 = (bf16[128,2048]{1,0:T(8,128)(2,1)S(1)}, bf16[16,2048]{1,0:T(8,128)(2,1)S(1)}, f32[1,128]{1,0:T(1,128)S(1)}) custom-call(bf16[128,2048]{1,0:T(8,128)(2,1)} %points_ref.1, bf16[16,2048]{1,0:T(8,128)(2,1)} %centers_ref.1), custom_call_target="tpu_custom_call" | custom-call | flops 524288 | bytes 524288 | tf_op jit(solution)/shard_map/pallas_call | solution.py:128
  13.6 1.4 %collective-permute-done.5.refs_6_ = bf16[16,2048]{1,0:T(8,128)(2,1)S(1)} collective-permute-done((bf16[16,2048]{1,0:T(8,128)(2,1)S(1)}, bf16[16,2048]{1,0:T(8,128)(2,1)S(1)}, u32[]{:S(2)}, u32[]{:S(2)}) %collective-permute-start.5) | collective-permute-done | bytes 65568 | tf_op jit(solution)/shard_map/ppermute | solution.py:110
  15.0 0.3 shard_map.38.r_2_
  15.4 0.4 %collective-permute-done.6.r_3_ = bf16[16,2048]{1,0:T(8,128)(2,1)S(1)} collective-permute-done((bf16[16,2048]{1,0:T(8,128)(2,1)S(1)}, bf16[16,2048]{1,0:T(8,128)(2,1)S(1)}, u32[]{:S(2)}, u32[]{:S(2)}) %collective-permute-start.6) | collective-permute-done | bytes 65568 | tf_op jit(solution)/shard_map/ppermute | solution.py:110
  15.8 0.2 shard_map.39
  16.0 1.3 %collective-permute-done.7 = f32[128,128]{1,0:T(8,128)S(1)} collective-permute-done((f32[128,128]{1,0:T(8,128)S(1)}, f32[128,128]{1,0:T(8,128)S(1)}, u32[]{:S(2)}, u32[]{:S(2)}) %collective-permute-start.7) | collective-permute-done | bytes 65568 | tf_op jit(solution)/shard_map/ppermute | solution.py:100
  17.3 1.6 %collective-permute-start.8 = (f32[128,128]{1,0:T(8,128)S(1)}, f32[128,128]{1,0:T(8,128)S(1)}, u32[]{:S(2)}, u32[]{:S(2)}) collective-permute-start(f32[128,128]{1,0:T(8,128)S(1)} %add.3.r_0_), channel_id=1, source_target_pairs={{0,2},{1,3},{2,0},{3,1},{4,6},{5,7},{6,4},{7,5},{8,10},{9,11},{10,... | collective-permute-start | bytes 196616 | tf_op jit(solution)/shard_map/ppermute | solution.py:100
  18.9 1.2 %collective-permute-done.9.r_3_ = bf16[16,256]{1,0:T(8,128)(2,1)S(1)} collective-permute-done((bf16[16,256]{1,0:T(8,128)(2,1)S(1)}, bf16[16,256]{1,0:T(8,128)(2,1)S(1)}, u32[]{:S(2)}, u32[]{:S(2)}) %collective-permute-start.9) | collective-permute-done | bytes 8224 | tf_op jit(solution)/shard_map/ppermute | solution.py:100
  20.1 1.6 %collective-permute-done.8.r_1_ = f32[128,128]{1,0:T(8,128)S(1)} collective-permute-done((f32[128,128]{1,0:T(8,128)S(1)}, f32[128,128]{1,0:T(8,128)S(1)}, u32[]{:S(2)}, u32[]{:S(2)}) %collective-permute-start.8) | collective-permute-done | bytes 65568 | tf_op jit(solution)/shard_map/ppermute | solution.py:100
  21.9 1.3 %collective-permute-start.11 = (bf16[192,128]{1,0:T(8,128)(2,1)S(1)}, bf16[192,128]{1,0:T(8,128)(2,1)S(1)}, u32[]{:S(2)}, u32[]{:S(2)}) collective-permute-start(bf16[192,128]{1,0:T(8,128)(2,1)S(1)} %shard_map.40.r_0_), channel_id=1, source_target_pairs={{0,4},{1,29},{2,6},{3,31},{4,0},{5,25},{6,2},{7,27},{8,12},{9,21},... | collective-permute-start | bytes 147464 | tf_op jit(solution)/shard_map/ppermute | solution.py:110
  23.2 2.0 %collective-permute-start.13 = (bf16[192,128]{1,0:T(8,128)(2,1)S(1)}, bf16[192,128]{1,0:T(8,128)(2,1)S(1)}, u32[]{:S(2)}, u32[]{:S(2)}) collective-permute-start(bf16[192,128]{1,0:T(8,128)(2,1)S(1)} %shard_map.40.r_0_), channel_id=1, source_target_pairs={{0,16},{1,25},{2,18},{3,27},{4,20},{5,29},{6,22},{7,31},{8,24},{9,... | collective-permute-start | bytes 147464 | tf_op jit(solution)/shard_map/ppermute | solution.py:110
  25.2 1.3 %collective-permute-start.12 = (bf16[192,128]{1,0:T(8,128)(2,1)S(1)}, bf16[192,128]{1,0:T(8,128)(2,1)S(1)}, u32[]{:S(2)}, u32[]{:S(2)}) collective-permute-start(bf16[192,128]{1,0:T(8,128)(2,1)S(1)} %shard_map.40.r_0_), channel_id=1, source_target_pairs={{0,8},{1,9},{2,10},{3,11},{4,12},{5,13},{6,14},{7,15},{8,0},{9,1},... | collective-permute-start | bytes 147464 | tf_op jit(solution)/shard_map/ppermute | solution.py:110
  26.4 0.3 collective-permute-done.10.r_1_
  26.7 1.4 %collective-permute-start.15 = (bf16[192,128]{1,0:T(8,128)(2,1)S(1)}, bf16[192,128]{1,0:T(8,128)(2,1)S(1)}, u32[]{:S(2)}, u32[]{:S(2)}) collective-permute-start(bf16[192,128]{1,0:T(8,128)(2,1)S(1)} %collective-permute-done.11.r_2_), channel_id=1, source_target_pairs={{0,1},{1,0},{2,3},{3,2},{4,5},{5,4},{6,7},{7,6},{8,9},{9,8},{10,11... | collective-permute-start | bytes 147464 | tf_op jit(solution)/shard_map/ppermute | solution.py:100
  28.1 0.7 %collective-permute-done.13.r_4_ = bf16[192,128]{1,0:T(8,128)(2,1)S(1)} collective-permute-done((bf16[192,128]{1,0:T(8,128)(2,1)S(1)}, bf16[192,128]{1,0:T(8,128)(2,1)S(1)}, u32[]{:S(2)}, u32[]{:S(2)}) %collective-permute-start.13) | collective-permute-done | bytes 49184 | tf_op jit(solution)/shard_map/ppermute | solution.py:110
  28.8 1.0 %collective-permute-done.12.r_3_ = bf16[192,128]{1,0:T(8,128)(2,1)S(1)} collective-permute-done((bf16[192,128]{1,0:T(8,128)(2,1)S(1)}, bf16[192,128]{1,0:T(8,128)(2,1)S(1)}, u32[]{:S(2)}, u32[]{:S(2)}) %collective-permute-start.12) | collective-permute-done | bytes 49184 | tf_op jit(solution)/shard_map/ppermute | solution.py:110
  30.0 0.6 %shard_map.41 = f32[16,256]{1,0:T(8,128)S(1)} custom-call(bf16[192,128]{1,0:T(8,128)(2,1)S(1)} %shard_map.40.r_0_, bf16[192,128]{1,0:T(8,128)(2,1)S(1)} %collective-permute-done.10.r_1_, bf16[192,128]{1,0:T(8,128)(2,1)S(1)} %collective-permute-done.11.r_2_, bf16[192,128]{1,0:T(8,128)(2,1)S(1)} %collective-permute-done.12.r_3_, ...), custom_call_target="tpu_custom_call" | custom-call | tf_op jit(solution)/shard_map/pallas_call | solution.py:24
  30.5 0.7 %copy.4 = f32[16,256]{1,0:T(8,128)} copy(f32[16,256]{1,0:T(8,128)S(1)} %shard_map.41) | data formatting | bytes 32768
  (19 shorter events, 0.7 us)
Async XLA Ops:
  0.0 7.3 %collective-permute-start.1 = (bf16[16,2048]{1,0:T(8,128)(2,1)}, bf16[16,2048]{1,0:T(8,128)(2,1)S(1)}, u32[]{:S(2)}, u32[]{:S(2)}) collective-permute-start(bf16[16,2048]{1,0:T(8,128)(2,1)} %centers_ref.1), channel_id=1, source_target_pairs={{0,4},{1,9},{2,6},{3,11},{4,0},{5,13},{6,2},{7,15},{8,12},{9,1},{1... | collective-permute-start | bytes 196616 | tf_op jit(solution)/shard_map/ppermute | solution.py:110
  2.9 8.6 %collective-permute-start.4 = (bf16[16,2048]{1,0:T(8,128)(2,1)}, bf16[16,2048]{1,0:T(8,128)(2,1)S(1)}, u32[]{:S(2)}, u32[]{:S(2)}) collective-permute-start(bf16[16,2048]{1,0:T(8,128)(2,1)} %centers_ref.1), channel_id=1, source_target_pairs={{0,24},{1,25},{2,26},{3,27},{4,28},{5,29},{6,30},{7,31},{8,16},{9,... | collective-permute-start | bytes 196616 | tf_op jit(solution)/shard_map/ppermute | solution.py:110
  6.5 6.9 %collective-permute-start = (bf16[16,2048]{1,0:T(8,128)(2,1)}, bf16[16,2048]{1,0:T(8,128)(2,1)S(1)}, u32[]{:S(2)}, u32[]{:S(2)}) collective-permute-start(bf16[16,2048]{1,0:T(8,128)(2,1)} %centers_ref.1), channel_id=1, source_target_pairs={{0,8},{1,21},{2,10},{3,23},{4,12},{5,17},{6,14},{7,19},{8,0},{9,29... | collective-permute-start | bytes 196616 | tf_op jit(solution)/shard_map/ppermute | solution.py:110
  6.5 7.1 %collective-permute-start.2 = (bf16[16,2048]{1,0:T(8,128)(2,1)}, bf16[16,2048]{1,0:T(8,128)(2,1)S(1)}, u32[]{:S(2)}, u32[]{:S(2)}) collective-permute-start(bf16[16,2048]{1,0:T(8,128)(2,1)} %centers_ref.1), channel_id=1, source_target_pairs={{0,16},{1,5},{2,18},{3,7},{4,20},{5,1},{6,22},{7,3},{8,24},{9,13},... | collective-permute-start | bytes 196616 | tf_op jit(solution)/shard_map/ppermute | solution.py:110
  7.3 6.3 %collective-permute-start.3 = (bf16[16,2048]{1,0:T(8,128)(2,1)S(1)}, bf16[16,2048]{1,0:T(8,128)(2,1)S(1)}, u32[]{:S(2)}, u32[]{:S(2)}) collective-permute-start(bf16[16,2048]{1,0:T(8,128)(2,1)S(1)} %collective-permute-done.1.refs_2_), channel_id=1, source_target_pairs={{0,8},{1,5},{2,10},{3,7},{4,12},{5,1},{6,14},{7,3},{8,0},{9,13},{1... | collective-permute-start | bytes 196616 | tf_op jit(solution)/shard_map/ppermute | solution.py:110
  8.6 6.5 %collective-permute-start.5 = (bf16[16,2048]{1,0:T(8,128)(2,1)S(1)}, bf16[16,2048]{1,0:T(8,128)(2,1)S(1)}, u32[]{:S(2)}, u32[]{:S(2)}) collective-permute-start(bf16[16,2048]{1,0:T(8,128)(2,1)S(1)} %collective-permute-done.1.refs_2_), channel_id=1, source_target_pairs={{0,16},{1,25},{2,18},{3,27},{4,20},{5,29},{6,22},{7,31},{8,24},{9,... | collective-permute-start | bytes 196616 | tf_op jit(solution)/shard_map/ppermute | solution.py:110
  11.5 4.3 %collective-permute-start.6 = (bf16[16,2048]{1,0:T(8,128)(2,1)S(1)}, bf16[16,2048]{1,0:T(8,128)(2,1)S(1)}, u32[]{:S(2)}, u32[]{:S(2)}) collective-permute-start(bf16[16,2048]{1,0:T(8,128)(2,1)S(1)} %collective-permute-done.4.refs_5_), channel_id=1, source_target_pairs={{0,4},{1,5},{2,6},{3,7},{4,0},{5,1},{6,2},{7,3},{8,12},{9,13},{10,... | collective-permute-start | bytes 196616 | tf_op jit(solution)/shard_map/ppermute | solution.py:110
  16.0 2.9 %copy-start = (bf16[16,256]{1,0:T(8,128)(2,1)S(1)}, bf16[16,256]{1,0:T(8,128)(2,1)}, u32[]{:S(2)}) copy-start(bf16[16,256]{1,0:T(8,128)(2,1)} %r_2_.1) | copy-start | bytes 24580
  16.0 1.3 %collective-permute-start.7 = (f32[128,128]{1,0:T(8,128)S(1)}, f32[128,128]{1,0:T(8,128)S(1)}, u32[]{:S(2)}, u32[]{:S(2)}) collective-permute-start(f32[128,128]{1,0:T(8,128)S(1)} %shard_map.39), channel_id=1, source_target_pairs={{0,1},{1,0},{2,3},{3,2},{4,5},{5,4},{6,7},{7,6},{8,9},{9,8},{10,11... | collective-permute-start | bytes 196616 | tf_op jit(solution)/shard_map/ppermute | solution.py:100
  17.3 4.3 %collective-permute-start.8 = (f32[128,128]{1,0:T(8,128)S(1)}, f32[128,128]{1,0:T(8,128)S(1)}, u32[]{:S(2)}, u32[]{:S(2)}) collective-permute-start(f32[128,128]{1,0:T(8,128)S(1)} %add.3.r_0_), channel_id=1, source_target_pairs={{0,2},{1,3},{2,0},{3,1},{4,6},{5,7},{6,4},{7,5},{8,10},{9,11},{10,... | collective-permute-start | bytes 196616 | tf_op jit(solution)/shard_map/ppermute | solution.py:100
  18.9 1.2 %collective-permute-start.9 = (bf16[16,256]{1,0:T(8,128)(2,1)S(1)}, bf16[16,256]{1,0:T(8,128)(2,1)S(1)}, u32[]{:S(2)}, u32[]{:S(2)}) collective-permute-start(bf16[16,256]{1,0:T(8,128)(2,1)S(1)} %copy-done), channel_id=1, source_target_pairs={{0,1},{1,0},{2,3},{3,2},{4,5},{5,4},{6,7},{7,6},{8,9},{9,8},{10,11... | collective-permute-start | bytes 24584 | tf_op jit(solution)/shard_map/ppermute | solution.py:100
  21.7 5.1 %collective-permute-start.10 = (bf16[192,128]{1,0:T(8,128)(2,1)S(1)}, bf16[192,128]{1,0:T(8,128)(2,1)S(1)}, u32[]{:S(2)}, u32[]{:S(2)}) collective-permute-start(bf16[192,128]{1,0:T(8,128)(2,1)S(1)} %shard_map.40.r_0_), channel_id=1, source_target_pairs={{0,12},{1,21},{2,14},{3,23},{4,8},{5,17},{6,10},{7,19},{8,4},{9,29... | collective-permute-start | bytes 147464 | tf_op jit(solution)/shard_map/ppermute | solution.py:110
  21.9 4.8 %collective-permute-start.11 = (bf16[192,128]{1,0:T(8,128)(2,1)S(1)}, bf16[192,128]{1,0:T(8,128)(2,1)S(1)}, u32[]{:S(2)}, u32[]{:S(2)}) collective-permute-start(bf16[192,128]{1,0:T(8,128)(2,1)S(1)} %shard_map.40.r_0_), channel_id=1, source_target_pairs={{0,4},{1,29},{2,6},{3,31},{4,0},{5,25},{6,2},{7,27},{8,12},{9,21},... | collective-permute-start | bytes 147464 | tf_op jit(solution)/shard_map/ppermute | solution.py:110
  23.2 5.6 %collective-permute-start.13 = (bf16[192,128]{1,0:T(8,128)(2,1)S(1)}, bf16[192,128]{1,0:T(8,128)(2,1)S(1)}, u32[]{:S(2)}, u32[]{:S(2)}) collective-permute-start(bf16[192,128]{1,0:T(8,128)(2,1)S(1)} %shard_map.40.r_0_), channel_id=1, source_target_pairs={{0,16},{1,25},{2,18},{3,27},{4,20},{5,29},{6,22},{7,31},{8,24},{9,... | collective-permute-start | bytes 147464 | tf_op jit(solution)/shard_map/ppermute | solution.py:110
  25.2 4.6 %collective-permute-start.12 = (bf16[192,128]{1,0:T(8,128)(2,1)S(1)}, bf16[192,128]{1,0:T(8,128)(2,1)S(1)}, u32[]{:S(2)}, u32[]{:S(2)}) collective-permute-start(bf16[192,128]{1,0:T(8,128)(2,1)S(1)} %shard_map.40.r_0_), channel_id=1, source_target_pairs={{0,8},{1,9},{2,10},{3,11},{4,12},{5,13},{6,14},{7,15},{8,0},{9,1},... | collective-permute-start | bytes 147464 | tf_op jit(solution)/shard_map/ppermute | solution.py:110
  26.7 3.1 %collective-permute-start.14 = (bf16[192,128]{1,0:T(8,128)(2,1)S(1)}, bf16[192,128]{1,0:T(8,128)(2,1)S(1)}, u32[]{:S(2)}, u32[]{:S(2)}) collective-permute-start(bf16[192,128]{1,0:T(8,128)(2,1)S(1)} %collective-permute-done.10.r_1_), channel_id=1, source_target_pairs={{0,1},{1,0},{2,3},{3,2},{4,5},{5,4},{6,7},{7,6},{8,9},{9,8},{10,11... | collective-permute-start | bytes 147464 | tf_op jit(solution)/shard_map/ppermute | solution.py:100
  26.7 3.1 %collective-permute-start.15 = (bf16[192,128]{1,0:T(8,128)(2,1)S(1)}, bf16[192,128]{1,0:T(8,128)(2,1)S(1)}, u32[]{:S(2)}, u32[]{:S(2)}) collective-permute-start(bf16[192,128]{1,0:T(8,128)(2,1)S(1)} %collective-permute-done.11.r_2_), channel_id=1, source_target_pairs={{0,1},{1,0},{2,3},{3,2},{4,5},{5,4},{6,7},{7,6},{8,9},{9,8},{10,11... | collective-permute-start | bytes 147464 | tf_op jit(solution)/shard_map/ppermute | solution.py:100
  28.7 1.2 %collective-permute-start.16 = (bf16[192,128]{1,0:T(8,128)(2,1)S(1)}, bf16[192,128]{1,0:T(8,128)(2,1)S(1)}, u32[]{:S(2)}, u32[]{:S(2)}) collective-permute-start(bf16[192,128]{1,0:T(8,128)(2,1)S(1)} %collective-permute-done.13.r_4_), channel_id=1, source_target_pairs={{0,1},{1,0},{2,3},{3,2},{4,5},{5,4},{6,7},{7,6},{8,9},{9,8},{10,11... | collective-permute-start | bytes 147464 | tf_op jit(solution)/shard_map/ppermute | solution.py:100

commit v10 on v9

--- a/solution.py
+++ b/solution.py
@@ -11,7 +11,7 @@
 F32 = jnp.float32
 VMEM = pl.BlockSpec(memory_space=pltpu.VMEM)
 
-GATHER = ((0, 2, 5), (0, 1, 2), (0, 4, 1), (2, 2, 1), (0, 6, 6), (2, 4, 6), (5, 1, 1))
+GATHER = ((0, 1, 2), (0, 2, 1), (1, 2, 1), (0, 4, 5), (0, 6, 6), (1, 4, 6), (5, 1, 1))
 LATE = (7,)
 SPREAD = ((0, 3, 5), (0, 1, 7), (0, 2, 2), (0, 4, 6))
 

time: 31.4 us -> 31.3 us (level)
  starting transfers between devices: 19.8 us -> 19.2 us
  waiting for transfers between devices: 8.18 us -> 8.68 us
    ppermute x6, starting transfers between devices: 2.97 us -> 2.3 us  [swap(): lax.ppermute(x, 'feat', [(f, f ^ bits) for f in range(lax.axis_size('feat...]
    ppermute x11, waiting for transfers between devices: 3.98 us -> 4.48 us  [swap_by_core(): return lax.ppermute(x, ('blk', 'feat'), pairs)]
  transfers between devices with their start and end apart: 17 -> 17, of which waited for: 10 -> 11; matrix products, arithmetic and copies ran while one was open for 0% -> 0% of each run, Pallas kernels for 5% -> 5%
where the time goes in v10:
time: 31.3 us; the launch traced here: 31.2 us
  starting transfers between devices  19.2 us (61%)
  waiting for transfers between devices  8.68 us (28%)
  Pallas kernels  2.55 us (8%)
  local copies, waits for them, and re-layouts  0.68 us (2%)
    ppermute x11, starting transfers between devices, swap_by_core(): return lax.ppermute(x, ('blk', 'feat'), pairs)  16.9 us
    ppermute x11, waiting for transfers between devices, swap_by_core(): return lax.ppermute(x, ('blk', 'feat'), pairs)  4.48 us
    ppermute x6, waiting for transfers between devices, swap(): lax.ppermute(x, 'feat', [(f, f ^ bits) for f in range(lax.axis_size('feat...  4.2 us
    ppermute x6, starting transfers between devices, swap(): lax.ppermute(x, 'feat', [(f, f ^ bits) for f in range(lax.axis_size('feat...  2.3 us
    pallas_call x1, Pallas kernels, on_device(): pl.pallas_call(prepare_kernel, out_shape=[pltpu.VMEM(points.shape, BF16),...  1.41 us
    pallas_call x4, Pallas kernels, call(): pl.pallas_call(kernel, out_shape=[pltpu.VMEM(*o) for o in outs], in_specs...  1.14 us
    unnamed x3, local copies, waits for them, and re-layouts  0.68 us
  transfers between devices with their start and end apart: 17, of which 11 were waited for; matrix products, arithmetic and copies ran while one was open for 0% of the time, Pallas kernels for 5%

profile of v10, /device:TPU:0, one launch (start us, length us, event | category | flops | bytes accessed | tf_op | source)
XLA Modules:
  0.0 31.2 jit_solution(14407666999906088860)
XLA Ops:
  0.0 2.9 %collective-permute-start = (bf16[16,2048]{1,0:T(8,128)(2,1)}, bf16[16,2048]{1,0:T(8,128)(2,1)S(1)}, u32[]{:S(2)}, u32[]{:S(2)}) collective-permute-start(bf16[16,2048]{1,0:T(8,128)(2,1)} %centers_ref.1), channel_id=1, source_target_pairs={{0,4},{1,9},{2,6},{3,11},{4,0},{5,13},{6,2},{7,15},{8,12},{9,1},{1... | collective-permute-start | bytes 196616 | tf_op jit(solution)/shard_map/ppermute | solution.py:110
  2.9 3.6 %collective-permute-start.4 = (bf16[16,2048]{1,0:T(8,128)(2,1)}, bf16[16,2048]{1,0:T(8,128)(2,1)S(1)}, u32[]{:S(2)}, u32[]{:S(2)}) collective-permute-start(bf16[16,2048]{1,0:T(8,128)(2,1)} %centers_ref.1), channel_id=1, source_target_pairs={{0,24},{1,25},{2,26},{3,27},{4,28},{5,29},{6,30},{7,31},{8,16},{9,... | collective-permute-start | bytes 196616 | tf_op jit(solution)/shard_map/ppermute | solution.py:110
  6.5 0.8 %collective-permute-start.3 = (bf16[16,2048]{1,0:T(8,128)(2,1)}, bf16[16,2048]{1,0:T(8,128)(2,1)S(1)}, u32[]{:S(2)}, u32[]{:S(2)}) collective-permute-start(bf16[16,2048]{1,0:T(8,128)(2,1)} %centers_ref.1), channel_id=1, source_target_pairs={{0,16},{1,21},{2,18},{3,23},{4,20},{5,17},{6,22},{7,19},{8,24},{9,... | collective-permute-start | bytes 196616 | tf_op jit(solution)/shard_map/ppermute | solution.py:110
  7.3 1.2 %collective-permute-start.2 = (bf16[16,2048]{1,0:T(8,128)(2,1)S(1)}, bf16[16,2048]{1,0:T(8,128)(2,1)S(1)}, u32[]{:S(2)}, u32[]{:S(2)}) collective-permute-start(bf16[16,2048]{1,0:T(8,128)(2,1)S(1)} %collective-permute-done.refs_1_), channel_id=1, source_target_pairs={{0,8},{1,5},{2,10},{3,7},{4,12},{5,1},{6,14},{7,3},{8,0},{9,13},{1... | collective-permute-start | bytes 196616 | tf_op jit(solution)/shard_map/ppermute | solution.py:110
  8.6 2.9 %collective-permute-start.5 = (bf16[16,2048]{1,0:T(8,128)(2,1)S(1)}, bf16[16,2048]{1,0:T(8,128)(2,1)S(1)}, u32[]{:S(2)}, u32[]{:S(2)}) collective-permute-start(bf16[16,2048]{1,0:T(8,128)(2,1)S(1)} %collective-permute-done.refs_1_), channel_id=1, source_target_pairs={{0,16},{1,25},{2,18},{3,27},{4,20},{5,29},{6,22},{7,31},{8,24},{9,... | collective-permute-start | bytes 196616 | tf_op jit(solution)/shard_map/ppermute | solution.py:110
  11.5 0.7 %collective-permute-start.6 = (bf16[16,2048]{1,0:T(8,128)(2,1)S(1)}, bf16[16,2048]{1,0:T(8,128)(2,1)S(1)}, u32[]{:S(2)}, u32[]{:S(2)}) collective-permute-start(bf16[16,2048]{1,0:T(8,128)(2,1)S(1)} %collective-permute-done.4.refs_5_), channel_id=1, source_target_pairs={{0,4},{1,5},{2,6},{3,7},{4,0},{5,1},{6,2},{7,3},{8,12},{9,13},{10,... | collective-permute-start | bytes 196616 | tf_op jit(solution)/shard_map/ppermute | solution.py:110
  12.2 1.4 %shard_map.37 = (bf16[128,2048]{1,0:T(8,128)(2,1)S(1)}, bf16[16,2048]{1,0:T(8,128)(2,1)S(1)}, f32[1,128]{1,0:T(1,128)S(1)}) custom-call(bf16[128,2048]{1,0:T(8,128)(2,1)} %points_ref.1, bf16[16,2048]{1,0:T(8,128)(2,1)} %centers_ref.1), custom_call_target="tpu_custom_call" | custom-call | flops 524288 | bytes 524288 | tf_op jit(solution)/shard_map/pallas_call | solution.py:128
  13.6 0.3 collective-permute-done.3.refs_4_
  13.9 1.4 %collective-permute-done.5.refs_6_ = bf16[16,2048]{1,0:T(8,128)(2,1)S(1)} collective-permute-done((bf16[16,2048]{1,0:T(8,128)(2,1)S(1)}, bf16[16,2048]{1,0:T(8,128)(2,1)S(1)}, u32[]{:S(2)}, u32[]{:S(2)}) %collective-permute-start.5) | collective-permute-done | bytes 65568 | tf_op jit(solution)/shard_map/ppermute | solution.py:110
  15.3 0.3 shard_map.38.r_2_
  16.0 1.3 %collective-permute-done.7 = f32[128,128]{1,0:T(8,128)S(1)} collective-permute-done((f32[128,128]{1,0:T(8,128)S(1)}, f32[128,128]{1,0:T(8,128)S(1)}, u32[]{:S(2)}, u32[]{:S(2)}) %collective-permute-start.7) | collective-permute-done | bytes 65568 | tf_op jit(solution)/shard_map/ppermute | solution.py:100
  17.3 1.6 %collective-permute-start.8 = (f32[128,128]{1,0:T(8,128)S(1)}, f32[128,128]{1,0:T(8,128)S(1)}, u32[]{:S(2)}, u32[]{:S(2)}) collective-permute-start(f32[128,128]{1,0:T(8,128)S(1)} %add.3.r_0_), channel_id=1, source_target_pairs={{0,2},{1,3},{2,0},{3,1},{4,6},{5,7},{6,4},{7,5},{8,10},{9,11},{10,... | collective-permute-start | bytes 196616 | tf_op jit(solution)/shard_map/ppermute | solution.py:100
  18.9 1.2 %collective-permute-done.9.r_3_ = bf16[16,256]{1,0:T(8,128)(2,1)S(1)} collective-permute-done((bf16[16,256]{1,0:T(8,128)(2,1)S(1)}, bf16[16,256]{1,0:T(8,128)(2,1)S(1)}, u32[]{:S(2)}, u32[]{:S(2)}) %collective-permute-start.9) | collective-permute-done | bytes 8224 | tf_op jit(solution)/shard_map/ppermute | solution.py:100
  20.1 1.6 %collective-permute-done.8.r_1_ = f32[128,128]{1,0:T(8,128)S(1)} collective-permute-done((f32[128,128]{1,0:T(8,128)S(1)}, f32[128,128]{1,0:T(8,128)S(1)}, u32[]{:S(2)}, u32[]{:S(2)}) %collective-permute-start.8) | collective-permute-done | bytes 65568 | tf_op jit(solution)/shard_map/ppermute | solution.py:100
  21.7 0.8 %collective-permute-start.10 = (bf16[192,128]{1,0:T(8,128)(2,1)S(1)}, bf16[192,128]{1,0:T(8,128)(2,1)S(1)}, u32[]{:S(2)}, u32[]{:S(2)}) collective-permute-start(bf16[192,128]{1,0:T(8,128)(2,1)S(1)} %shard_map.40.r_0_), channel_id=1, source_target_pairs={{0,12},{1,21},{2,14},{3,23},{4,8},{5,17},{6,10},{7,19},{8,4},{9,29... | collective-permute-start | bytes 147464 | tf_op jit(solution)/shard_map/ppermute | solution.py:110
  22.4 0.8 %collective-permute-start.11 = (bf16[192,128]{1,0:T(8,128)(2,1)S(1)}, bf16[192,128]{1,0:T(8,128)(2,1)S(1)}, u32[]{:S(2)}, u32[]{:S(2)}) collective-permute-start(bf16[192,128]{1,0:T(8,128)(2,1)S(1)} %shard_map.40.r_0_), channel_id=1, source_target_pairs={{0,4},{1,29},{2,6},{3,31},{4,0},{5,25},{6,2},{7,27},{8,12},{9,21},... | collective-permute-start | bytes 147464 | tf_op jit(solution)/shard_map/ppermute | solution.py:110
  23.2 1.9 %collective-permute-start.13 = (bf16[192,128]{1,0:T(8,128)(2,1)S(1)}, bf16[192,128]{1,0:T(8,128)(2,1)S(1)}, u32[]{:S(2)}, u32[]{:S(2)}) collective-permute-start(bf16[192,128]{1,0:T(8,128)(2,1)S(1)} %shard_map.40.r_0_), channel_id=1, source_target_pairs={{0,16},{1,25},{2,18},{3,27},{4,20},{5,29},{6,22},{7,31},{8,24},{9,... | collective-permute-start | bytes 147464 | tf_op jit(solution)/shard_map/ppermute | solution.py:110
  25.1 1.3 %collective-permute-start.12 = (bf16[192,128]{1,0:T(8,128)(2,1)S(1)}, bf16[192,128]{1,0:T(8,128)(2,1)S(1)}, u32[]{:S(2)}, u32[]{:S(2)}) collective-permute-start(bf16[192,128]{1,0:T(8,128)(2,1)S(1)} %shard_map.40.r_0_), channel_id=1, source_target_pairs={{0,8},{1,9},{2,10},{3,11},{4,12},{5,13},{6,14},{7,15},{8,0},{9,1},... | collective-permute-start | bytes 147464 | tf_op jit(solution)/shard_map/ppermute | solution.py:110
  26.4 0.4 %collective-permute-done.10.r_1_ = bf16[192,128]{1,0:T(8,128)(2,1)S(1)} collective-permute-done((bf16[192,128]{1,0:T(8,128)(2,1)S(1)}, bf16[192,128]{1,0:T(8,128)(2,1)S(1)}, u32[]{:S(2)}, u32[]{:S(2)}) %collective-permute-start.10) | collective-permute-done | bytes 49184 | tf_op jit(solution)/shard_map/ppermute | solution.py:110
  27.0 0.7 %collective-permute-start.15 = (bf16[192,128]{1,0:T(8,128)(2,1)S(1)}, bf16[192,128]{1,0:T(8,128)(2,1)S(1)}, u32[]{:S(2)}, u32[]{:S(2)}) collective-permute-start(bf16[192,128]{1,0:T(8,128)(2,1)S(1)} %collective-permute-done.11.r_2_), channel_id=1, source_target_pairs={{0,1},{1,0},{2,3},{3,2},{4,5},{5,4},{6,7},{7,6},{8,9},{9,8},{10,11... | collective-permute-start | bytes 147464 | tf_op jit(solution)/shard_map/ppermute | solution.py:100
  27.7 1.0 %collective-permute-done.13.r_4_ = bf16[192,128]{1,0:T(8,128)(2,1)S(1)} collective-permute-done((bf16[192,128]{1,0:T(8,128)(2,1)S(1)}, bf16[192,128]{1,0:T(8,128)(2,1)S(1)}, u32[]{:S(2)}, u32[]{:S(2)}) %collective-permute-start.13) | collective-permute-done | bytes 49184 | tf_op jit(solution)/shard_map/ppermute | solution.py:110
  28.7 1.0 %collective-permute-done.12.r_3_ = bf16[192,128]{1,0:T(8,128)(2,1)S(1)} collective-permute-done((bf16[192,128]{1,0:T(8,128)(2,1)S(1)}, bf16[192,128]{1,0:T(8,128)(2,1)S(1)}, u32[]{:S(2)}, u32[]{:S(2)}) %collective-permute-start.12) | collective-permute-done | bytes 49184 | tf_op jit(solution)/shard_map/ppermute | solution.py:110
  30.0 0.6 %shard_map.41 = f32[16,256]{1,0:T(8,128)S(1)} custom-call(bf16[192,128]{1,0:T(8,128)(2,1)S(1)} %shard_map.40.r_0_, bf16[192,128]{1,0:T(8,128)(2,1)S(1)} %collective-permute-done.10.r_1_, bf16[192,128]{1,0:T(8,128)(2,1)S(1)} %collective-permute-done.11.r_2_, bf16[192,128]{1,0:T(8,128)(2,1)S(1)} %collective-permute-done.12.r_3_, ...), custom_call_target="tpu_custom_call" | custom-call | tf_op jit(solution)/shard_map/pallas_call | solution.py:24
  30.5 0.7 %copy.4 = f32[16,256]{1,0:T(8,128)} copy(f32[16,256]{1,0:T(8,128)S(1)} %shard_map.41) | data formatting | bytes 32768
  (19 shorter events, 0.9 us)
Async XLA Ops:
  0.0 7.3 %collective-permute-start = (bf16[16,2048]{1,0:T(8,128)(2,1)}, bf16[16,2048]{1,0:T(8,128)(2,1)S(1)}, u32[]{:S(2)}, u32[]{:S(2)}) collective-permute-start(bf16[16,2048]{1,0:T(8,128)(2,1)} %centers_ref.1), channel_id=1, source_target_pairs={{0,4},{1,9},{2,6},{3,11},{4,0},{5,13},{6,2},{7,15},{8,12},{9,1},{1... | collective-permute-start | bytes 196616 | tf_op jit(solution)/shard_map/ppermute | solution.py:110
  2.9 8.6 %collective-permute-start.4 = (bf16[16,2048]{1,0:T(8,128)(2,1)}, bf16[16,2048]{1,0:T(8,128)(2,1)S(1)}, u32[]{:S(2)}, u32[]{:S(2)}) collective-permute-start(bf16[16,2048]{1,0:T(8,128)(2,1)} %centers_ref.1), channel_id=1, source_target_pairs={{0,24},{1,25},{2,26},{3,27},{4,28},{5,29},{6,30},{7,31},{8,16},{9,... | collective-permute-start | bytes 196616 | tf_op jit(solution)/shard_map/ppermute | solution.py:110
  6.5 7.1 %collective-permute-start.1 = (bf16[16,2048]{1,0:T(8,128)(2,1)}, bf16[16,2048]{1,0:T(8,128)(2,1)S(1)}, u32[]{:S(2)}, u32[]{:S(2)}) collective-permute-start(bf16[16,2048]{1,0:T(8,128)(2,1)} %centers_ref.1), channel_id=1, source_target_pairs={{0,8},{1,5},{2,10},{3,7},{4,12},{5,1},{6,14},{7,3},{8,0},{9,13},{1... | collective-permute-start | bytes 196616 | tf_op jit(solution)/shard_map/ppermute | solution.py:110
  6.5 7.3 %collective-permute-start.3 = (bf16[16,2048]{1,0:T(8,128)(2,1)}, bf16[16,2048]{1,0:T(8,128)(2,1)S(1)}, u32[]{:S(2)}, u32[]{:S(2)}) collective-permute-start(bf16[16,2048]{1,0:T(8,128)(2,1)} %centers_ref.1), channel_id=1, source_target_pairs={{0,16},{1,21},{2,18},{3,23},{4,20},{5,17},{6,22},{7,19},{8,24},{9,... | collective-permute-start | bytes 196616 | tf_op jit(solution)/shard_map/ppermute | solution.py:110
  7.3 6.5 %collective-permute-start.2 = (bf16[16,2048]{1,0:T(8,128)(2,1)S(1)}, bf16[16,2048]{1,0:T(8,128)(2,1)S(1)}, u32[]{:S(2)}, u32[]{:S(2)}) collective-permute-start(bf16[16,2048]{1,0:T(8,128)(2,1)S(1)} %collective-permute-done.refs_1_), channel_id=1, source_target_pairs={{0,8},{1,5},{2,10},{3,7},{4,12},{5,1},{6,14},{7,3},{8,0},{9,13},{1... | collective-permute-start | bytes 196616 | tf_op jit(solution)/shard_map/ppermute | solution.py:110
  8.6 6.7 %collective-permute-start.5 = (bf16[16,2048]{1,0:T(8,128)(2,1)S(1)}, bf16[16,2048]{1,0:T(8,128)(2,1)S(1)}, u32[]{:S(2)}, u32[]{:S(2)}) collective-permute-start(bf16[16,2048]{1,0:T(8,128)(2,1)S(1)} %collective-permute-done.refs_1_), channel_id=1, source_target_pairs={{0,16},{1,25},{2,18},{3,27},{4,20},{5,29},{6,22},{7,31},{8,24},{9,... | collective-permute-start | bytes 196616 | tf_op jit(solution)/shard_map/ppermute | solution.py:110
  11.5 4.3 %collective-permute-start.6 = (bf16[16,2048]{1,0:T(8,128)(2,1)S(1)}, bf16[16,2048]{1,0:T(8,128)(2,1)S(1)}, u32[]{:S(2)}, u32[]{:S(2)}) collective-permute-start(bf16[16,2048]{1,0:T(8,128)(2,1)S(1)} %collective-permute-done.4.refs_5_), channel_id=1, source_target_pairs={{0,4},{1,5},{2,6},{3,7},{4,0},{5,1},{6,2},{7,3},{8,12},{9,13},{10,... | collective-permute-start | bytes 196616 | tf_op jit(solution)/shard_map/ppermute | solution.py:110
  16.0 2.9 %copy-start = (bf16[16,256]{1,0:T(8,128)(2,1)S(1)}, bf16[16,256]{1,0:T(8,128)(2,1)}, u32[]{:S(2)}) copy-start(bf16[16,256]{1,0:T(8,128)(2,1)} %r_2_.1) | copy-start | bytes 24580
  16.0 1.3 %collective-permute-start.7 = (f32[128,128]{1,0:T(8,128)S(1)}, f32[128,128]{1,0:T(8,128)S(1)}, u32[]{:S(2)}, u32[]{:S(2)}) collective-permute-start(f32[128,128]{1,0:T(8,128)S(1)} %shard_map.39), channel_id=1, source_target_pairs={{0,1},{1,0},{2,3},{3,2},{4,5},{5,4},{6,7},{7,6},{8,9},{9,8},{10,11... | collective-permute-start | bytes 196616 | tf_op jit(solution)/shard_map/ppermute | solution.py:100
  17.3 4.3 %collective-permute-start.8 = (f32[128,128]{1,0:T(8,128)S(1)}, f32[128,128]{1,0:T(8,128)S(1)}, u32[]{:S(2)}, u32[]{:S(2)}) collective-permute-start(f32[128,128]{1,0:T(8,128)S(1)} %add.3.r_0_), channel_id=1, source_target_pairs={{0,2},{1,3},{2,0},{3,1},{4,6},{5,7},{6,4},{7,5},{8,10},{9,11},{10,... | collective-permute-start | bytes 196616 | tf_op jit(solution)/shard_map/ppermute | solution.py:100
  18.9 1.2 %collective-permute-start.9 = (bf16[16,256]{1,0:T(8,128)(2,1)S(1)}, bf16[16,256]{1,0:T(8,128)(2,1)S(1)}, u32[]{:S(2)}, u32[]{:S(2)}) collective-permute-start(bf16[16,256]{1,0:T(8,128)(2,1)S(1)} %copy-done), channel_id=1, source_target_pairs={{0,1},{1,0},{2,3},{3,2},{4,5},{5,4},{6,7},{7,6},{8,9},{9,8},{10,11... | collective-permute-start | bytes 24584 | tf_op jit(solution)/shard_map/ppermute | solution.py:100
  21.7 5.2 %collective-permute-start.10 = (bf16[192,128]{1,0:T(8,128)(2,1)S(1)}, bf16[192,128]{1,0:T(8,128)(2,1)S(1)}, u32[]{:S(2)}, u32[]{:S(2)}) collective-permute-start(bf16[192,128]{1,0:T(8,128)(2,1)S(1)} %shard_map.40.r_0_), channel_id=1, source_target_pairs={{0,12},{1,21},{2,14},{3,23},{4,8},{5,17},{6,10},{7,19},{8,4},{9,29... | collective-permute-start | bytes 147464 | tf_op jit(solution)/shard_map/ppermute | solution.py:110
  22.4 4.6 %collective-permute-start.11 = (bf16[192,128]{1,0:T(8,128)(2,1)S(1)}, bf16[192,128]{1,0:T(8,128)(2,1)S(1)}, u32[]{:S(2)}, u32[]{:S(2)}) collective-permute-start(bf16[192,128]{1,0:T(8,128)(2,1)S(1)} %shard_map.40.r_0_), channel_id=1, source_target_pairs={{0,4},{1,29},{2,6},{3,31},{4,0},{5,25},{6,2},{7,27},{8,12},{9,21},... | collective-permute-start | bytes 147464 | tf_op jit(solution)/shard_map/ppermute | solution.py:110
  23.2 5.5 %collective-permute-start.13 = (bf16[192,128]{1,0:T(8,128)(2,1)S(1)}, bf16[192,128]{1,0:T(8,128)(2,1)S(1)}, u32[]{:S(2)}, u32[]{:S(2)}) collective-permute-start(bf16[192,128]{1,0:T(8,128)(2,1)S(1)} %shard_map.40.r_0_), channel_id=1, source_target_pairs={{0,16},{1,25},{2,18},{3,27},{4,20},{5,29},{6,22},{7,31},{8,24},{9,... | collective-permute-start | bytes 147464 | tf_op jit(solution)/shard_map/ppermute | solution.py:110
  25.1 4.6 %collective-permute-start.12 = (bf16[192,128]{1,0:T(8,128)(2,1)S(1)}, bf16[192,128]{1,0:T(8,128)(2,1)S(1)}, u32[]{:S(2)}, u32[]{:S(2)}) collective-permute-start(bf16[192,128]{1,0:T(8,128)(2,1)S(1)} %shard_map.40.r_0_), channel_id=1, source_target_pairs={{0,8},{1,9},{2,10},{3,11},{4,12},{5,13},{6,14},{7,15},{8,0},{9,1},... | collective-permute-start | bytes 147464 | tf_op jit(solution)/shard_map/ppermute | solution.py:110
  26.8 2.9 %collective-permute-start.14 = (bf16[192,128]{1,0:T(8,128)(2,1)S(1)}, bf16[192,128]{1,0:T(8,128)(2,1)S(1)}, u32[]{:S(2)}, u32[]{:S(2)}) collective-permute-start(bf16[192,128]{1,0:T(8,128)(2,1)S(1)} %collective-permute-done.10.r_1_), channel_id=1, source_target_pairs={{0,1},{1,0},{2,3},{3,2},{4,5},{5,4},{6,7},{7,6},{8,9},{9,8},{10,11... | collective-permute-start | bytes 147464 | tf_op jit(solution)/shard_map/ppermute | solution.py:100
  27.0 2.7 %collective-permute-start.15 = (bf16[192,128]{1,0:T(8,128)(2,1)S(1)}, bf16[192,128]{1,0:T(8,128)(2,1)S(1)}, u32[]{:S(2)}, u32[]{:S(2)}) collective-permute-start(bf16[192,128]{1,0:T(8,128)(2,1)S(1)} %collective-permute-done.11.r_2_), channel_id=1, source_target_pairs={{0,1},{1,0},{2,3},{3,2},{4,5},{5,4},{6,7},{7,6},{8,9},{9,8},{10,11... | collective-permute-start | bytes 147464 | tf_op jit(solution)/shard_map/ppermute | solution.py:100
  28.7 1.2 %collective-permute-start.16 = (bf16[192,128]{1,0:T(8,128)(2,1)S(1)}, bf16[192,128]{1,0:T(8,128)(2,1)S(1)}, u32[]{:S(2)}, u32[]{:S(2)}) collective-permute-start(bf16[192,128]{1,0:T(8,128)(2,1)S(1)} %collective-permute-done.13.r_4_), channel_id=1, source_target_pairs={{0,1},{1,0},{2,3},{3,2},{4,5},{5,4},{6,7},{7,6},{8,9},{9,8},{10,11... | collective-permute-start | bytes 147464 | tf_op jit(solution)/shard_map/ppermute | solution.py:100
